TPU v7x, 32 devices: a whole 2x2x4 slice. The times are simulated.
32 devices in a mesh: groups: 2 (over y), src: 4 (over z), tile: 2 (over x), pix: 2 (over core).
Axes of the slice: x: 2, y: 2, z: 4, core: 2. Of those that a mesh axis runs over, the one named last changes fastest.
Arguments:
- mask: float32 [4, 1024, 1024], P(('groups', 'tile'), ('src', 'pix')), parts along dimension 0, may hold values from -1 to 1
- target: float32 [4, 1024, 1024], P(('groups', 'tile'), ('src', 'pix')), parts along dimension 0, may hold values from 0 to 1
- tile_class: int32 [4], P(('groups', 'tile')), parts along dimension 0, may hold values from 0 to 3
- thresholds: float32 [4], replicated, may hold values from 0.3 to 1.2
- source_pupil: bfloat16 [512, 2048], P('src'), as said below
- source_weight: bfloat16 [512], P('src'), may hold values from 0.125 to 1.25
- source_cell: int32 [512], P('src'), may hold values from 0 to 288
- active_count: int32 [4], replicated, may hold values from 1 to 6, as said below
Outputs:
- intensity: float32 [4, 1024, 1024], P(('groups', 'tile'), ('src', 'pix')), parts along dimension 0
- mask_grad: float32 [4, 1024, 1024], P(('groups', 'tile'), ('src', 'pix')), parts along dimension 0
- source_grad: float32 [1024], P(('groups', 'src')), parts along dimension 0
There are 2 independent parts, one for each index of `groups`. A program takes and returns all parts, laid end to end along the dimension named above; an argument that names none is the same for every part. Nothing has to cross between parts.
Inputs may be any that keep to these rules, and one draw needn't show every extreme that they name: Index d of src has active_count[d] live slots, its first ones; some index has exactly 6. `source_pupil`: each row holds a source point's 32 x 32 pupil samples, real parts then imaginary parts.
All inputs are finite; a program needn't handle non-finite values.
Results may differ from a plain program's by a relative error of at most 0.011.
Values may be sent and summed in bfloat16 or wider, within the bound.
No kernel may reach another device: no remote copies, remote signals or barrier semaphores. Data moves between devices by JAX's collectives and lax.ppermute only.
A program may use at most 64 MiB of HBM per device.

v0:
```python
import math

import jax
import jax.numpy as jnp
from jax import lax
from jax.sharding import PartitionSpec as P

K = 32
SG = 17
W = 48
MOST = 6
CLASSES = 4


steep = 4.0


def phase_pair(freqs, places, period):
    turns = freqs[:, None] * places[None, :] % period
    angle = 2.0 * jnp.pi / period * turns.astype(jnp.float32)
    return (jnp.cos(angle), jnp.sin(angle))


def mix_table(back_cos, back_sin):
    upper = jnp.concatenate([back_cos, back_sin], 1)
    lower = jnp.concatenate([-back_sin, back_cos], 1)
    return jnp.concatenate([upper, lower], 0).astype(jnp.bfloat16)


def left_of(row_ids, period):
    narrow = jnp.arange(K, dtype=jnp.int32) - K // 2
    cos_part, sin_part = phase_pair(row_ids, narrow, period)
    upper = jnp.concatenate([cos_part, -sin_part], 1)
    lower = jnp.concatenate([sin_part, cos_part], 1)
    return jnp.concatenate([upper, lower], 0).astype(jnp.bfloat16)


def make_stack(spectrum, pupil, row_shift, col_shift, back_mix, period):
    window = lax.dynamic_slice(spectrum, (jnp.int32(0), row_shift, col_shift), (2, K, K))
    wave_re = (pupil[0] * window[0] - pupil[1] * window[1]).astype(jnp.bfloat16)
    wave_im = (pupil[0] * window[1] + pupil[1] * window[0]).astype(jnp.bfloat16)
    joined = jnp.dot(
        jnp.concatenate([wave_re, wave_im], 1), back_mix, preferred_element_type=jnp.float32
    )
    return jnp.concatenate([joined[:, :period], joined[:, period:]], 0).astype(jnp.bfloat16)


def field_of(left_table, stacked):
    raw = jnp.dot(left_table, stacked, preferred_element_type=jnp.float32) * (1.0 / K)
    return lax.optimization_barrier(raw.astype(jnp.bfloat16)).astype(jnp.float32)


def spread_into(grad_spec, grad_stack, pupil, row_shift, col_shift, back_cos, back_sin):
    exact = lax.Precision.HIGHEST
    grad_re = grad_stack[:K]
    grad_im = grad_stack[K:]
    wave_re = jnp.dot(grad_re, back_cos.T, precision=exact) + jnp.dot(
        grad_im, back_sin.T, precision=exact
    )
    wave_im = jnp.dot(grad_im, back_cos.T, precision=exact) - jnp.dot(
        grad_re, back_sin.T, precision=exact
    )
    spot = (jnp.int32(0), row_shift, col_shift)
    before = lax.dynamic_slice(grad_spec, spot, (2, K, K))
    after = before + jnp.stack(
        [pupil[0] * wave_re + pupil[1] * wave_im, pupil[0] * wave_im - pupil[1] * wave_re]
    )
    return lax.dynamic_update_slice(grad_spec, after, spot)


def band_rows(first_row, row_count, span, pix_count, pix_index):
    local = first_row + jnp.arange(row_count, dtype=jnp.int32)
    return (local // span * pix_count + pix_index) * span + local % span


def shards(
    mask, target, tile_class, thresholds, source_pupil, source_weight, source_cell, active_count
):
    exact = lax.Precision.HIGHEST
    tile_rows = mask[0]
    aim_rows = target[0]
    span, period = tile_rows.shape
    slot_count = source_pupil.shape[0]
    src_count = lax.axis_size("src")
    pix_count = lax.axis_size("pix")
    src_index = lax.axis_index("src")
    pix_index = lax.axis_index("pix")
    band = span * src_count
    pixels = jnp.arange(period, dtype=jnp.int32)
    wide = jnp.arange(W, dtype=jnp.int32) - W // 2
    narrow = jnp.arange(K, dtype=jnp.int32) - K // 2
    my_rows = band_rows(src_index * span, span, span, pix_count, pix_index)
    spec_cos, spec_sin = phase_pair(wide, pixels, period)
    row_cos, row_sin = phase_pair(wide, my_rows, period)
    back_cos, back_sin = phase_pair(narrow, pixels, period)
    back_mix = mix_table(back_cos, back_sin)
    part_re = jnp.dot(tile_rows, spec_cos.T, precision=exact)
    part_im = -jnp.dot(tile_rows, spec_sin.T, precision=exact)
    partial_spec = (
        jnp.stack(
            [
                jnp.dot(row_cos, part_re, precision=exact)
                + jnp.dot(row_sin, part_im, precision=exact),
                jnp.dot(row_cos, part_im, precision=exact)
                - jnp.dot(row_sin, part_re, precision=exact),
            ]
        )
        / period
    )
    spectrum = lax.psum(partial_spec, ("src", "pix"))
    threshold = jnp.sum(
        jnp.where(jnp.arange(CLASSES, dtype=jnp.int32) == tile_class[0], thresholds, 0.0)
    )
    pupils = source_pupil[:MOST]
    weights = source_weight[:MOST]
    shift_rows = source_cell[:MOST] // SG
    shift_cols = source_cell[:MOST] % SG
    active = active_count[src_index]

    def make_field(position, store):
        pupil = pupils[position].reshape(2, K, K).astype(jnp.float32)
        stacked = make_stack(
            spectrum, pupil, shift_rows[position], shift_cols[position], back_mix, period
        )
        return lax.dynamic_update_slice(store, stacked[None], (position, 0, 0))

    fields = lax.fori_loop(0, active, make_field, jnp.zeros((MOST, 2 * K, period), jnp.bfloat16))

    def block_power(begin, step):
        left_table = left_of(band_rows(begin, step, span, pix_count, pix_index), period)

        def add_source(position, total_power):
            field_now = field_of(left_table, fields[position])
            return total_power + weights[position].astype(jnp.float32) * (
                field_now[:step] ** 2 + field_now[step:] ** 2
            )

        return lax.fori_loop(0, active, add_source, jnp.zeros((step, period), jnp.float32))

    step = math.gcd(band, 128)
    begins = 0 + step * jnp.arange(band // step, dtype=jnp.int32)

    def intensity_one_block(begin):
        return block_power(begin, step)

    whole = lax.psum(lax.map(intensity_one_block, begins).reshape(band, period), "src")
    intensity = lax.dynamic_slice_in_dim(whole, src_index * span, span, 0)
    resist = jax.nn.sigmoid(steep * (intensity - threshold))
    slope = (2.0 * (resist - aim_rows) * steep * resist * (1.0 - resist)).astype(jnp.bfloat16)

    def absorb_block(state, rows_in, begin):
        step = rows_in.shape[0]
        left_table = left_of(band_rows(begin, step, span, pix_count, pix_index), period)
        slope_now = rows_in.astype(jnp.float32)

        def one_source(position, inner):
            grad_fields, grad_weights = inner
            field_now = field_of(left_table, fields[position])
            power_now = field_now[:step] ** 2 + field_now[step:] ** 2
            grad_weights = grad_weights.at[position].add(jnp.sum(slope_now * power_now))
            scaled = 2.0 / K * weights[position].astype(jnp.float32) * slope_now
            pull = (jnp.concatenate([scaled, scaled], 0) * field_now).astype(jnp.bfloat16)
            update = lax.dot_general(
                left_table, pull, (((0,), (0,)), ((), ())), preferred_element_type=jnp.float32
            )
            grad_fields = lax.dynamic_update_slice(
                grad_fields, (grad_fields[position] + update)[None], (position, 0, 0)
            )
            return (grad_fields, grad_weights)

        return lax.fori_loop(0, active, one_source, state)

    empty_fields = jnp.zeros((MOST, 2 * K, period), jnp.float32)
    empty_weights = jnp.zeros((MOST,), jnp.float32)
    received = lax.all_gather(slope, "src", axis=0, tiled=True)
    row_count = received.shape[0]
    absorb_step = math.gcd(row_count, 128)

    def absorb_one_block(block, inner):
        rows_in = lax.dynamic_slice_in_dim(received, block * absorb_step, absorb_step, 0)
        return absorb_block(inner, rows_in, block * absorb_step)

    grad_fields, grad_weights = lax.fori_loop(
        0, row_count // absorb_step, absorb_one_block, (empty_fields, empty_weights)
    )

    def gather_back(position, grad_acc):
        pupil = pupils[position].reshape(2, K, K).astype(jnp.float32)
        return spread_into(
            grad_acc,
            grad_fields[position],
            pupil,
            shift_rows[position],
            shift_cols[position],
            back_cos,
            back_sin,
        )

    grad_spec = lax.fori_loop(0, active, gather_back, jnp.zeros((2, W, W), jnp.float32))
    grad_weights = lax.psum(grad_weights, ("tile", "pix"))
    kept = jnp.where(jnp.arange(MOST, dtype=jnp.int32) < active, grad_weights, 0.0)
    source_grad = jnp.zeros((slot_count,), jnp.float32).at[:MOST].set(kept)
    grad_spec = lax.psum(grad_spec, ("src", "pix"))
    z_one = jnp.dot(grad_spec[0], spec_cos, precision=exact) - jnp.dot(
        grad_spec[1], spec_sin, precision=exact
    )
    z_two = -jnp.dot(grad_spec[0], spec_sin, precision=exact) - jnp.dot(
        grad_spec[1], spec_cos, precision=exact
    )
    mask_grad = (
        jnp.dot(row_cos.T, z_one, precision=exact) + jnp.dot(row_sin.T, z_two, precision=exact)
    ) / period
    source_grad = source_grad * (1.0 / (period * K))
    return (intensity[None], mask_grad[None], source_grad)


def solution(mesh):
    in_specs = (
        P(("groups", "tile"), ("src", "pix"), None),
        P(("groups", "tile"), ("src", "pix"), None),
        P(("groups", "tile")),
        P(),
        P("src", None),
        P("src"),
        P("src"),
        P(),
    )
    out_specs = (
        P(("groups", "tile"), ("src", "pix"), None),
        P(("groups", "tile"), ("src", "pix"), None),
        P(("groups", "src")),
    )
    return jax.shard_map(shards, mesh=mesh, in_specs=in_specs, out_specs=out_specs, check_vma=False)
```

profile of v0, /device:TPU:0, one launch (start us, length us, event | category | flops | bytes accessed | tf_op | source)
XLA Modules:
  0.0 548.4 jit_solution(5891984044252353755)
XLA Ops:
  7.3 1.0 copy-done
  8.2 1.3 convolution_negate_fusion.1
  9.6 1.3 fusion.85
  12.3 30.7 %psum.28 = f32[2,48,48]{2,1,0:T(8,128)S(1)} all-reduce(f32[2,48,48]{2,1,0:T(8,128)S(1)} %maximum_multiply_fusion.1), channel_id=1, replica_groups=mesh['groups'=2,'src'=4,'tile'=2,'pix'=2] {'src','pix'}, use_global_device_ids=true, to_apply=%region_0.1 | all-reduce | flops 4608 | bytes 36864 | tf_op jit(solution)/shard_map/psum | solution.py:110
  44.4 7.0 %while.110 = (s32[]{:T(128)}, bf16[6,64,1024]{2,1,0:T(8,128)(2,1)S(1)}, s32[]{:T(128)}, bf16[6,2048]{1,0:T(8,128)(2,1)S(1)}, s32[6]{0:T(128)S(1)}, /*index=5*/s3...) while((s32[]{:T(128)}, ...), condition=%wide.region_2.3_spmd, body=%wide.region_1.2_spmd.sunk | while | flops 8734732 | bytes 987419 | solution.py:127
  51.5 77.4 %while.112 = (s32[]{:T(128)}, f32[4,128,1024]{1,0,2:T(4,128)}, s32[4]{0:T(128)S(1)}, s32[]{:T(128)}, s32[]{:T(128)}, /*index=5*/bf16[6]{0:T(256)(128)(2,1)S(1)},...) while((s32[]{:T(128)}, f32[4,128,1024]{1,0,2:T(4,128)}, ...), condition=%wide.region_6.7_spmd, body=%wide.region_3.6_spmd.sunk | while | flops 35204132 | bytes 6112902 | solution.py:146
  53.1 3.3 while.116
  56.5 14.4 %dynamic_update_slice.27 = f32[4,128,1024]{1,0,2:T(4,128)} dynamic-update-slice(f32[4,128,1024]{1,0,2:T(4,128)} %get-tuple-element.1250, f32[1,128,1024]{1,0,2:T(1,128)S(1)} %bitcast.165, s32[]{:T(128)} %get-tuple-element.1249, s32[]{:T(128)} %constant.423.clone.1..sunk.1, s32[]{:T(128)} %constant.423.clone.1..sunk.1) | dynamic-update-slice | bytes 1048580 | tf_op jit(solution)/shard_map/while/body/jit(dynamic_update_index_in_dim)/dynamic_update_slice | solution.py:146
  72.5 3.3 while.116
  75.8 14.4 %dynamic_update_slice.27 = f32[4,128,1024]{1,0,2:T(4,128)} dynamic-update-slice(f32[4,128,1024]{1,0,2:T(4,128)} %get-tuple-element.1250, f32[1,128,1024]{1,0,2:T(1,128)S(1)} %bitcast.165, s32[]{:T(128)} %get-tuple-element.1249, s32[]{:T(128)} %constant.423.clone.1..sunk.1, s32[]{:T(128)} %constant.423.clone.1..sunk.1) | dynamic-update-slice | bytes 1048580 | tf_op jit(solution)/shard_map/while/body/jit(dynamic_update_index_in_dim)/dynamic_update_slice | solution.py:146
  91.8 3.3 while.116
  95.2 14.4 %dynamic_update_slice.27 = f32[4,128,1024]{1,0,2:T(4,128)} dynamic-update-slice(f32[4,128,1024]{1,0,2:T(4,128)} %get-tuple-element.1250, f32[1,128,1024]{1,0,2:T(1,128)S(1)} %bitcast.165, s32[]{:T(128)} %get-tuple-element.1249, s32[]{:T(128)} %constant.423.clone.1..sunk.1, s32[]{:T(128)} %constant.423.clone.1..sunk.1) | dynamic-update-slice | bytes 1048580 | tf_op jit(solution)/shard_map/while/body/jit(dynamic_update_index_in_dim)/dynamic_update_slice | solution.py:146
  111.2 3.3 while.116
  114.5 14.4 %dynamic_update_slice.27 = f32[4,128,1024]{1,0,2:T(4,128)} dynamic-update-slice(f32[4,128,1024]{1,0,2:T(4,128)} %get-tuple-element.1250, f32[1,128,1024]{1,0,2:T(1,128)S(1)} %bitcast.165, s32[]{:T(128)} %get-tuple-element.1249, s32[]{:T(128)} %constant.423.clone.1..sunk.1, s32[]{:T(128)} %constant.423.clone.1..sunk.1) | dynamic-update-slice | bytes 1048580 | tf_op jit(solution)/shard_map/while/body/jit(dynamic_update_index_in_dim)/dynamic_update_slice | solution.py:146
  128.9 3.1 copy.25
  132.1 1.0 copy-done.1
  134.5 163.1 %all-reduce.3.cloned.1.call-done = f32[512,1024]{0,1:T(8,128)} async-done(((f32[512,1024]{0,1:T(8,128)}), f32[512,1024]{0,1:T(8,128)}) %all-reduce.3.cloned.1.call-update) | async-done | bytes 2097168 | tf_op jit(solution)/shard_map/psum | solution.py:146
  297.6 2.6 fusion.83
  300.2 1.0 copy.17
  301.2 28.3 %all-gather.2.cloned.1.call-done = bf16[512,1024]{0,1:T(8,128)(2,1)} async-done(((bf16[128,1024]{0,1:T(8,128)(2,1)}), bf16[512,1024]{0,1:T(8,128)(2,1)}) %all-gather.2.cloned.1.call-update) | async-done | bytes 1048592 | tf_op jit(solution)/shard_map/all_gather | solution.py:175
  329.7 25.5 %while.114 = (s32[]{:T(128)}, f32[6,64,1024]{2,1,0:T(8,128)S(1)}, f32[6]{0:T(128)S(1)}, s32[]{:T(128)}, bf16[512,1024]{0,1:T(8,128)(2,1)}, /*index=5*/s32[]{:T(1...) while((s32[]{:T(128)}, f32[6,64,1024]{2,1,0:T(8,128)S(1)}, ...), condition=%wide.region_13.14_spmd, body=%wide.region_9.13_spmd.sunk | while | flops 70134824 | bytes 7489370 | solution.py:183
  330.1 1.0 dynamic-slice_convert_fusion.7
  331.1 5.0 while.117
  333.5 0.8 fusion.225
  336.5 1.0 dynamic-slice_convert_fusion.7
  337.5 5.0 while.117
  339.9 0.8 fusion.225
  341.0 0.8 fusion.227
  342.8 1.0 dynamic-slice_convert_fusion.7
  343.8 5.0 while.117
  346.3 0.8 fusion.225
  347.4 0.8 fusion.227
  349.2 1.0 dynamic-slice_convert_fusion.7
  350.2 5.0 while.117
  352.6 0.8 fusion.225
  355.3 11.2 %while.115 = (s32[]{:T(128)}, f32[2,48,48]{2,1,0:T(8,128)S(1)}, s32[]{:T(128)}, s32[6]{0:T(128)S(1)}, s32[6]{0:T(128)S(1)}, /*index=5*/bf16[6,2048]{1,0:T(8,128)...) while((s32[]{:T(128)}, f32[2,48,48]{2,1,0:T(8,128)S(1)}, ...), condition=%wide.region_15.16_spmd.clone.clone.clone, body=%wide.region_14.15_spmd.clone.clone.clone.sunk | while | flops 52180996 | bytes 715055 | solution.py:199
  356.0 0.8 fusion.218
  356.8 0.8 convolution_subtract_fusion.5
  357.6 0.8 fusion.219
  358.7 0.8 add_bitcast_fusion.2
  364.6 1.1 dynamic_update_slice.28
  366.5 161.4 %psum.30 = f32[2,48,48]{2,1,0:T(8,128)S(1)} all-reduce(f32[2,48,48]{2,1,0:T(8,128)S(1)} %get-tuple-element.576), channel_id=1, replica_groups=mesh['groups'=2,'src'=4,'tile'=2,'pix'=2] {'src','pix'}, use_global_device_ids=true, to_apply=%region_16.17 | all-reduce | flops 4608 | bytes 36864 | tf_op jit(solution)/shard_map/psum | solution.py:203
  527.9 1.1 convolution_negate_fusion
  529.0 1.1 fusion.102
  530.1 1.1 convolution_subtract_fusion.1
  531.2 1.1 convolution_subtract_fusion.2
  533.1 5.7 %psum.31 = f32[6]{0:T(128)S(1)} all-reduce(f32[6]{0:T(128)S(1)} %get-tuple-element.577), channel_id=1, replica_groups=mesh['groups'=2,'src'=4,'tile'=2,'pix'=2] {'tile','pix'}, use_global_device_ids=true, to_apply=%region_17.18 | all-reduce | flops 6 | bytes 48 | tf_op jit(solution)/shard_map/psum | solution.py:200
  540.0 1.6 fusion.77
  (142 shorter events, 28.5 us)
Async XLA Ops:
  7.2 1.0 copy-start
  7.2 36.4 %copy-start.2 = (s32[128]{0:T(128)S(1)}, s32[128]{0:T(128)}, u32[]{:S(2)}) copy-start(s32[128]{0:T(128)} %param.30) | copy-start | bytes 1540
  7.2 36.4 %copy-start.3 = (s32[4]{0:T(128)S(1)}, s32[4]{0:T(128)}, u32[]{:S(2)}) copy-start(s32[4]{0:T(128)} %param.31) | copy-start | bytes 52
  7.2 290.4 %all-reduce.3.cloned.1.call-start = ((), (), s32[]{:S(2)}) async-start(), calls=%async_computation | async-start | bytes 4194304 | tf_op jit(solution)/shard_map/psum | solution.py:146
  9.6 34.9 %slice-start = ((bf16[128,2048]{1,0:T(8,128)(2,1)}), bf16[6,2048]{1,0:T(8,128)(2,1)S(1)}, s32[]{:S(2)}) async-start(bf16[128,2048]{1,0:T(8,128)(2,1)} %param.28), calls=%async_computation.2 | async-start | bytes 65536 | tf_op jit(solution)/shard_map/slice | solution.py:114
  44.4 7.1 %copy-start.5 = (bf16[128]{0:T(256)(128)(2,1)S(1)}, bf16[128]{0:T(256)(128)(2,1)}, u32[]{:S(2)}) copy-start(bf16[128]{0:T(256)(128)(2,1)} %param.29) | copy-start | bytes 772
  132.0 1.0 copy-start.1
  132.0 1.9 copy-start.4
  132.0 197.5 %all-gather.2.cloned.1.call-start = ((), (), s32[]{:S(2)}) async-start(), calls=%async_computation.1 | async-start | bytes 1310720 | tf_op jit(solution)/shard_map/all_gather | solution.py:175
Sparse Core Ops, SparseCore 0:
  132.1 165.4 all-reduce.2
  300.4 29.1 all-gather.1
where the time goes:
time: 555 us; the launch traced here: 548 us
  blocking collectives  198 us (36%)
  waiting for transfers between devices  191 us (34%)
  local copies, waits for them, and re-layouts  77.1 us (14%)
  loops' own time  27.6 us (5%)
  other arithmetic  21.4 us (4%)
  matrix products  18 us (3%)
  between operations  15 us (3%)
    psum x1, waiting for transfers between devices, shards(): lax.psum(lax.map(intensity_one_block, begins).reshape(band, period), 'src')  163 us
    psum x1, blocking collectives, shards(): grad_spec = lax.psum(grad_spec, ('src', 'pix'))  161 us
    dynamic_update_slice x4, local copies, waits for them, and re-layouts, shards(): lax.map(intensity_one_block, begins).reshape(band, period)  57.7 us
    psum x1, blocking collectives, shards(): spectrum = lax.psum(partial_spec, ('src', 'pix'))  30.7 us
    all_gather x1, waiting for transfers between devices, shards(): received = lax.all_gather(slope, 'src', axis=0, tiled=True)  28.3 us
  transfers between devices with their start and end apart: 2, of which 2 were waited for; matrix products, arithmetic and copies ran while one was open for 0% of the time, Pallas kernels for 0%

commit v1 on v0

v1 whole, which is shorter than its diff:
```python
import functools
import math

import jax
import jax.numpy as jnp
import ml_dtypes
import numpy as np
from jax import lax
from jax.experimental import pallas as pl
from jax.experimental.pallas import tpu as pltpu
from jax.sharding import PartitionSpec as P

K = 32
SG = 17
W = 48
MOST = 6
CLASSES = 4
STEEP = 4.0

M = 64
LANES = 128
GROUP = 3
PUPIL_ROWS = MOST * W + 16

f32 = jnp.float32
bf16 = jnp.bfloat16


def split_np(table):
    table = np.asarray(table, np.float32)
    high = table.astype(ml_dtypes.bfloat16)
    low = (table - high.astype(np.float32)).astype(ml_dtypes.bfloat16)
    return high, low


def halves(left, right):
    out = np.zeros((left.shape[0], LANES))
    out[:, : left.shape[1]] = left
    out[:, M : M + right.shape[1]] = right
    return out


@functools.lru_cache(maxsize=None)
def tables(period, span):
    blocks = period // span
    freqs = np.arange(W) - W // 2
    pixels = np.arange(period)
    wide = 2.0 * np.pi / period * ((freqs[:, None] * pixels[None, :]) % period)
    wide_cos, wide_sin = np.cos(wide), np.sin(wide)
    coarse = 2.0 * np.pi / M * ((freqs[:, None] * np.arange(M)[None, :]) % M)
    coarse_cos, coarse_sin = np.cos(coarse), np.sin(coarse)
    high, low = split_np(halves(wide_cos.T, -wide_sin.T))
    spec_cols = np.concatenate([high, low], 1)
    rows = np.concatenate(
        [wide_cos.reshape(W, blocks, span), wide_sin.reshape(W, blocks, span)], 2
    ).transpose(1, 0, 2)
    high, low = split_np(rows / period)
    spec_rows = np.concatenate([high, low], 1)
    lift = np.concatenate(
        [
            np.pad(np.concatenate([coarse_cos, coarse_sin], 1), ((0, M - W), (0, 0))),
            np.pad(np.concatenate([-coarse_sin, coarse_cos], 1), ((0, M - W), (0, 0))),
        ],
        0,
    )
    high, low = split_np(lift)
    lift_cols = np.concatenate([high, low], 0)
    left = np.concatenate([coarse_cos.T, coarse_sin.T], 0) / K
    high, low = split_np(left)
    lift_rows = np.concatenate([high, low, high], 1)
    orders = np.arange(-(M // 2 - 1), M // 2)
    places = pixels[:, None] * (M / period) - np.arange(M)[None, :]
    inter = np.cos(2.0 * np.pi / M * places[:, :, None] * orders).sum(-1) / M
    high, low = split_np(inter)
    fine_cols = np.concatenate([high.T, low.T, high.T, low.T], 0)
    fold_cols = np.concatenate([high, low], 1)
    fine_rows = np.concatenate([high, low, high, low], 1).reshape(blocks, span, 4 * M)
    high_t = high.reshape(blocks, span, M).transpose(0, 2, 1)
    low_t = low.reshape(blocks, span, M).transpose(0, 2, 1)
    fold_rows = np.concatenate([high_t, low_t, high_t], 2)
    high, low = split_np(np.concatenate([coarse_cos, coarse_sin], 0))
    drop_rows = np.concatenate([high, low, high], 1)
    drop = np.concatenate(
        [halves(coarse_cos.T, -coarse_sin.T), halves(coarse_sin.T, coarse_cos.T)], 0
    )
    high, low = split_np(drop)
    drop_cols = np.concatenate([high, low, high], 0)
    rows = np.concatenate(
        [
            wide_cos.reshape(W, blocks, span).transpose(1, 2, 0),
            wide_sin.reshape(W, blocks, span).transpose(1, 2, 0),
        ],
        2,
    )
    high, low = split_np(rows / period)
    grad_rows = np.concatenate([high, low, high], 2)
    high, low = split_np(
        np.concatenate(
            [
                np.pad(wide_cos, ((0, M - W), (0, 0))),
                np.pad(wide_sin, ((0, M - W), (0, 0))),
            ],
            0,
        )
    )
    grad_cols = np.concatenate([high, low], 0)
    return dict(
        spec_cols=spec_cols,
        spec_rows=spec_rows,
        lift_cols=lift_cols,
        lift_rows=lift_rows,
        fine_cols=fine_cols,
        fold_cols=fold_cols,
        fine_rows=fine_rows,
        fold_rows=fold_rows,
        drop_rows=drop_rows,
        drop_cols=drop_cols,
        grad_rows=grad_rows,
        grad_cols=grad_cols,
    )


def dot(left, right):
    return jnp.dot(left, right, preferred_element_type=f32)


def split(value):
    high = value.astype(bf16)
    return high, (value - high.astype(f32)).astype(bf16)


def lane_of(shape):
    return lax.broadcasted_iota(jnp.int32, shape, len(shape) - 1)


def swap(value):
    return pltpu.roll(value, M, 1)


def signs(rows, low, high):
    return jnp.where(lane_of((rows, LANES)) < M, f32(low), f32(high))


def my_block():
    return lax.axis_index("src") * lax.axis_size("pix") + lax.axis_index("pix")


def spectrum_kernel(
    mask_ref, pupil_ref, weight_ref, cell_ref, active_ref, cols_ref, rows_ref,
    part_ref, placed_ref, lined, spread,
):
    src = lax.axis_index("src")
    active = active_ref[src]
    raw = pupil_ref[...].astype(f32)[:8]
    for piece in range(16):
        lined[pl.ds(piece, 8, stride=16), :] = raw[:, piece * LANES : (piece + 1) * LANES]
    spread[...] = jnp.zeros_like(spread)
    lane = lane_of((8, LANES))
    for slot in range(MOST):
        cell = cell_ref[slot]
        row, col = lax.div(cell, SG), lax.rem(cell, SG)
        live = slot < active
        real = lined[pl.ds(slot * 16, 8), :]
        imag = lined[pl.ds(slot * 16 + 8, 8), :]
        in_real = (lane >= col) & (lane < col + K) & live
        in_imag = (lane >= col + M) & (lane < col + M + K) & live
        for turn in range(4):
            shift = LANES - K * turn
            moved_real = pltpu.roll(real, lax.rem(col + shift, LANES), 1)
            moved_imag = pltpu.roll(imag, lax.rem(col + shift + M, LANES), 1)
            placed = jnp.where(in_real, moved_real, jnp.where(in_imag, moved_imag, 0.0))
            spread[pl.ds(slot * W + row + turn, 8, stride=4), :] = placed
    placed_ref[: MOST * W] = spread[...].astype(bf16)
    weights = jnp.broadcast_to(weight_ref[...].astype(f32).reshape(1, -1), (16, weight_ref.shape[-1]))
    diagonal = lax.broadcasted_iota(jnp.int32, weights.shape, 0) == lane_of(weights.shape)
    column = jnp.sum(jnp.where(diagonal, weights, 0.0), 1, keepdims=True)
    placed_ref[MOST * W :] = jnp.broadcast_to(column, (16, LANES)).astype(bf16)
    high, low = split(mask_ref[0])
    both = dot(high, cols_ref[...])
    part = both[:, :LANES] + both[:, LANES:] + dot(low, cols_ref[:, :LANES])
    turned = swap(part) * signs(part.shape[0], 1.0, -1.0)
    high, low = split(jnp.concatenate([part, turned], 0))
    table = rows_ref[my_block()]
    product = dot(table, jnp.concatenate([high, low], 1))
    part_ref[...] = product[:W, :LANES] + product[:W, LANES:] + product[W:, :LANES]


def spread_pupil(placed):
    other = swap(placed)
    low = lane_of(placed.shape) < M
    return jnp.where(low, placed, other), jnp.where(low, other, placed)


def source_index(part, item, count, src):
    return jnp.bitwise_xor(src, part) if count == 1 else item


def for_groups(pupil_refs, active_ref, body, state):
    src = lax.axis_index("src")
    for part, ref in enumerate(pupil_refs):
        count = ref.shape[0]

        def owners(item, state, part=part, ref=ref, count=count):
            owner = source_index(part, item, count, src)
            groups = lax.div(active_ref[owner] + (GROUP - 1), GROUP)
            return lax.fori_loop(
                0, groups, lambda group, inner: body(inner, ref, item, owner, group), state
            )

        state = owners(0, state) if count == 1 else lax.fori_loop(0, count, owners, state)
    return state


def weight_row(ref, item, slot):
    rows = ref[item, pl.ds(MOST * W, 16), :].astype(f32)
    pick = lax.broadcasted_iota(jnp.int32, rows.shape, 0) == slot
    return jnp.sum(jnp.where(pick, rows, 0.0), 0, keepdims=True)


def image_kernel(counts, *refs):
    n_spec, n_pupil, rows_out = counts
    spec_refs, refs = refs[:n_spec], refs[n_spec:]
    pupil_refs, refs = refs[:n_pupil], refs[n_pupil:]
    (
        target_ref, active_ref, class_ref, thresholds_ref,
        lift_cols, lift_rows, fine_rows, fine_cols, fold_cols, fold_rows,
        intensity_ref, fold_ref, fields_ref,
    ) = refs
    spectrum = sum(ref[...] for ref in spec_refs[1:]) + spec_refs[0][...] if n_spec > 1 else spec_refs[0][...]
    turned = swap(spectrum) * signs(W, -1.0, 1.0)
    many = jnp.concatenate([spectrum] * GROUP, 0)
    many_turned = jnp.concatenate([turned] * GROUP, 0)
    left = lift_rows[...]
    turn = signs(M, -1.0, 1.0)

    def forward(total, ref, item, owner, group):
        start = pl.multiple_of(group * (GROUP * W), 16)
        real, imag = spread_pupil(ref[item, pl.ds(start, GROUP * W), :].astype(f32))
        wave = (real * many + imag * many_turned).astype(bf16)
        high, low = split(dot(jnp.concatenate([wave, wave], 1), lift_cols[...]))
        for slot in range(GROUP):
            here = slice(slot * W, (slot + 1) * W)
            raw = dot(left, jnp.concatenate([high[here], high[here], low[here]], 0))
            field = raw[:M] + turn * swap(raw[M:])
            number = owner * MOST + group * GROUP + slot
            fields_ref[number] = field
            weight = weight_row(ref, item, group * GROUP + slot)
            total = total + weight * (field * field)
        return total

    power = for_groups(pupil_refs, active_ref, forward, jnp.zeros((M, LANES), f32))
    high, low = split(power + swap(power))
    block = my_block()
    half = dot(fine_rows[block], jnp.concatenate([high, high, low, low], 0))
    high, low = split(half)
    intensity = dot(jnp.concatenate([high, low], 1), fine_cols[...])
    intensity_ref[0] = intensity
    kind = class_ref[0]
    threshold = thresholds_ref[0]
    for number in range(1, CLASSES):
        threshold = jnp.where(kind == number, thresholds_ref[number], threshold)
    resist = 1.0 / (1.0 + jnp.exp(-STEEP * (intensity - threshold)))
    slope = (2.0 * STEEP * (resist - target_ref[0]) * resist * (1.0 - resist)).astype(bf16)
    folded = dot(slope, fold_cols[...])
    high, low = split(folded + swap(folded))
    grid = dot(fold_rows[block], jnp.concatenate([high, high, low], 0))
    lane = lane_of((M // 2, LANES))
    fold_ref[: M // 2] = jnp.where(lane < M, grid[: M // 2], grid[M // 2 :])
    fold_ref[M // 2 :] = jnp.zeros((rows_out - M // 2, LANES), f32)

    def weigh(none, ref, item, owner, group):
        for slot in range(GROUP):
            number = owner * MOST + group * GROUP + slot
            field = fields_ref[number]
            fold_ref[pl.ds(M // 2 + number, 1), :] = jnp.sum(grid * (field * field), 0, keepdims=True)
        return none

    for_groups(pupil_refs, active_ref, weigh, 0)


def gradient_kernel(counts, *refs):
    n_fold, n_pupil = counts
    fold_refs, refs = refs[:n_fold], refs[n_fold:]
    pupil_refs, refs = refs[:n_pupil], refs[n_pupil:]
    fields_ref, active_ref, drop_rows, drop_cols, grad_rows, grad_cols, mask_grad_ref = refs
    packed = fold_refs[0][: M // 2]
    for ref in fold_refs[1:]:
        packed = packed + ref[: M // 2]
    other = swap(packed)
    low_half = lane_of(packed.shape) < M
    grid = jnp.concatenate(
        [jnp.where(low_half, packed, other), jnp.where(low_half, other, packed)], 0
    )
    left = drop_rows[...]
    turn = signs(W, 1.0, -1.0)
    turn_many = signs(GROUP * W, 1.0, -1.0)

    def backward(total, ref, item, owner, group):
        waves = []
        for slot in range(GROUP):
            number = owner * MOST + group * GROUP + slot
            high, low = split(grid * fields_ref[number])
            raw = dot(left, jnp.concatenate([high, high, low], 0))
            waves.append(raw[:W] + turn * swap(raw[W:]))
        high, low = split(jnp.concatenate(waves, 0))
        back = dot(jnp.concatenate([high, high, low], 1), drop_cols[...])
        start = pl.multiple_of(group * (GROUP * W), 16)
        real, imag = spread_pupil(ref[item, pl.ds(start, GROUP * W), :].astype(f32))
        product = real * back + imag * (turn_many * swap(back))
        for slot in range(GROUP):
            weight = weight_row(ref, item, group * GROUP + slot) * (2.0 / K)
            total = total + weight * product[slot * W : (slot + 1) * W]
        return total

    grad = for_groups(pupil_refs, active_ref, backward, jnp.zeros((W, LANES), f32))
    high, low = split(jnp.concatenate([grad * turn, -swap(grad)], 0))
    half = dot(grad_rows[my_block()], jnp.concatenate([high, high, low], 0))
    high, low = split(half)
    mask_grad_ref[0] = dot(jnp.concatenate([high, high], 1), grad_cols[...]) + dot(
        low, grad_cols[:LANES]
    )


VMEM = pl.BlockSpec(memory_space=pltpu.VMEM)
SMEM = pl.BlockSpec(memory_space=pltpu.SMEM)
PARAMS = pltpu.CompilerParams(vmem_limit_bytes=48 * 1024 * 1024)


def others(value, axis):
    size = lax.axis_size(axis)
    return [
        lax.ppermute(value, axis, [(i, i ^ step) for i in range(size)]) for step in range(1, size)
    ]


def shards(
    mask, target, tile_class, thresholds, source_pupil, source_weight, source_cell, active_count
):
    span, period = mask.shape[1:]
    slots = source_pupil.shape[0]
    src_count = lax.axis_size("src")
    few = src_count in (2, 4)
    table = {name: jnp.asarray(value) for name, value in tables(period, span).items()}
    src = lax.axis_index("src")

    part, placed = pl.pallas_call(
        spectrum_kernel,
        grid=(1,),
        in_specs=[
            VMEM,
            pl.BlockSpec((16, source_pupil.shape[1]), lambda i: (0, 0)),
            VMEM, SMEM, SMEM, VMEM, VMEM,
        ],
        out_specs=[VMEM, VMEM],
        out_shape=[
            jax.ShapeDtypeStruct((W, LANES), f32),
            jax.ShapeDtypeStruct((PUPIL_ROWS, LANES), bf16),
        ],
        scratch_shapes=[pltpu.VMEM((LANES, LANES), f32), pltpu.VMEM((MOST * W, LANES), f32)],
        compiler_params=PARAMS,
        name="spectrum",
    )(
        mask, source_pupil, source_weight, source_cell, active_count,
        table["spec_cols"], table["spec_rows"],
    )

    def reduced(value):
        for other in others(value, "pix"):
            value = value + other
        if few:
            return [value] + others(value, "src")
        return [lax.psum(value, "src")]

    if few:
        pupils = [placed[None]] + [other[None] for other in others(placed, "src")]
    else:
        pupils = [lax.all_gather(placed, "src")]
    spectra = reduced(part)

    numbers = src_count * MOST
    fold_rows_out = M // 2 + -(-numbers // 8) * 8
    intensity, folded, fields = pl.pallas_call(
        functools.partial(image_kernel, (len(spectra), len(pupils), fold_rows_out)),
        in_specs=[VMEM] * (len(spectra) + len(pupils) + 1) + [SMEM] * 3 + [VMEM] * 6,
        out_specs=[VMEM] * 3,
        out_shape=[
            jax.ShapeDtypeStruct((1, span, period), f32),
            jax.ShapeDtypeStruct((fold_rows_out, LANES), f32),
            jax.ShapeDtypeStruct((numbers, M, LANES), f32),
        ],
        compiler_params=PARAMS,
        name="image",
    )(
        *spectra, *pupils, target, active_count, tile_class, thresholds,
        table["lift_cols"], table["lift_rows"], table["fine_rows"], table["fine_cols"],
        table["fold_cols"], table["fold_rows"],
    )

    folds = reduced(folded)
    first = M // 2 + src * MOST
    rows = sum(lax.dynamic_slice_in_dim(fold, first, MOST, 0) for fold in folds)
    for other in others(rows, "tile"):
        rows = rows + other
    mask_grad = pl.pallas_call(
        functools.partial(gradient_kernel, (len(folds), len(pupils))),
        in_specs=[VMEM] * (len(folds) + len(pupils) + 1) + [SMEM] + [VMEM] * 4,
        out_specs=VMEM,
        out_shape=jax.ShapeDtypeStruct((1, span, period), f32),
        compiler_params=PARAMS,
        name="gradient",
    )(
        *folds, *pupils, fields, active_count,
        table["drop_rows"], table["drop_cols"], table["grad_rows"], table["grad_cols"],
    )
    sums = jnp.sum(rows[:, :M] + rows[:, M:], 1) * (1.0 / (period * K))
    live = jnp.arange(MOST, dtype=jnp.int32) < active_count[src]
    source_grad = jnp.pad(jnp.where(live, sums, 0.0), (0, slots - MOST))
    return intensity, mask_grad, source_grad


def solution(mesh):
    in_specs = (
        P(("groups", "tile"), ("src", "pix"), None),
        P(("groups", "tile"), ("src", "pix"), None),
        P(("groups", "tile")),
        P(),
        P("src", None),
        P("src"),
        P("src"),
        P(),
    )
    out_specs = (
        P(("groups", "tile"), ("src", "pix"), None),
        P(("groups", "tile"), ("src", "pix"), None),
        P(("groups", "src")),
    )
    return jax.shard_map(shards, mesh=mesh, in_specs=in_specs, out_specs=out_specs, check_vma=False)
```

time: 555 us -> 52.2 us (0.09); the launches traced: 548 us -> 51.8 us
  blocking collectives: 198 us -> 0 us
  waiting for transfers between devices: 191 us -> 10 us
  local copies, waits for them, and re-layouts: 77.1 us -> 10.3 us
  loops' own time: 27.6 us -> 0 us
  other arithmetic: 21.4 us -> 0.86 us
  starting transfers between devices: 0.08 us -> 18.9 us
  matrix products: 18 us -> 0 us
  between operations: 15 us -> 1.41 us
  Pallas kernels: 0 us -> 10.3 us
    psum x3 -> x0, blocking collectives: 198 us -> none  [the longest x1 161 us: shards(): grad_spec = lax.psum(grad_spec, ('src', 'pix'))]
    psum x1 -> x0, waiting for transfers between devices: 163 us -> none  [shards(): lax.psum(lax.map(intensity_one_block, begins).reshape(band, period), 'src')]
    dynamic_update_slice x5 -> x0, local copies, waits for them, and re-layouts: 58.8 us -> none  [the longest x4 57.7 us: shards(): lax.map(intensity_one_block, begins).reshape(band, period)]
    all_gather x1 -> x0, waiting for transfers between devices: 28.3 us -> none  [shards(): received = lax.all_gather(slope, 'src', axis=0, tiled=True)]
    another operation x12 -> x0, loops' own time: 27.6 us -> none  [the longest x4 8.29 us: block_power(): lax.fori_loop(0, active, add_source, jnp.zeros((step, period), jnp.float32))]
    ppermute x0 -> x12, starting transfers between devices: none -> 18.9 us  [others(): lax.ppermute(value, axis, [(i, i ^ step) for i in range(size)])]
    dot_general x29 -> x0, matrix products: 18 us -> none  [the longest x8 2.65 us: field_of(): jnp.dot(left_table, stacked, preferred_element_type=jnp.float32) * (1.0 / K)]
    dynamic_slice x22 -> x1, local copies, waits for them, and re-layouts: 11.4 us -> 0.58 us  [shards(): live = jnp.arange(MOST, dtype=jnp.int32) < active_count[src]]
  transfers between devices with their start and end apart: 2 -> 12, of which waited for: 2 -> 6; matrix products, arithmetic and copies ran while one was open for 0% -> 1% of each run, Pallas kernels for 0% -> 9%
where the time goes in v1:
time: 52.2 us; the launch traced here: 51.8 us
  starting transfers between devices  18.9 us (36%)
  local copies, waits for them, and re-layouts  10.3 us (20%)
  Pallas kernels  10.3 us (20%)
  waiting for transfers between devices  10 us (19%)
  between operations  1.41 us (3%)
  other arithmetic  0.86 us (2%)
    ppermute x12, starting transfers between devices, others(): lax.ppermute(value, axis, [(i, i ^ step) for i in range(size)])  18.9 us
    ppermute x12, waiting for transfers between devices, others(): lax.ppermute(value, axis, [(i, i ^ step) for i in range(size)])  10 us
    unnamed x40, local copies, waits for them, and re-layouts  9.16 us
    pallas_call x1, Pallas kernels, shards(): pl.pallas_call(functools.partial(image_kernel, (len(spectra), len(pupils)...  4.86 us
    pallas_call x1, Pallas kernels, shards(): pl.pallas_call(functools.partial(gradient_kernel, (len(folds), len(pupils...  4.41 us
    pallas_call x1, Pallas kernels, shards(): pl.pallas_call(spectrum_kernel, grid=(1,), in_specs=[VMEM, pl.BlockSpec((...  1.08 us
  transfers between devices with their start and end apart: 12, of which 6 were waited for; matrix products, arithmetic and copies ran while one was open for 1% of the time, Pallas kernels for 9%

profile of v1, /device:TPU:0, one launch (start us, length us, event | category | flops | bytes accessed | tf_op | source)
XLA Modules:
  0.0 51.8 jit_solution(6921267717598608176)
XLA Ops:
  0.6 1.0 %copy-done.1 = f32[1,128,1024]{2,1,0:T(8,128)S(1)} copy-done((f32[1,128,1024]{2,1,0:T(8,128)S(1)}, f32[1,128,1024]{2,1,0:T(8,128)}, u32[]{:S(2)}) %copy-start.1) | copy-done | bytes 524312
  1.7 1.0 %copy-done.2 = bf16[128,2048]{1,0:T(8,128)(2,1)S(1)} copy-done((bf16[128,2048]{1,0:T(8,128)(2,1)S(1)}, bf16[128,2048]{1,0:T(8,128)(2,1)}, u32[]{:S(2)}) %copy-start.2) | copy-done | bytes 524312
  2.7 1.0 %copy-done.7 = bf16[1024,256]{1,0:T(8,128)(2,1)S(1)} copy-done((bf16[1024,256]{1,0:T(8,128)(2,1)S(1)}, bf16[1024,256]{1,0:T(8,128)(2,1)}, u32[]{:S(2)}) %copy-start.7) | copy-done | bytes 524312
  3.8 1.0 %copy-done.9 = bf16[8,96,256]{2,1,0:T(8,128)(2,1)S(1)} copy-done((bf16[8,96,256]{2,1,0:T(8,128)(2,1)S(1)}, bf16[8,96,256]{2,1,0:T(8,128)(2,1)}, u32[]{:S(2)}) %copy-start.9) | copy-done | bytes 393240
  4.8 0.7 %copy-done.15 = s32[4]{0:T(128)S(1)} copy-done((s32[4]{0:T(128)S(1)}, s32[4]{0:T(128)}, u32[]{:S(2)}) %copy-start.15) | copy-done | bytes 40
  5.4 0.7 %copy-done.17 = bf16[128]{0:T(256)(128)(2,1)S(1)} copy-done((bf16[128]{0:T(256)(128)(2,1)S(1)}, bf16[128]{0:T(256)(128)(2,1)}, u32[]{:S(2)}) %copy-start.17) | copy-done | bytes 280
  6.1 0.7 %copy-done.18 = s32[128]{0:T(128)S(1)} copy-done((s32[128]{0:T(128)S(1)}, s32[128]{0:T(128)}, u32[]{:S(2)}) %copy-start.18) | copy-done | bytes 536
  6.7 1.1 %spectrum.1 = (f32[48,128]{1,0:T(8,128)S(1)}, bf16[304,128]{1,0:T(8,128)(2,1)S(1)}) custom-call(f32[1,128,1024]{2,1,0:T(8,128)S(1)} %copy-done.1, bf16[128,2048]{1,0:T(8,128)(2,1)S(1)} %copy-done.2, bf16[128]{0:T(256)(128)(2,1)S(1)} %copy-done.17, s32[128]{0:T(128)S(1)} %copy-done.18, s32[4]{0:T(128)S(1)} %copy-done.15, bf16[1024,256]{1,0:T(8,128)(2,1)S(1)} %copy-done.7, ...), custom_call_target="tpu_custom_call" | custom-call | tf_op jit(solution)/shard_map/spectrum/pallas_call | solution.py:346
  7.8 0.0 copy-start.12
  7.8 3.1 %collective-permute-start.4 = (bf16[304,128]{1,0:T(8,128)(2,1)S(1)}, bf16[304,128]{1,0:T(8,128)(2,1)S(1)}, u32[]{:S(2)}, u32[]{:S(2)}) collective-permute-start(bf16[304,128]{1,0:T(8,128)(2,1)S(1)} %get-tuple-element.9), channel_id=1, source_target_pairs={{0,4},{4,0},{8,12},{12,8},{1,5},{5,1},{9,13},{13,9},{2,6},{6,2},{1... | collective-permute-start | bytes 233480 | tf_op jit(solution)/shard_map/ppermute | solution.py:332
  10.9 2.6 %collective-permute-start.5 = (bf16[304,128]{1,0:T(8,128)(2,1)S(1)}, bf16[304,128]{1,0:T(8,128)(2,1)S(1)}, u32[]{:S(2)}, u32[]{:S(2)}) collective-permute-start(bf16[304,128]{1,0:T(8,128)(2,1)S(1)} %get-tuple-element.9), channel_id=1, source_target_pairs={{0,8},{4,12},{8,0},{12,4},{1,9},{5,13},{9,1},{13,5},{2,10},{6,14},... | collective-permute-start | bytes 233480 | tf_op jit(solution)/shard_map/ppermute | solution.py:332
  13.5 0.0 collective-permute-start.6
  13.5 0.0 collective-permute-start
  13.5 1.2 %collective-permute-done = f32[48,128]{1,0:T(8,128)S(1)} collective-permute-done((f32[48,128]{1,0:T(8,128)S(1)}, f32[48,128]{1,0:T(8,128)S(1)}, u32[]{:S(2)}, u32[]{:S(2)}) %collective-permute-start) | collective-permute-done | bytes 24608 | tf_op jit(solution)/shard_map/ppermute | solution.py:332
  14.7 0.9 %collective-permute-start.1 = (f32[48,128]{1,0:T(8,128)S(1)}, f32[48,128]{1,0:T(8,128)S(1)}, u32[]{:S(2)}, u32[]{:S(2)}) collective-permute-start(f32[48,128]{1,0:T(8,128)S(1)} %add.34.refs_0_), channel_id=1, source_target_pairs={{0,4},{4,0},{8,12},{12,8},{1,5},{5,1},{9,13},{13,9},{2,6},{6,2},{1... | collective-permute-start | bytes 73736 | tf_op jit(solution)/shard_map/ppermute | solution.py:332
  15.6 3.5 %collective-permute-start.2 = (f32[48,128]{1,0:T(8,128)S(1)}, f32[48,128]{1,0:T(8,128)S(1)}, u32[]{:S(2)}, u32[]{:S(2)}) collective-permute-start(f32[48,128]{1,0:T(8,128)S(1)} %add.34.refs_0_), channel_id=1, source_target_pairs={{0,8},{4,12},{8,0},{12,4},{1,9},{5,13},{9,1},{13,5},{2,10},{6,14},... | collective-permute-start | bytes 73736 | tf_op jit(solution)/shard_map/ppermute | solution.py:332
  19.1 0.8 %collective-permute-done.1.refs_1_ = f32[48,128]{1,0:T(8,128)S(1)} collective-permute-done((f32[48,128]{1,0:T(8,128)S(1)}, f32[48,128]{1,0:T(8,128)S(1)}, u32[]{:S(2)}, u32[]{:S(2)}) %collective-permute-start.1) | collective-permute-done | bytes 24608 | tf_op jit(solution)/shard_map/ppermute | solution.py:332
  19.9 2.9 %collective-permute-start.3 = (f32[48,128]{1,0:T(8,128)S(1)}, f32[48,128]{1,0:T(8,128)S(1)}, u32[]{:S(2)}, u32[]{:S(2)}) collective-permute-start(f32[48,128]{1,0:T(8,128)S(1)} %add.34.refs_0_), channel_id=1, source_target_pairs={{0,12},{4,8},{8,4},{12,0},{1,13},{5,9},{9,5},{13,1},{2,14},{6,10},... | collective-permute-start | bytes 73736 | tf_op jit(solution)/shard_map/ppermute | solution.py:332
  23.4 0.0 collective-permute-done.2.refs_2_
  23.4 2.1 %collective-permute-done.3.refs_3_ = f32[48,128]{1,0:T(8,128)S(1)} collective-permute-done((f32[48,128]{1,0:T(8,128)S(1)}, f32[48,128]{1,0:T(8,128)S(1)}, u32[]{:S(2)}, u32[]{:S(2)}) %collective-permute-start.3) | collective-permute-done | bytes 24608 | tf_op jit(solution)/shard_map/ppermute | solution.py:332
  25.5 0.0 collective-permute-done.4
  25.5 0.0 collective-permute-done.5
  25.5 0.0 collective-permute-done.6
  25.5 0.0 copy-start.19
  25.5 0.0 copy-done.3
  25.6 0.0 copy-done.5
  25.6 0.0 copy-done.6
  25.6 0.0 copy-done.8
  25.6 0.6 %copy-done.19 = f32[4]{0:T(128)S(1)} copy-done((f32[4]{0:T(128)S(1)}, f32[4]{0:T(128)}, u32[]{:S(2)}) %copy-start.19) | copy-done | bytes 40
  26.2 0.9 %copy-done.10 = bf16[1024,128]{1,0:T(8,128)(2,1)S(1)} copy-done((bf16[1024,128]{1,0:T(8,128)(2,1)S(1)}, bf16[1024,128]{1,0:T(8,128)(2,1)}, u32[]{:S(2)}) %copy-start.10) | copy-done | bytes 262168
  27.1 0.8 %copy-done.13 = bf16[128,144]{1,0:T(8,128)(2,1)S(1)} copy-done((bf16[128,144]{1,0:T(8,128)(2,1)S(1)}, bf16[128,144]{1,0:T(8,128)(2,1)}, u32[]{:S(2)}) %copy-start.13) | copy-done | bytes 36888
  28.0 4.9 %image.1 = (f32[1,128,1024]{2,1,0:T(8,128)}, f32[56,128]{1,0:T(8,128)S(1)}, f32[24,64,128]{2,1,0:T(8,128)S(1)}) custom-call(f32[48,128]{1,0:T(8,128)S(1)} %add.34.refs_0_, f32[48,128]{1,0:T(8,128)S(1)} %collective-permute-done.1.refs_1_, f32[48,128]{1,0:T(8,128)S(1)} %collective-permute-done.2.refs_2_, f32[48,128]{1,0:T(8,128)S(1)} %collective-permute-done.3.refs_3_, ...), custom_call_target="tpu_custom_call" | custom-call | tf_op jit(solution)/shard_map/image/pallas_call | solution.py:382
  32.9 0.0 collective-permute-start.7
  32.9 1.2 %collective-permute-done.7 = f32[56,128]{1,0:T(8,128)S(1)} collective-permute-done((f32[56,128]{1,0:T(8,128)S(1)}, f32[56,128]{1,0:T(8,128)S(1)}, u32[]{:S(2)}, u32[]{:S(2)}) %collective-permute-start.7) | collective-permute-done | bytes 28704 | tf_op jit(solution)/shard_map/ppermute | solution.py:332
  34.1 0.0 collective-permute-start.8
  34.1 3.4 %collective-permute-start.9 = (f32[56,128]{1,0:T(8,128)S(1)}, f32[56,128]{1,0:T(8,128)S(1)}, u32[]{:S(2)}, u32[]{:S(2)}) collective-permute-start(f32[56,128]{1,0:T(8,128)S(1)} %add.35.refs_0_), channel_id=1, source_target_pairs={{0,8},{4,12},{8,0},{12,4},{1,9},{5,13},{9,1},{13,5},{2,10},{6,14},... | collective-permute-start | bytes 86024 | tf_op jit(solution)/shard_map/ppermute | solution.py:332
  37.5 1.0 %collective-permute-start.10 = (f32[56,128]{1,0:T(8,128)S(1)}, f32[56,128]{1,0:T(8,128)S(1)}, u32[]{:S(2)}, u32[]{:S(2)}) collective-permute-start(f32[56,128]{1,0:T(8,128)S(1)} %add.35.refs_0_), channel_id=1, source_target_pairs={{0,12},{4,8},{8,4},{12,0},{1,13},{5,9},{9,5},{13,1},{2,14},{6,10},... | collective-permute-start | bytes 86024 | tf_op jit(solution)/shard_map/ppermute | solution.py:332
  38.5 0.0 collective-permute-done.8.refs_1_
  38.5 1.1 %collective-permute-done.9.refs_2_ = f32[56,128]{1,0:T(8,128)S(1)} collective-permute-done((f32[56,128]{1,0:T(8,128)S(1)}, f32[56,128]{1,0:T(8,128)S(1)}, u32[]{:S(2)}, u32[]{:S(2)}) %collective-permute-start.9) | collective-permute-done | bytes 28704 | tf_op jit(solution)/shard_map/ppermute | solution.py:332
  39.6 3.6 %collective-permute-done.10.refs_3_ = f32[56,128]{1,0:T(8,128)S(1)} collective-permute-done((f32[56,128]{1,0:T(8,128)S(1)}, f32[56,128]{1,0:T(8,128)S(1)}, u32[]{:S(2)}, u32[]{:S(2)}) %collective-permute-start.10) | collective-permute-done | bytes 28704 | tf_op jit(solution)/shard_map/ppermute | solution.py:332
  43.2 1.6 %collective-permute-start.11 = (f32[6,128]{1,0:T(8,128)S(1)}, f32[6,128]{1,0:T(8,128)S(1)}, u32[]{:S(2)}, u32[]{:S(2)}) collective-permute-start(f32[6,128]{1,0:T(8,128)S(1)} %dynamic-slice_add_fusion), channel_id=1, source_target_pairs={{0,2},{2,0},{1,3},{3,1},{4,6},{6,4},{5,7},{7,5},{8,10},{10,8},{9,1... | collective-permute-start | bytes 9224 | tf_op jit(solution)/shard_map/ppermute | solution.py:332
  44.7 0.7 %copy-done.16 = s32[4]{0:T(128)S(1)} copy-done((s32[4]{0:T(128)S(1)}, s32[4]{0:T(128)}, u32[]{:S(2)}) %copy-start.16) | copy-done | bytes 40
  45.4 0.6 %dynamic_slice.15 = s32[1]{0:T(128)} dynamic-slice(s32[4]{0:T(128)S(1)} %copy-done.16, s32[]{:T(128)S(6)} %select_n.13), dynamic_slice_sizes={1} | dynamic-slice | bytes 12 | tf_op jit(solution)/shard_map/dynamic_slice | solution.py:416
  46.0 4.4 %gradient.1 = f32[1,128,1024]{2,1,0:T(8,128)} custom-call(f32[56,128]{1,0:T(8,128)S(1)} %add.35.refs_0_, f32[56,128]{1,0:T(8,128)S(1)} %collective-permute-done.8.refs_1_, f32[56,128]{1,0:T(8,128)S(1)} %collective-permute-done.9.refs_2_, f32[56,128]{1,0:T(8,128)S(1)} %collective-permute-done.10.refs_3_, bf16[1,304,128]{2,1,0:T(8,128)(2,1)S(1)} %bitcast.6, ...), custom_call_target="tpu_custom_call" | custom-call | tf_op jit(solution)/shard_map/gradient/pallas_call | solution.py:404
  50.4 0.0 collective-permute-done.11
  50.4 0.2 add_reduce_fusion
  50.6 0.7 %compare_select_fusion = f32[6]{0:T(128)S(1)} fusion(f32[6]{0:T(128)S(1)} %add_reduce_fusion, s32[]{:T(128)} %bitcast.4), kind=kLoop, calls=%fused_computation.2 | loop fusion | flops 18 | bytes 52 | tf_op jit(solution)/shard_map/jit(_where)/select_n | solution.py:417
  51.3 0.5 pad.4
  (27 shorter events, 0.1 us)
Async XLA Ops:
  0.6 1.0 %copy-start.1 = (f32[1,128,1024]{2,1,0:T(8,128)S(1)}, f32[1,128,1024]{2,1,0:T(8,128)}, u32[]{:S(2)}) copy-start(f32[1,128,1024]{2,1,0:T(8,128)} %mask_ref.1) | copy-start | bytes 1572868
  1.7 1.0 %copy-start.2 = (bf16[128,2048]{1,0:T(8,128)(2,1)S(1)}, bf16[128,2048]{1,0:T(8,128)(2,1)}, u32[]{:S(2)}) copy-start(bf16[128,2048]{1,0:T(8,128)(2,1)} %pupil_ref.1) | copy-start | bytes 1572868
  2.7 1.0 %copy-start.7 = (bf16[1024,256]{1,0:T(8,128)(2,1)S(1)}, bf16[1024,256]{1,0:T(8,128)(2,1)}, u32[]{:S(2)}) copy-start(bf16[1024,256]{1,0:T(8,128)(2,1)} %constant.45.clone.cols_ref) | copy-start | bytes 1572868
  3.8 1.0 %copy-start.9 = (bf16[8,96,256]{2,1,0:T(8,128)(2,1)S(1)}, bf16[8,96,256]{2,1,0:T(8,128)(2,1)}, u32[]{:S(2)}) copy-start(bf16[8,96,256]{2,1,0:T(8,128)(2,1)} %constant.46.clone.rows_ref) | copy-start | bytes 1179652
  4.8 0.7 %copy-start.15 = (s32[4]{0:T(128)S(1)}, s32[4]{0:T(128)}, u32[]{:S(2)}) copy-start(s32[4]{0:T(128)} %refs_9_.3) | copy-start | bytes 52
  5.4 0.7 %copy-start.17 = (bf16[128]{0:T(256)(128)(2,1)S(1)}, bf16[128]{0:T(256)(128)(2,1)}, u32[]{:S(2)}) copy-start(bf16[128]{0:T(256)(128)(2,1)} %weight_ref.1) | copy-start | bytes 772
  6.1 0.7 %copy-start.18 = (s32[128]{0:T(128)S(1)}, s32[128]{0:T(128)}, u32[]{:S(2)}) copy-start(s32[128]{0:T(128)} %cell_ref.1) | copy-start | bytes 1540
  6.7 18.8 %copy-start.3 = (f32[1,128,1024]{2,1,0:T(8,128)S(1)}, f32[1,128,1024]{2,1,0:T(8,128)}, u32[]{:S(2)}) copy-start(f32[1,128,1024]{2,1,0:T(8,128)} %refs_8_.1) | copy-start | bytes 1572868
  6.7 18.8 %copy-start.5 = (bf16[8,128,256]{2,1,0:T(8,128)(2,1)S(1)}, bf16[8,128,256]{2,1,0:T(8,128)(2,1)}, u32[]{:S(2)}) copy-start(bf16[8,128,256]{2,1,0:T(8,128)(2,1)} %constant.51.clone.refs_14_) | copy-start | bytes 1572868
  6.7 18.8 %copy-start.6 = (bf16[256,1024]{1,0:T(8,128)(2,1)S(1)}, bf16[256,1024]{1,0:T(8,128)(2,1)}, u32[]{:S(2)}) copy-start(bf16[256,1024]{1,0:T(8,128)(2,1)} %constant.49.clone.refs_15_) | copy-start | bytes 1572868
  6.7 18.9 %copy-start.8 = (bf16[8,64,384]{2,1,0:T(8,128)(2,1)S(1)}, bf16[8,64,384]{2,1,0:T(8,128)(2,1)}, u32[]{:S(2)}) copy-start(bf16[8,64,384]{2,1,0:T(8,128)(2,1)} %constant.52.clone.refs_17_) | copy-start | bytes 1179652
  7.8 17.8 %copy-start.12 = (bf16[256,128]{1,0:T(8,128)(2,1)S(1)}, bf16[256,128]{1,0:T(8,128)(2,1)}, u32[]{:S(2)}) copy-start(bf16[256,128]{1,0:T(8,128)(2,1)} %constant.47.clone.refs_12_) | copy-start | bytes 196612
  7.8 17.7 %collective-permute-start.4 = (bf16[304,128]{1,0:T(8,128)(2,1)S(1)}, bf16[304,128]{1,0:T(8,128)(2,1)S(1)}, u32[]{:S(2)}, u32[]{:S(2)}) collective-permute-start(bf16[304,128]{1,0:T(8,128)(2,1)S(1)} %get-tuple-element.9), channel_id=1, source_target_pairs={{0,4},{4,0},{8,12},{12,8},{1,5},{5,1},{9,13},{13,9},{2,6},{6,2},{1... | collective-permute-start | bytes 233480 | tf_op jit(solution)/shard_map/ppermute | solution.py:332
  10.9 14.6 %collective-permute-start.5 = (bf16[304,128]{1,0:T(8,128)(2,1)S(1)}, bf16[304,128]{1,0:T(8,128)(2,1)S(1)}, u32[]{:S(2)}, u32[]{:S(2)}) collective-permute-start(bf16[304,128]{1,0:T(8,128)(2,1)S(1)} %get-tuple-element.9), channel_id=1, source_target_pairs={{0,8},{4,12},{8,0},{12,4},{1,9},{5,13},{9,1},{13,5},{2,10},{6,14},... | collective-permute-start | bytes 233480 | tf_op jit(solution)/shard_map/ppermute | solution.py:332
  13.5 12.0 %collective-permute-start.6 = (bf16[304,128]{1,0:T(8,128)(2,1)S(1)}, bf16[304,128]{1,0:T(8,128)(2,1)S(1)}, u32[]{:S(2)}, u32[]{:S(2)}) collective-permute-start(bf16[304,128]{1,0:T(8,128)(2,1)S(1)} %get-tuple-element.9), channel_id=1, source_target_pairs={{0,12},{4,8},{8,4},{12,0},{1,13},{5,9},{9,5},{13,1},{2,14},{6,10},... | collective-permute-start | bytes 233480 | tf_op jit(solution)/shard_map/ppermute | solution.py:332
  13.5 1.2 %collective-permute-start = (f32[48,128]{1,0:T(8,128)S(1)}, f32[48,128]{1,0:T(8,128)S(1)}, u32[]{:S(2)}, u32[]{:S(2)}) collective-permute-start(f32[48,128]{1,0:T(8,128)S(1)} %get-tuple-element.8), channel_id=1, source_target_pairs={{0,1},{1,0},{2,3},{3,2},{4,5},{5,4},{6,7},{7,6},{8,9},{9,8},{10,11... | collective-permute-start | bytes 73736 | tf_op jit(solution)/shard_map/ppermute | solution.py:332
  14.7 5.2 %collective-permute-start.1 = (f32[48,128]{1,0:T(8,128)S(1)}, f32[48,128]{1,0:T(8,128)S(1)}, u32[]{:S(2)}, u32[]{:S(2)}) collective-permute-start(f32[48,128]{1,0:T(8,128)S(1)} %add.34.refs_0_), channel_id=1, source_target_pairs={{0,4},{4,0},{8,12},{12,8},{1,5},{5,1},{9,13},{13,9},{2,6},{6,2},{1... | collective-permute-start | bytes 73736 | tf_op jit(solution)/shard_map/ppermute | solution.py:332
  15.6 7.8 %collective-permute-start.2 = (f32[48,128]{1,0:T(8,128)S(1)}, f32[48,128]{1,0:T(8,128)S(1)}, u32[]{:S(2)}, u32[]{:S(2)}) collective-permute-start(f32[48,128]{1,0:T(8,128)S(1)} %add.34.refs_0_), channel_id=1, source_target_pairs={{0,8},{4,12},{8,0},{12,4},{1,9},{5,13},{9,1},{13,5},{2,10},{6,14},... | collective-permute-start | bytes 73736 | tf_op jit(solution)/shard_map/ppermute | solution.py:332
  19.9 5.6 %collective-permute-start.3 = (f32[48,128]{1,0:T(8,128)S(1)}, f32[48,128]{1,0:T(8,128)S(1)}, u32[]{:S(2)}, u32[]{:S(2)}) collective-permute-start(f32[48,128]{1,0:T(8,128)S(1)} %add.34.refs_0_), channel_id=1, source_target_pairs={{0,12},{4,8},{8,4},{12,0},{1,13},{5,9},{9,5},{13,1},{2,14},{6,10},... | collective-permute-start | bytes 73736 | tf_op jit(solution)/shard_map/ppermute | solution.py:332
  25.5 0.7 %copy-start.19 = (f32[4]{0:T(128)S(1)}, f32[4]{0:T(128)}, u32[]{:S(2)}) copy-start(f32[4]{0:T(128)} %refs_11_.2) | copy-start | bytes 52
  26.2 0.9 %copy-start.10 = (bf16[1024,128]{1,0:T(8,128)(2,1)S(1)}, bf16[1024,128]{1,0:T(8,128)(2,1)}, u32[]{:S(2)}) copy-start(bf16[1024,128]{1,0:T(8,128)(2,1)} %constant.50.clone.refs_16_) | copy-start | bytes 786436
  27.1 0.8 %copy-start.13 = (bf16[128,144]{1,0:T(8,128)(2,1)S(1)}, bf16[128,144]{1,0:T(8,128)(2,1)}, u32[]{:S(2)}) copy-start(bf16[128,144]{1,0:T(8,128)(2,1)} %constant.48.clone.refs_13_) | copy-start | bytes 110596
  28.0 18.0 %copy-start = (bf16[8,128,288]{2,1,0:T(8,128)(2,1)S(1)}, bf16[8,128,288]{2,1,0:T(8,128)(2,1)}, u32[]{:S(2)}) copy-start(bf16[8,128,288]{2,1,0:T(8,128)(2,1)} %constant.55.clone.refs_12_) | copy-start | bytes 1769476
  28.0 18.0 %copy-start.4 = (bf16[256,1024]{1,0:T(8,128)(2,1)S(1)}, bf16[256,1024]{1,0:T(8,128)(2,1)}, u32[]{:S(2)}) copy-start(bf16[256,1024]{1,0:T(8,128)(2,1)} %constant.56.clone.refs_13_) | copy-start | bytes 1572868
  28.0 18.0 %copy-start.14 = (bf16[96,192]{1,0:T(8,128)(2,1)S(1)}, bf16[96,192]{1,0:T(8,128)(2,1)}, u32[]{:S(2)}) copy-start(bf16[96,192]{1,0:T(8,128)(2,1)} %constant.53.clone.refs_10_) | copy-start | bytes 110596
  32.9 13.1 %copy-start.11 = (bf16[384,128]{1,0:T(8,128)(2,1)S(1)}, bf16[384,128]{1,0:T(8,128)(2,1)}, u32[]{:S(2)}) copy-start(bf16[384,128]{1,0:T(8,128)(2,1)} %constant.54.clone.refs_11_) | copy-start | bytes 294916
  32.9 1.2 %collective-permute-start.7 = (f32[56,128]{1,0:T(8,128)S(1)}, f32[56,128]{1,0:T(8,128)S(1)}, u32[]{:S(2)}, u32[]{:S(2)}) collective-permute-start(f32[56,128]{1,0:T(8,128)S(1)} %get-tuple-element.11), channel_id=1, source_target_pairs={{0,1},{1,0},{2,3},{3,2},{4,5},{5,4},{6,7},{7,6},{8,9},{9,8},{10,11... | collective-permute-start | bytes 86024 | tf_op jit(solution)/shard_map/ppermute | solution.py:332
  34.1 4.4 %collective-permute-start.8 = (f32[56,128]{1,0:T(8,128)S(1)}, f32[56,128]{1,0:T(8,128)S(1)}, u32[]{:S(2)}, u32[]{:S(2)}) collective-permute-start(f32[56,128]{1,0:T(8,128)S(1)} %add.35.refs_0_), channel_id=1, source_target_pairs={{0,4},{4,0},{8,12},{12,8},{1,5},{5,1},{9,13},{13,9},{2,6},{6,2},{1... | collective-permute-start | bytes 86024 | tf_op jit(solution)/shard_map/ppermute | solution.py:332
  34.1 5.5 %collective-permute-start.9 = (f32[56,128]{1,0:T(8,128)S(1)}, f32[56,128]{1,0:T(8,128)S(1)}, u32[]{:S(2)}, u32[]{:S(2)}) collective-permute-start(f32[56,128]{1,0:T(8,128)S(1)} %add.35.refs_0_), channel_id=1, source_target_pairs={{0,8},{4,12},{8,0},{12,4},{1,9},{5,13},{9,1},{13,5},{2,10},{6,14},... | collective-permute-start | bytes 86024 | tf_op jit(solution)/shard_map/ppermute | solution.py:332
  37.5 5.7 %collective-permute-start.10 = (f32[56,128]{1,0:T(8,128)S(1)}, f32[56,128]{1,0:T(8,128)S(1)}, u32[]{:S(2)}, u32[]{:S(2)}) collective-permute-start(f32[56,128]{1,0:T(8,128)S(1)} %add.35.refs_0_), channel_id=1, source_target_pairs={{0,12},{4,8},{8,4},{12,0},{1,13},{5,9},{9,5},{13,1},{2,14},{6,10},... | collective-permute-start | bytes 86024 | tf_op jit(solution)/shard_map/ppermute | solution.py:332
  43.2 7.2 %collective-permute-start.11 = (f32[6,128]{1,0:T(8,128)S(1)}, f32[6,128]{1,0:T(8,128)S(1)}, u32[]{:S(2)}, u32[]{:S(2)}) collective-permute-start(f32[6,128]{1,0:T(8,128)S(1)} %dynamic-slice_add_fusion), channel_id=1, source_target_pairs={{0,2},{2,0},{1,3},{3,1},{4,6},{6,4},{5,7},{7,5},{8,10},{10,8},{9,1... | collective-permute-start | bytes 9224 | tf_op jit(solution)/shard_map/ppermute | solution.py:332
  44.7 0.7 %copy-start.16 = (s32[4]{0:T(128)S(1)}, s32[4]{0:T(128)}, u32[]{:S(2)}) copy-start(s32[4]{0:T(128)} %refs_9_.3) | copy-start | bytes 52

commit v2 on v1

v2 whole, which is shorter than its diff:
```python
import functools

import jax
import jax.numpy as jnp
import ml_dtypes
import numpy as np
from jax import lax
from jax.experimental import pallas as pl
from jax.experimental.pallas import tpu as pltpu
from jax.sharding import PartitionSpec as P

K = 32
SG = 17
W = 48
MOST = 6
CLASSES = 4
STEEP = 4.0

M = 64
LANES = 128
PAIRS = MOST // 2
AT_PUPILS = 2 * W
AT_TAIL = AT_PUPILS + PAIRS * K
ROWS = AT_TAIL + 16
TAIL_PAIR, TAIL_CELL = 8, 12

f32 = jnp.float32
bf16 = jnp.bfloat16


def split_np(table):
    table = np.asarray(table, np.float32)
    high = table.astype(ml_dtypes.bfloat16)
    low = (table - high.astype(np.float32)).astype(ml_dtypes.bfloat16)
    return high, low


def halves(left, right):
    out = np.zeros((left.shape[0], LANES))
    out[:, : left.shape[1]] = left
    out[:, M : M + right.shape[1]] = right
    return out


@functools.lru_cache(maxsize=None)
def tables(period, span):
    blocks = period // span
    freqs = np.arange(W) - W // 2
    pixels = np.arange(period)
    wide = 2.0 * np.pi / period * ((freqs[:, None] * pixels[None, :]) % period)
    wide_cos, wide_sin = np.cos(wide), np.sin(wide)
    narrow = np.arange(K) - K // 2
    coarse = 2.0 * np.pi / M * ((narrow[:, None] * np.arange(M)[None, :]) % M)
    coarse_cos, coarse_sin = np.cos(coarse), np.sin(coarse)
    near = 2.0 * np.pi / period * ((narrow[:, None] * pixels[None, :]) % period)
    gain = sum(
        (wave * wave.astype(np.float32).astype(ml_dtypes.bfloat16).astype(np.float64)).mean(1)
        for wave in (np.cos(near), np.sin(near))
    )
    rounded_cos, rounded_sin = gain[:, None] * coarse_cos, gain[:, None] * coarse_sin
    high, low = split_np(halves(wide_cos.T, -wide_sin.T))
    spec_cols = np.concatenate([high, low], 1)
    rows = np.concatenate(
        [wide_cos.reshape(W, blocks, span), wide_sin.reshape(W, blocks, span)], 2
    ).transpose(1, 0, 2)
    high, low = split_np(rows / period)
    spec_rows = np.concatenate([high, low], 1)
    def pair_table(cos, sin):
        out = np.zeros((4 * K, 4 * M))
        for slot in range(2):
            real, imag, at = slot * K, (2 + slot) * K, slot * 2 * M
            out[real : real + K, at : at + 2 * M] = np.concatenate([cos, sin], 1)
            out[imag : imag + K, at : at + 2 * M] = np.concatenate([-sin, cos], 1)
        return out

    high, low = split_np(pair_table(rounded_cos, rounded_sin))
    lift_cols = np.concatenate([high, low], 0)
    high, low = split_np(np.concatenate([rounded_cos.T, rounded_sin.T], 0) / K)
    lift_rows = np.concatenate([high, low, high], 1)
    orders = np.arange(-(M // 2 - 1), M // 2)
    places = pixels[:, None] * (M / period) - np.arange(M)[None, :]
    inter = np.cos(2.0 * np.pi / M * places[:, :, None] * orders).sum(-1) / M
    high, low = split_np(inter)
    fine_cols = np.concatenate([high.T, low.T, high.T, low.T], 0)
    fold_cols = np.concatenate([high, low], 1)
    fine_rows = np.concatenate([high, low, high, low], 1).reshape(blocks, span, 4 * M)
    high_t = high.reshape(blocks, span, M).transpose(0, 2, 1)
    low_t = low.reshape(blocks, span, M).transpose(0, 2, 1)
    fold_rows = np.concatenate([high_t, low_t, high_t], 2)
    high, low = split_np(np.concatenate([rounded_cos, rounded_sin], 0))
    drop_rows = np.concatenate([high, low, high], 1)
    high, low = split_np(pair_table(coarse_cos, coarse_sin).T)
    drop_cols = np.concatenate([high, low, high], 0)
    rows = np.concatenate(
        [
            wide_cos.reshape(W, blocks, span).transpose(1, 2, 0),
            wide_sin.reshape(W, blocks, span).transpose(1, 2, 0),
        ],
        2,
    )
    high, low = split_np(rows / period)
    grad_rows = np.concatenate([high, low, high], 2)
    padded = [np.pad(part, ((0, M - W), (0, 0))) for part in (wide_cos, wide_sin)]
    high, low = split_np(np.concatenate(padded, 0))
    grad_cols = np.concatenate([high, low], 0)
    return dict(
        spec_cols=spec_cols,
        spec_rows=spec_rows,
        lift_cols=lift_cols,
        lift_rows=lift_rows,
        fine_cols=fine_cols,
        fold_cols=fold_cols,
        fine_rows=fine_rows,
        fold_rows=fold_rows,
        drop_rows=drop_rows,
        drop_cols=drop_cols,
        grad_rows=grad_rows,
        grad_cols=grad_cols,
    )


def dot(left, right):
    return jnp.dot(left, right, preferred_element_type=f32)


def split(value):
    high = value.astype(bf16)
    return high, (value - high.astype(f32)).astype(bf16)


def lane_of(shape):
    return lax.broadcasted_iota(jnp.int32, shape, len(shape) - 1)


def row_of(shape):
    return lax.broadcasted_iota(jnp.int32, shape, 0)


def swap(value):
    return pltpu.roll(value, M, 1)


def signs(rows, low, high):
    return jnp.where(lane_of((rows, LANES)) < M, f32(low), f32(high))


def my_block():
    return lax.axis_index("src") * lax.axis_size("pix") + lax.axis_index("pix")


def copies(sems, *pairs):
    out = [
        pltpu.make_async_copy(source, place, sems.at[number])
        for number, (source, place) in enumerate(pairs)
    ]
    for copy in out:
        copy.start()
    return out


def spectrum_kernel(
    mask_ref, pupil_ref, weight_ref, cell_ref, active_ref, cols_ref, rows_ref,
    part_ref, sent_ref,
    mask_in, pupil_in, weight_in, cell_in, active_in, cols, rows, sems, lined, paired,
):
    get_active, get_cell, get_pupil, get_weight, get_mask, get_cols, get_rows = copies(
        sems,
        (active_ref, active_in),
        (cell_ref, cell_in),
        (pupil_ref.at[pl.ds(0, 16)], pupil_in),
        (weight_ref, weight_in),
        (mask_ref.at[0], mask_in),
        (cols_ref, cols),
        (rows_ref.at[my_block()], rows),
    )
    get_active.wait()
    get_cell.wait()
    get_pupil.wait()
    get_weight.wait()
    active = active_in[lax.axis_index("src")]
    raw = pupil_in[...].astype(f32)[:8]
    raw = jnp.where(row_of(raw.shape) < active, raw, 0.0)
    for piece in range(16):
        lined[pl.ds(piece, 8, stride=16), :] = raw[:, piece * LANES : (piece + 1) * LANES]
    quarter = lane_of((8, LANES)) // K
    for pair in range(PAIRS):
        first, second = pair * 32, pair * 32 + 16
        quarters = [lined[pl.ds(start, 8), :] for start in (first, second, first + 8, second + 8)]
        for turn in range(4):
            moved = [
                value if number == turn else pltpu.roll(value, K * (number - turn) % LANES, 1)
                for number, value in enumerate(quarters)
            ]
            out = moved[3]
            for number in range(3):
                out = jnp.where(quarter == number, moved[number], out)
            paired[pl.ds(pair * K + turn, 8, stride=4), :] = out
    sent_ref[: PAIRS * K] = paired[...].astype(bf16)
    shape = (8, LANES)
    weights = jnp.broadcast_to(weight_in[...].astype(f32).reshape(1, -1)[:, :LANES], shape)
    column = jnp.sum(jnp.where(row_of(shape) == lane_of(shape), weights, 0.0), 1, keepdims=True)
    column = jnp.broadcast_to(column, shape)
    tail = [column]
    for pair in range(PAIRS):
        even = lane_of((1, LANES)) // K % 2 == 0
        tail.append(jnp.where(even, column[2 * pair : 2 * pair + 1], column[2 * pair + 1 : 2 * pair + 2]))
    tail.append(jnp.zeros((1, LANES), f32))
    place = lane_of((1, LANES))
    row_code, col_code = jnp.zeros((1, LANES), f32), jnp.zeros((1, LANES), f32)
    for slot in range(MOST):
        cell = cell_in[slot]
        row_code = jnp.where(place == slot, lax.div(cell, SG).astype(f32), row_code)
        col_code = jnp.where(place == slot, lax.rem(cell, SG).astype(f32), col_code)
    tail += [row_code, col_code, jnp.zeros((2, LANES), f32)]
    sent_ref[PAIRS * K :] = jnp.concatenate(tail, 0).astype(bf16)
    get_mask.wait()
    get_cols.wait()
    get_rows.wait()
    high, low = split(mask_in[...])
    both = dot(high, cols[...])
    part = both[:, :LANES] + both[:, LANES:] + dot(low, cols[:, :LANES])
    turned = swap(part) * signs(part.shape[0], 1.0, -1.0)
    high, low = split(jnp.concatenate([part, turned], 0))
    product = dot(rows[...], jnp.concatenate([high, low], 1))
    part_ref[...] = product[:W, :LANES] + product[:W, LANES:] + product[W:, :LANES]


def pack_kernel(part_ref, *refs):
    *other_refs, sent_ref, out_ref = refs
    part = part_ref[...]
    for ref in other_refs:
        part = part + ref[...]
    high, low = split(part)
    out_ref[:W] = high
    out_ref[W : 2 * W] = low
    out_ref[AT_PUPILS:] = sent_ref[...]


def owners_of(refs):
    src = lax.axis_index("src")
    if len(refs) > 1:
        return [(ref, jnp.bitwise_xor(src, step)) for step, ref in enumerate(refs)]
    return None


def over_owners(refs, body, carry):
    together = owners_of(refs)
    if together is not None:
        return body(carry, together)
    (ref,) = refs
    return lax.fori_loop(
        0, ref.shape[0], lambda owner, carry: body(carry, [(ref.at[owner], owner)]), carry
    )


def codes_of(refs, codes_v):
    def body(none, items):
        for ref, owner in items:
            tail = ref[pl.ds(AT_TAIL, 16), :].astype(f32)
            code = tail[TAIL_CELL : TAIL_CELL + 1] * 32.0 + tail[TAIL_CELL + 1 : TAIL_CELL + 2]
            codes_v[pl.ds(owner, 1), :] = code.astype(jnp.int32)
        return none

    over_owners(refs, body, 0)


def window_of(codes, owner, slot):
    code = codes[owner, slot]
    return lax.div(code, 32), lax.rem(code, 32)


def pair_parts(ref, pair):
    value = ref[pl.ds(AT_PUPILS + pair * K, K), :].astype(f32)
    other = swap(value)
    low = lane_of(value.shape) < M
    return jnp.where(low, value, other), jnp.where(low, other, value)


def slot_lanes(rows):
    return lane_of((rows, LANES)) // K % 2 == 0


def image_kernel(n_sent, *refs):
    sent_refs, refs = refs[:n_sent], refs[n_sent:]
    (
        target_ref, class_ref, thresholds_ref,
        lift_cols_ref, lift_rows_ref, fine_rows_ref, fine_cols_ref, fold_cols_ref, fold_rows_ref,
        intensity_ref, fold_ref, fields_ref,
        target, kinds, thresholds,
        lift_cols, lift_rows, fine_rows, fine_cols, fold_cols, fold_rows,
        sems, codes_v, codes, spectrum, intensity_out,
    ) = refs
    block = my_block()
    codes_of(sent_refs, codes_v)
    gets = copies(
        sems,
        (codes_v, codes),
        (lift_cols_ref, lift_cols),
        (lift_rows_ref, lift_rows),
        (class_ref, kinds),
        (thresholds_ref, thresholds),
        (fine_rows_ref.at[block], fine_rows),
        (fine_cols_ref, fine_cols),
        (target_ref.at[0], target),
        (fold_cols_ref, fold_cols),
        (fold_rows_ref.at[block], fold_rows),
    )

    def gather(total, items):
        for ref, owner in items:
            total = total + (ref[:W].astype(f32) + ref[W : 2 * W].astype(f32))
        return total

    spectrum[...] = over_owners(sent_refs, gather, jnp.zeros((W, LANES), f32))
    for get in gets[:3]:
        get.wait()
    even = slot_lanes(K)
    turn_low = signs(K, -1.0, 1.0)
    turn = signs(M, -1.0, 1.0)

    def forward(total, items):
        waves = []
        for ref, owner in items:
            for pair in range(PAIRS):
                real, imag = pair_parts(ref, pair)
                row, col = window_of(codes, owner, 2 * pair)
                left = pltpu.roll(spectrum[pl.ds(row, K), :], lax.rem(LANES - col, LANES), 1)
                row, col = window_of(codes, owner, 2 * pair + 1)
                right = pltpu.roll(spectrum[pl.ds(row, K), :], lax.rem(LANES + K - col, LANES), 1)
                window = jnp.where(even, left, right)
                waves.append((real * window + imag * (turn_low * swap(window))).astype(bf16))
        wave = jnp.concatenate(waves, 0)
        high, low = split(dot(jnp.concatenate([wave, wave], 1), lift_cols[...]))
        number = 0
        for ref, owner in items:
            weights = ref[pl.ds(AT_TAIL, 16), :].astype(f32)
            for pair in range(PAIRS):
                here = slice(number * K, (number + 1) * K)
                number += 1
                raw = dot(lift_rows[...], jnp.concatenate([high[here], high[here], low[here]], 0))
                for slot in range(2):
                    mine = raw[:, slot * LANES : (slot + 1) * LANES]
                    field = mine[:M] + turn * swap(mine[M:])
                    fields_ref[owner * MOST + 2 * pair + slot] = field
                    at = 2 * pair + slot
                    total = total + weights[at : at + 1] * (field * field)
        return total

    power = over_owners(sent_refs, forward, jnp.zeros((M, LANES), f32))
    for get in gets[3:]:
        get.wait()
    high, low = split(power + swap(power))
    half = dot(fine_rows[...], jnp.concatenate([high, high, low, low], 0))
    high, low = split(half)
    intensity = dot(jnp.concatenate([high, low], 1), fine_cols[...])
    intensity_out[...] = intensity
    put = pltpu.make_async_copy(intensity_out, intensity_ref.at[0], sems.at[len(gets)])
    put.start()
    kind = kinds[0]
    threshold = thresholds[0]
    for number in range(1, CLASSES):
        threshold = jnp.where(kind == number, thresholds[number], threshold)
    resist = 1.0 / (1.0 + jnp.exp(-STEEP * (intensity - threshold)))
    slope = (2.0 * STEEP * (resist - target[...]) * resist * (1.0 - resist)).astype(bf16)
    folded = dot(slope, fold_cols[...])
    high, low = split(folded + swap(folded))
    grid = dot(fold_rows[...], jnp.concatenate([high, high, low], 0))
    lane = lane_of((M // 2, LANES))
    fold_ref[: M // 2] = jnp.where(lane < M, grid[: M // 2], grid[M // 2 :])

    def weigh(none, items):
        for ref, owner in items:
            for slot in range(MOST):
                number = owner * MOST + slot
                field = fields_ref[number]
                total = jnp.sum(grid * (field * field), 0, keepdims=True)
                fold_ref[pl.ds(M // 2 + number, 1), :] = total
        return none

    over_owners(sent_refs, weigh, 0)
    put.wait()


def gradient_kernel(n_fold, n_sent, *refs):
    fold_refs, refs = refs[:n_fold], refs[n_fold:]
    sent_refs, refs = refs[:n_sent], refs[n_sent:]
    (
        fields_ref, drop_rows_ref, drop_cols_ref, grad_rows_ref, grad_cols_ref,
        mask_grad_ref,
        drop_rows, drop_cols, grad_rows, grad_cols, sems, codes_v, codes, sums, mask_grad_out,
    ) = refs
    codes_of(sent_refs, codes_v)
    gets = copies(
        sems,
        (drop_rows_ref, drop_rows),
        (codes_v, codes),
        (drop_cols_ref, drop_cols),
        (grad_rows_ref.at[my_block()], grad_rows),
        (grad_cols_ref, grad_cols),
    )
    packed = fold_refs[0][: M // 2]
    for ref in fold_refs[1:]:
        packed = packed + ref[: M // 2]
    other = swap(packed)
    low_half = lane_of(packed.shape) < M
    grid = jnp.concatenate(
        [jnp.where(low_half, packed, other), jnp.where(low_half, other, packed)], 0
    )
    for number in range(2):
        sums[number] = jnp.zeros((W, LANES), f32)
    turn = signs(K, 1.0, -1.0)
    even = slot_lanes(K)
    real_or_imag = lane_of((K, LANES)) % M < K
    for get in gets[:3]:
        get.wait()

    def backward(none, items):
        waves = []
        for ref, owner in items:
            for pair in range(PAIRS):
                fields = [grid * fields_ref[owner * MOST + 2 * pair + slot] for slot in range(2)]
                high, low = split(jnp.concatenate(fields, 1))
                raw = dot(drop_rows[...], jnp.concatenate([high, high, low], 0))
                wave = []
                for slot in range(2):
                    mine = raw[:, slot * LANES : (slot + 1) * LANES]
                    wave.append(mine[:K] + turn * swap(mine[K:]))
                waves.append(jnp.concatenate(wave, 1))
        high, low = split(jnp.concatenate(waves, 0))
        back = dot(jnp.concatenate([high, high, low], 1), drop_cols[...])
        number = 0
        for ref, owner in items:
            weights = ref[pl.ds(AT_TAIL, 16), :].astype(f32) * (2.0 / K)
            for pair in range(PAIRS):
                mine = back[number * K : (number + 1) * K]
                number += 1
                real, imag = pair_parts(ref, pair)
                product = real * mine + imag * (turn * swap(mine))
                product = weights[TAIL_PAIR + pair : TAIL_PAIR + pair + 1] * product
                for slot in range(2):
                    row, col = window_of(codes, owner, 2 * pair + slot)
                    keep = even if slot == 0 else jnp.logical_not(even)
                    shift = lax.rem(col + LANES - slot * K, LANES)
                    moved = pltpu.roll(jnp.where(keep, product, 0.0), shift, 1)
                    sums[slot, pl.ds(row, K), :] += moved
        return none

    over_owners(sent_refs, backward, 0)
    for get in gets[3:]:
        get.wait()
    grad = sums[0] + sums[1]
    turn = signs(W, 1.0, -1.0)
    high, low = split(jnp.concatenate([grad * turn, -swap(grad)], 0))
    half = dot(grad_rows[...], jnp.concatenate([high, high, low], 0))
    high, low = split(half)
    mask_grad_out[...] = dot(jnp.concatenate([high, high], 1), grad_cols[...]) + dot(
        low, grad_cols[:LANES]
    )
    put = pltpu.make_async_copy(mask_grad_out, mask_grad_ref.at[0], sems.at[len(gets)])
    put.start()
    put.wait()


VMEM = pl.BlockSpec(memory_space=pltpu.VMEM)
HBM = pl.BlockSpec(memory_space=pltpu.HBM)
PARAMS = pltpu.CompilerParams(vmem_limit_bytes=48 * 1024 * 1024)


def others(value, axis):
    size = lax.axis_size(axis)
    return [
        lax.ppermute(value, axis, [(i, i ^ step) for i in range(size)]) for step in range(1, size)
    ]


def like(value):
    return pltpu.VMEM(value.shape, value.dtype)


def shards(
    mask, target, tile_class, thresholds, source_pupil, source_weight, source_cell, active_count
):
    span, period = mask.shape[1:]
    slots = source_pupil.shape[0]
    src_count = lax.axis_size("src")
    few = src_count in (2, 4)
    table = {name: jnp.asarray(value) for name, value in tables(period, span).items()}
    src = lax.axis_index("src")
    sems = pltpu.SemaphoreType.DMA
    smem = pltpu.SMEM

    part, sent = pl.pallas_call(
        spectrum_kernel,
        in_specs=[HBM] * 7,
        out_specs=[VMEM, VMEM],
        out_shape=[
            jax.ShapeDtypeStruct((W, LANES), f32),
            jax.ShapeDtypeStruct((ROWS - AT_PUPILS, LANES), bf16),
        ],
        scratch_shapes=[
            like(mask[0]),
            like(source_pupil[:16]),
            like(source_weight),
            smem(source_cell.shape, jnp.int32),
            smem(active_count.shape, jnp.int32),
            like(table["spec_cols"]),
            like(table["spec_rows"][0]),
            sems((7,)),
            pltpu.VMEM((LANES, LANES), f32),
            pltpu.VMEM((PAIRS * K, LANES), f32),
        ],
        compiler_params=PARAMS,
        name="spectrum",
    )(
        mask, source_pupil, source_weight, source_cell, active_count,
        table["spec_cols"], table["spec_rows"],
    )
    from_pix = others(part, "pix")
    sent = pl.pallas_call(
        pack_kernel,
        in_specs=[VMEM] * (2 + len(from_pix)),
        out_specs=VMEM,
        out_shape=jax.ShapeDtypeStruct((ROWS, LANES), bf16),
        compiler_params=PARAMS,
        name="pack",
    )(part, *from_pix, sent)
    if few:
        parcels = [sent] + others(sent, "src")
    else:
        parcels = [lax.all_gather(sent, "src")]

    numbers = src_count * MOST
    owners_up = -(-src_count // 8) * 8
    fold_out = M // 2 + -(-numbers // 8) * 8
    codes = [pltpu.VMEM((owners_up, LANES), jnp.int32), smem((owners_up, LANES), jnp.int32)]
    intensity, folded, fields = pl.pallas_call(
        functools.partial(image_kernel, len(parcels)),
        in_specs=[VMEM] * len(parcels) + [HBM] * 9,
        out_specs=[HBM, VMEM, VMEM],
        out_shape=[
            jax.ShapeDtypeStruct((1, span, period), f32),
            jax.ShapeDtypeStruct((fold_out, LANES), f32),
            jax.ShapeDtypeStruct((numbers, M, LANES), f32),
        ],
        scratch_shapes=[
            like(target[0]),
            smem(tile_class.shape, jnp.int32),
            smem(thresholds.shape, f32),
            like(table["lift_cols"]),
            like(table["lift_rows"]),
            like(table["fine_rows"][0]),
            like(table["fine_cols"]),
            like(table["fold_cols"]),
            like(table["fold_rows"][0]),
            sems((11,)),
            *codes,
            pltpu.VMEM((W, LANES), f32),
            like(target[0]),
        ],
        compiler_params=PARAMS,
        name="image",
    )(
        *parcels, target, tile_class, thresholds,
        table["lift_cols"], table["lift_rows"], table["fine_rows"], table["fine_cols"],
        table["fold_cols"], table["fold_rows"],
    )

    for other in others(folded, "pix"):
        folded = folded + other
    folds = [folded] + others(folded, "src") if few else [lax.psum(folded, "src")]
    first = M // 2 + src * MOST
    rows = sum(lax.dynamic_slice_in_dim(fold, first, MOST, 0) for fold in folds)
    for other in others(rows, "tile"):
        rows = rows + other
    mask_grad = pl.pallas_call(
        functools.partial(gradient_kernel, len(folds), len(parcels)),
        in_specs=[VMEM] * (len(folds) + len(parcels) + 1) + [HBM] * 4,
        out_specs=HBM,
        out_shape=jax.ShapeDtypeStruct((1, span, period), f32),
        scratch_shapes=[
            like(table["drop_rows"]),
            like(table["drop_cols"]),
            like(table["grad_rows"][0]),
            like(table["grad_cols"]),
            sems((6,)),
            *codes,
            pltpu.VMEM((2, W, LANES), f32),
            like(mask[0]),
        ],
        compiler_params=PARAMS,
        name="gradient",
    )(
        *folds, *parcels, fields,
        table["drop_rows"], table["drop_cols"], table["grad_rows"], table["grad_cols"],
    )
    sums = jnp.sum(rows, 1) * (1.0 / (period * K))
    source_grad = jnp.zeros((slots,), f32).at[:MOST].set(sums)
    return intensity, mask_grad, source_grad


def solution(mesh):
    in_specs = (
        P(("groups", "tile"), ("src", "pix"), None),
        P(("groups", "tile"), ("src", "pix"), None),
        P(("groups", "tile")),
        P(),
        P("src", None),
        P("src"),
        P("src"),
        P(),
    )
    out_specs = (
        P(("groups", "tile"), ("src", "pix"), None),
        P(("groups", "tile"), ("src", "pix"), None),
        P(("groups", "src")),
    )
    return jax.shard_map(shards, mesh=mesh, in_specs=in_specs, out_specs=out_specs, check_vma=False)
```

time: 52.2 us -> 40.6 us (0.78)
  starting transfers between devices: 18.9 us -> 12.2 us
  Pallas kernels: 10.3 us -> 7.54 us
  local copies, waits for them, and re-layouts: 10.3 us -> 8.47 us
  other arithmetic: 0.86 us -> 0.14 us
    ppermute x12 -> x9, starting transfers between devices: 18.9 us -> 12.2 us  [others(): lax.ppermute(value, axis, [(i, i ^ step) for i in range(size)])]
    pallas_call x3 -> x4, Pallas kernels: 10.3 us -> 7.54 us  [the longest x1 3.16 us: shards(): pl.pallas_call(functools.partial(image_kernel, len(parcels)), in_specs=[V...]
    unnamed x40 -> x38, local copies, waits for them, and re-layouts: 9.16 us -> 7.95 us
    select_n x1 -> x0, other arithmetic: 0.65 us -> none  [shards(): source_grad = jnp.pad(jnp.where(live, sums, 0.0), (0, slots - MOST))]
    dynamic_slice x1 -> x0, local copies, waits for them, and re-layouts: 0.58 us -> none  [shards(): live = jnp.arange(MOST, dtype=jnp.int32) < active_count[src]]
    ppermute x12 -> x9, waiting for transfers between devices: 10 us -> 10.5 us  [others(): lax.ppermute(value, axis, [(i, i ^ step) for i in range(size)])]
  transfers between devices with their start and end apart: 12 -> 9, of which waited for: 6 -> 6; matrix products, arithmetic and copies ran while one was open for 1% -> 0% of each run, Pallas kernels for 9% -> 8%
where the time goes in v2:
time: 40.6 us; the launch traced here: 40.2 us
  starting transfers between devices  12.2 us (30%)
  waiting for transfers between devices  10.5 us (26%)
  local copies, waits for them, and re-layouts  8.47 us (21%)
  Pallas kernels  7.54 us (19%)
  between operations  1.47 us (4%)
    ppermute x9, starting transfers between devices, others(): lax.ppermute(value, axis, [(i, i ^ step) for i in range(size)])  12.2 us
    ppermute x9, waiting for transfers between devices, others(): lax.ppermute(value, axis, [(i, i ^ step) for i in range(size)])  10.5 us
    unnamed x38, local copies, waits for them, and re-layouts  7.95 us
    pallas_call x1, Pallas kernels, shards(): pl.pallas_call(functools.partial(image_kernel, len(parcels)), in_specs=[V...  3.16 us
    pallas_call x1, Pallas kernels, shards(): pl.pallas_call(functools.partial(gradient_kernel, len(folds), len(parcels...  3.08 us
    pallas_call x1, Pallas kernels, shards(): pl.pallas_call(spectrum_kernel, in_specs=[HBM] * 7, out_specs=[VMEM, VMEM...  1.29 us
  transfers between devices with their start and end apart: 9, of which 6 were waited for; matrix products, arithmetic and copies ran while one was open for 0% of the time, Pallas kernels for 8%

profile of v2, /device:TPU:0, one launch (start us, length us, event | category | flops | bytes accessed | tf_op | source)
XLA Modules:
  0.0 40.2 jit_solution(3074702648087314149)
XLA Ops:
  0.6 0.0 copy-start.3
  0.6 0.0 copy-start.4
  0.7 0.0 copy-start.1
  0.7 0.0 copy-start.5
  0.7 1.1 %copy-done.5 = f32[1,128,1024]{2,1,0:T(8,128)S(1)} copy-done((f32[1,128,1024]{2,1,0:T(8,128)S(1)}, f32[1,128,1024]{2,1,0:T(8,128)}, u32[]{:S(2)}) %copy-start.5) | copy-done | bytes 524312
  1.8 1.0 %copy-done.6 = bf16[128,2048]{1,0:T(8,128)(2,1)S(1)} copy-done((bf16[128,2048]{1,0:T(8,128)(2,1)S(1)}, bf16[128,2048]{1,0:T(8,128)(2,1)}, u32[]{:S(2)}) %copy-start.6) | copy-done | bytes 524312
  2.9 1.0 %copy-done.7 = bf16[1024,256]{1,0:T(8,128)(2,1)S(1)} copy-done((bf16[1024,256]{1,0:T(8,128)(2,1)S(1)}, bf16[1024,256]{1,0:T(8,128)(2,1)}, u32[]{:S(2)}) %copy-start.7) | copy-done | bytes 524312
  3.9 1.0 %copy-done.9 = bf16[8,96,256]{2,1,0:T(8,128)(2,1)S(1)} copy-done((bf16[8,96,256]{2,1,0:T(8,128)(2,1)S(1)}, bf16[8,96,256]{2,1,0:T(8,128)(2,1)}, u32[]{:S(2)}) %copy-start.9) | copy-done | bytes 393240
  4.9 0.7 %copy-done.16 = bf16[128]{0:T(256)(128)(2,1)S(1)} copy-done((bf16[128]{0:T(256)(128)(2,1)S(1)}, bf16[128]{0:T(256)(128)(2,1)}, u32[]{:S(2)}) %copy-start.16) | copy-done | bytes 280
  5.6 0.7 %copy-done.17 = s32[128]{0:T(128)S(1)} copy-done((s32[128]{0:T(128)S(1)}, s32[128]{0:T(128)}, u32[]{:S(2)}) %copy-start.17) | copy-done | bytes 536
  6.2 0.7 %copy-done.18 = s32[4]{0:T(128)S(1)} copy-done((s32[4]{0:T(128)S(1)}, s32[4]{0:T(128)}, u32[]{:S(2)}) %copy-start.18) | copy-done | bytes 40
  6.9 1.3 %spectrum.1 = (f32[48,128]{1,0:T(8,128)S(1)}, bf16[112,128]{1,0:T(8,128)(2,1)S(1)}) custom-call(f32[1,128,1024]{2,1,0:T(8,128)S(1)} %copy-done.5, bf16[128,2048]{1,0:T(8,128)(2,1)S(1)} %copy-done.6, bf16[128]{0:T(256)(128)(2,1)S(1)} %copy-done.16, s32[128]{0:T(128)S(1)} %copy-done.17, s32[4]{0:T(128)S(1)} %copy-done.18, bf16[1024,256]{1,0:T(8,128)(2,1)S(1)} %copy-done.7, ...), custom_call_target="tpu_custom_call" | custom-call | tf_op jit(solution)/shard_map/spectrum/pallas_call | solution.py:492
  8.2 0.0 copy-start.12
  8.2 0.5 %collective-permute-start = (f32[48,128]{1,0:T(8,128)S(1)}, f32[48,128]{1,0:T(8,128)S(1)}, u32[]{:S(2)}, u32[]{:S(2)}) collective-permute-start(f32[48,128]{1,0:T(8,128)S(1)} %get-tuple-element.20.part_ref), channel_id=1, source_target_pairs={{0,1},{1,0},{2,3},{3,2},{4,5},{5,4},{6,7},{7,6},{8,9},{9,8},{10,11... | collective-permute-start | bytes 73736 | tf_op jit(solution)/shard_map/ppermute | solution.py:472
  8.7 0.8 %collective-permute-done.refs_0_ = f32[48,128]{1,0:T(8,128)S(1)} collective-permute-done((f32[48,128]{1,0:T(8,128)S(1)}, f32[48,128]{1,0:T(8,128)S(1)}, u32[]{:S(2)}, u32[]{:S(2)}) %collective-permute-start) | collective-permute-done | bytes 24608 | tf_op jit(solution)/shard_map/ppermute | solution.py:472
  9.6 0.0 copy-start.15
  9.6 3.0 %collective-permute-start.1 = (bf16[208,128]{1,0:T(8,128)(2,1)S(1)}, bf16[208,128]{1,0:T(8,128)(2,1)S(1)}, u32[]{:S(2)}, u32[]{:S(2)}) collective-permute-start(bf16[208,128]{1,0:T(8,128)(2,1)S(1)} %pack.1.refs_0_.refs_4_), channel_id=1, source_target_pairs={{0,4},{4,0},{8,12},{12,8},{1,5},{5,1},{9,13},{13,9},{2,6},{6,2},{1... | collective-permute-start | bytes 159752 | tf_op jit(solution)/shard_map/ppermute | solution.py:472
  12.6 2.6 %collective-permute-start.2 = (bf16[208,128]{1,0:T(8,128)(2,1)S(1)}, bf16[208,128]{1,0:T(8,128)(2,1)S(1)}, u32[]{:S(2)}, u32[]{:S(2)}) collective-permute-start(bf16[208,128]{1,0:T(8,128)(2,1)S(1)} %pack.1.refs_0_.refs_4_), channel_id=1, source_target_pairs={{0,8},{4,12},{8,0},{12,4},{1,9},{5,13},{9,1},{13,5},{2,10},{6,14},... | collective-permute-start | bytes 159752 | tf_op jit(solution)/shard_map/ppermute | solution.py:472
  15.1 0.0 collective-permute-start.3
  15.8 0.0 copy-start
  15.8 0.0 copy-start.2
  15.8 0.0 collective-permute-done.1.refs_1_.refs_5_
  15.8 2.9 %collective-permute-done.2.refs_2_.refs_6_ = bf16[208,128]{1,0:T(8,128)(2,1)S(1)} collective-permute-done((bf16[208,128]{1,0:T(8,128)(2,1)S(1)}, bf16[208,128]{1,0:T(8,128)(2,1)S(1)}, u32[]{:S(2)}, u32[]{:S(2)}) %collective-permute-start.2) | collective-permute-done | bytes 53280 | tf_op jit(solution)/shard_map/ppermute | solution.py:472
  18.8 2.3 %collective-permute-done.3.refs_3_.refs_7_ = bf16[208,128]{1,0:T(8,128)(2,1)S(1)} collective-permute-done((bf16[208,128]{1,0:T(8,128)(2,1)S(1)}, bf16[208,128]{1,0:T(8,128)(2,1)S(1)}, u32[]{:S(2)}, u32[]{:S(2)}) %collective-permute-start.3) | collective-permute-done | bytes 53280 | tf_op jit(solution)/shard_map/ppermute | solution.py:472
  21.1 0.0 copy-done.3
  21.1 0.0 copy-done.4
  21.1 0.0 copy-done.1
  21.1 0.0 copy-done.8
  21.1 0.0 copy-done.12
  21.1 0.0 copy-start.10
  21.1 0.9 %copy-done.10 = bf16[1024,128]{1,0:T(8,128)(2,1)S(1)} copy-done((bf16[1024,128]{1,0:T(8,128)(2,1)S(1)}, bf16[1024,128]{1,0:T(8,128)(2,1)}, u32[]{:S(2)}) %copy-start.10) | copy-done | bytes 262168
  22.1 0.8 %copy-done.14 = bf16[128,96]{1,0:T(8,128)(2,1)S(1)} copy-done((bf16[128,96]{1,0:T(8,128)(2,1)S(1)}, bf16[128,96]{1,0:T(8,128)(2,1)}, u32[]{:S(2)}) %copy-start.14) | copy-done | bytes 24600
  22.8 3.2 %image.1 = (f32[1,128,1024]{2,1,0:T(8,128)}, f32[56,128]{1,0:T(8,128)S(1)}, f32[24,64,128]{2,1,0:T(8,128)S(1)}) custom-call(bf16[208,128]{1,0:T(8,128)(2,1)S(1)} %pack.1.refs_0_.refs_4_, bf16[208,128]{1,0:T(8,128)(2,1)S(1)} %collective-permute-done.1.refs_1_.refs_5_, bf16[208,128]{1,0:T(8,128)(2,1)S(1)} %collective-permute-done.2.refs_2_.refs_6_, ...), custom_call_target="tpu_custom_call" | custom-call | tf_op jit(solution)/shard_map/image/pallas_call | solution.py:536
  26.0 0.1 collective-permute-start.4
  26.1 1.2 %collective-permute-done.4 = f32[56,128]{1,0:T(8,128)S(1)} collective-permute-done((f32[56,128]{1,0:T(8,128)S(1)}, f32[56,128]{1,0:T(8,128)S(1)}, u32[]{:S(2)}, u32[]{:S(2)}) %collective-permute-start.4) | collective-permute-done | bytes 28704 | tf_op jit(solution)/shard_map/ppermute | solution.py:472
  27.3 0.1 collective-permute-start.5
  27.4 1.9 %collective-permute-start.6 = (f32[56,128]{1,0:T(8,128)S(1)}, f32[56,128]{1,0:T(8,128)S(1)}, u32[]{:S(2)}, u32[]{:S(2)}) collective-permute-start(f32[56,128]{1,0:T(8,128)S(1)} %add.27.refs_0_), channel_id=1, source_target_pairs={{0,8},{4,12},{8,0},{12,4},{1,9},{5,13},{9,1},{13,5},{2,10},{6,14},... | collective-permute-start | bytes 86024 | tf_op jit(solution)/shard_map/ppermute | solution.py:472
  29.2 2.5 %collective-permute-start.7 = (f32[56,128]{1,0:T(8,128)S(1)}, f32[56,128]{1,0:T(8,128)S(1)}, u32[]{:S(2)}, u32[]{:S(2)}) collective-permute-start(f32[56,128]{1,0:T(8,128)S(1)} %add.27.refs_0_), channel_id=1, source_target_pairs={{0,12},{4,8},{8,4},{12,0},{1,13},{5,9},{9,5},{13,1},{2,14},{6,10},... | collective-permute-start | bytes 86024 | tf_op jit(solution)/shard_map/ppermute | solution.py:472
  31.7 0.0 collective-permute-done.5.refs_1_
  31.7 1.0 %collective-permute-done.6.refs_2_ = f32[56,128]{1,0:T(8,128)S(1)} collective-permute-done((f32[56,128]{1,0:T(8,128)S(1)}, f32[56,128]{1,0:T(8,128)S(1)}, u32[]{:S(2)}, u32[]{:S(2)}) %collective-permute-start.6) | collective-permute-done | bytes 28704 | tf_op jit(solution)/shard_map/ppermute | solution.py:472
  32.7 2.2 %collective-permute-done.7.refs_3_ = f32[56,128]{1,0:T(8,128)S(1)} collective-permute-done((f32[56,128]{1,0:T(8,128)S(1)}, f32[56,128]{1,0:T(8,128)S(1)}, u32[]{:S(2)}, u32[]{:S(2)}) %collective-permute-start.7) | collective-permute-done | bytes 28704 | tf_op jit(solution)/shard_map/ppermute | solution.py:472
  34.9 1.6 %collective-permute-start.8 = (f32[6,128]{1,0:T(8,128)S(1)}, f32[6,128]{1,0:T(8,128)S(1)}, u32[]{:S(2)}, u32[]{:S(2)}) collective-permute-start(f32[6,128]{1,0:T(8,128)S(1)} %dynamic-slice_add_fusion), channel_id=1, source_target_pairs={{0,2},{2,0},{1,3},{3,1},{4,6},{6,4},{5,7},{7,5},{8,10},{10,8},{9,1... | collective-permute-start | bytes 9224 | tf_op jit(solution)/shard_map/ppermute | solution.py:472
  36.5 0.0 copy-done.2
  36.5 0.0 copy-done.13
  36.5 3.1 %gradient.1 = f32[1,128,1024]{2,1,0:T(8,128)} custom-call(f32[56,128]{1,0:T(8,128)S(1)} %add.27.refs_0_, f32[56,128]{1,0:T(8,128)S(1)} %collective-permute-done.5.refs_1_, f32[56,128]{1,0:T(8,128)S(1)} %collective-permute-done.6.refs_2_, f32[56,128]{1,0:T(8,128)S(1)} %collective-permute-done.7.refs_3_, bf16[208,128]{1,0:T(8,128)(2,1)S(1)} %pack.1.refs_0_.refs_4_, ...), custom_call_target="tpu_custom_call" | custom-call | tf_op jit(solution)/shard_map/gradient/pallas_call | solution.py:575
  39.6 0.0 collective-permute-done.8
  39.6 0.1 add_reduce_fusion
  39.7 0.5 %scatter.4 = f32[128]{0:T(128)} pad(f32[6]{0:T(128)S(1)} %broadcast_multiply_fusion, f32[]{:T(128)} %constant.64.clone.1), padding=0_122 | pad | bytes 540 | tf_op jit(solution)/shard_map/scatter | solution.py:597
  (17 shorter events, 0.1 us)
Async XLA Ops:
  0.6 20.5 %copy-start.3 = (bf16[8,128,256]{2,1,0:T(8,128)(2,1)S(1)}, bf16[8,128,256]{2,1,0:T(8,128)(2,1)}, u32[]{:S(2)}) copy-start(bf16[8,128,256]{2,1,0:T(8,128)(2,1)} %constant.72.clone.refs_9_) | copy-start | bytes 1572868
  0.6 20.4 %copy-start.4 = (bf16[256,1024]{1,0:T(8,128)(2,1)S(1)}, bf16[256,1024]{1,0:T(8,128)(2,1)}, u32[]{:S(2)}) copy-start(bf16[256,1024]{1,0:T(8,128)(2,1)} %constant.70.clone.refs_10_) | copy-start | bytes 1572868
  0.7 20.4 %copy-start.1 = (f32[1,128,1024]{2,1,0:T(8,128)S(1)}, f32[1,128,1024]{2,1,0:T(8,128)}, u32[]{:S(2)}) copy-start(f32[1,128,1024]{2,1,0:T(8,128)} %refs_4_.1) | copy-start | bytes 1572868
  0.7 1.2 %copy-start.5 = (f32[1,128,1024]{2,1,0:T(8,128)S(1)}, f32[1,128,1024]{2,1,0:T(8,128)}, u32[]{:S(2)}) copy-start(f32[1,128,1024]{2,1,0:T(8,128)} %mask_ref.1) | copy-start | bytes 1572868
  1.8 1.0 %copy-start.6 = (bf16[128,2048]{1,0:T(8,128)(2,1)S(1)}, bf16[128,2048]{1,0:T(8,128)(2,1)}, u32[]{:S(2)}) copy-start(bf16[128,2048]{1,0:T(8,128)(2,1)} %pupil_ref.1) | copy-start | bytes 1572868
  2.9 1.0 %copy-start.7 = (bf16[1024,256]{1,0:T(8,128)(2,1)S(1)}, bf16[1024,256]{1,0:T(8,128)(2,1)}, u32[]{:S(2)}) copy-start(bf16[1024,256]{1,0:T(8,128)(2,1)} %constant.66.clone.cols_ref) | copy-start | bytes 1572868
  3.9 1.0 %copy-start.9 = (bf16[8,96,256]{2,1,0:T(8,128)(2,1)S(1)}, bf16[8,96,256]{2,1,0:T(8,128)(2,1)}, u32[]{:S(2)}) copy-start(bf16[8,96,256]{2,1,0:T(8,128)(2,1)} %constant.67.clone.rows_ref) | copy-start | bytes 1179652
  4.9 0.7 %copy-start.16 = (bf16[128]{0:T(256)(128)(2,1)S(1)}, bf16[128]{0:T(256)(128)(2,1)}, u32[]{:S(2)}) copy-start(bf16[128]{0:T(256)(128)(2,1)} %weight_ref.1) | copy-start | bytes 772
  5.6 0.7 %copy-start.17 = (s32[128]{0:T(128)S(1)}, s32[128]{0:T(128)}, u32[]{:S(2)}) copy-start(s32[128]{0:T(128)} %cell_ref.1) | copy-start | bytes 1540
  6.2 0.7 %copy-start.18 = (s32[4]{0:T(128)S(1)}, s32[4]{0:T(128)}, u32[]{:S(2)}) copy-start(s32[4]{0:T(128)} %active_ref.1) | copy-start | bytes 52
  6.9 14.2 %copy-start.8 = (bf16[8,64,384]{2,1,0:T(8,128)(2,1)S(1)}, bf16[8,64,384]{2,1,0:T(8,128)(2,1)}, u32[]{:S(2)}) copy-start(bf16[8,64,384]{2,1,0:T(8,128)(2,1)} %constant.73.clone.refs_12_) | copy-start | bytes 1179652
  8.2 12.9 %copy-start.12 = (bf16[256,256]{1,0:T(8,128)(2,1)S(1)}, bf16[256,256]{1,0:T(8,128)(2,1)}, u32[]{:S(2)}) copy-start(bf16[256,256]{1,0:T(8,128)(2,1)} %constant.68.clone.refs_7_) | copy-start | bytes 393220
  8.2 1.4 %collective-permute-start = (f32[48,128]{1,0:T(8,128)S(1)}, f32[48,128]{1,0:T(8,128)S(1)}, u32[]{:S(2)}, u32[]{:S(2)}) collective-permute-start(f32[48,128]{1,0:T(8,128)S(1)} %get-tuple-element.20.part_ref), channel_id=1, source_target_pairs={{0,1},{1,0},{2,3},{3,2},{4,5},{5,4},{6,7},{7,6},{8,9},{9,8},{10,11... | collective-permute-start | bytes 73736 | tf_op jit(solution)/shard_map/ppermute | solution.py:472
  9.6 11.6 %copy-start.15 = (f32[4]{0:T(128)S(1)}, f32[4]{0:T(128)}, u32[]{:S(2)}) copy-start(f32[4]{0:T(128)} %refs_6_.1) | copy-start | bytes 52
  9.6 6.3 %collective-permute-start.1 = (bf16[208,128]{1,0:T(8,128)(2,1)S(1)}, bf16[208,128]{1,0:T(8,128)(2,1)S(1)}, u32[]{:S(2)}, u32[]{:S(2)}) collective-permute-start(bf16[208,128]{1,0:T(8,128)(2,1)S(1)} %pack.1.refs_0_.refs_4_), channel_id=1, source_target_pairs={{0,4},{4,0},{8,12},{12,8},{1,5},{5,1},{9,13},{13,9},{2,6},{6,2},{1... | collective-permute-start | bytes 159752 | tf_op jit(solution)/shard_map/ppermute | solution.py:472
  12.6 6.2 %collective-permute-start.2 = (bf16[208,128]{1,0:T(8,128)(2,1)S(1)}, bf16[208,128]{1,0:T(8,128)(2,1)S(1)}, u32[]{:S(2)}, u32[]{:S(2)}) collective-permute-start(bf16[208,128]{1,0:T(8,128)(2,1)S(1)} %pack.1.refs_0_.refs_4_), channel_id=1, source_target_pairs={{0,8},{4,12},{8,0},{12,4},{1,9},{5,13},{9,1},{13,5},{2,10},{6,14},... | collective-permute-start | bytes 159752 | tf_op jit(solution)/shard_map/ppermute | solution.py:472
  15.1 5.9 %collective-permute-start.3 = (bf16[208,128]{1,0:T(8,128)(2,1)S(1)}, bf16[208,128]{1,0:T(8,128)(2,1)S(1)}, u32[]{:S(2)}, u32[]{:S(2)}) collective-permute-start(bf16[208,128]{1,0:T(8,128)(2,1)S(1)} %pack.1.refs_0_.refs_4_), channel_id=1, source_target_pairs={{0,12},{4,8},{8,4},{12,0},{1,13},{5,9},{9,5},{13,1},{2,14},{6,10},... | collective-permute-start | bytes 159752 | tf_op jit(solution)/shard_map/ppermute | solution.py:472
  15.8 20.7 %copy-start = (bf16[8,128,288]{2,1,0:T(8,128)(2,1)S(1)}, bf16[8,128,288]{2,1,0:T(8,128)(2,1)}, u32[]{:S(2)}) copy-start(bf16[8,128,288]{2,1,0:T(8,128)(2,1)} %constant.76.clone.refs_11_) | copy-start | bytes 1769476
  15.8 20.7 %copy-start.2 = (bf16[256,1024]{1,0:T(8,128)(2,1)S(1)}, bf16[256,1024]{1,0:T(8,128)(2,1)}, u32[]{:S(2)}) copy-start(bf16[256,1024]{1,0:T(8,128)(2,1)} %constant.77.clone.refs_12_) | copy-start | bytes 1572868
  21.1 1.0 %copy-start.10 = (bf16[1024,128]{1,0:T(8,128)(2,1)S(1)}, bf16[1024,128]{1,0:T(8,128)(2,1)}, u32[]{:S(2)}) copy-start(bf16[1024,128]{1,0:T(8,128)(2,1)} %constant.71.clone.refs_11_) | copy-start | bytes 786436
  22.1 0.8 %copy-start.14 = (bf16[128,96]{1,0:T(8,128)(2,1)S(1)}, bf16[128,96]{1,0:T(8,128)(2,1)}, u32[]{:S(2)}) copy-start(bf16[128,96]{1,0:T(8,128)(2,1)} %constant.69.clone.refs_8_) | copy-start | bytes 73732
  22.8 13.7 %copy-start.11 = (bf16[768,128]{1,0:T(8,128)(2,1)S(1)}, bf16[768,128]{1,0:T(8,128)(2,1)}, u32[]{:S(2)}) copy-start(bf16[768,128]{1,0:T(8,128)(2,1)} %constant.75.clone.refs_10_) | copy-start | bytes 589828
  26.0 1.3 %collective-permute-start.4 = (f32[56,128]{1,0:T(8,128)S(1)}, f32[56,128]{1,0:T(8,128)S(1)}, u32[]{:S(2)}, u32[]{:S(2)}) collective-permute-start(f32[56,128]{1,0:T(8,128)S(1)} %get-tuple-element.23), channel_id=1, source_target_pairs={{0,1},{1,0},{2,3},{3,2},{4,5},{5,4},{6,7},{7,6},{8,9},{9,8},{10,11... | collective-permute-start | bytes 86024 | tf_op jit(solution)/shard_map/ppermute | solution.py:472
  27.3 9.2 %copy-start.13 = (bf16[64,192]{1,0:T(8,128)(2,1)S(1)}, bf16[64,192]{1,0:T(8,128)(2,1)}, u32[]{:S(2)}) copy-start(bf16[64,192]{1,0:T(8,128)(2,1)} %constant.74.clone.refs_9_) | copy-start | bytes 73732
  27.3 4.5 %collective-permute-start.5 = (f32[56,128]{1,0:T(8,128)S(1)}, f32[56,128]{1,0:T(8,128)S(1)}, u32[]{:S(2)}, u32[]{:S(2)}) collective-permute-start(f32[56,128]{1,0:T(8,128)S(1)} %add.27.refs_0_), channel_id=1, source_target_pairs={{0,4},{4,0},{8,12},{12,8},{1,5},{5,1},{9,13},{13,9},{2,6},{6,2},{1... | collective-permute-start | bytes 86024 | tf_op jit(solution)/shard_map/ppermute | solution.py:472
  27.4 5.4 %collective-permute-start.6 = (f32[56,128]{1,0:T(8,128)S(1)}, f32[56,128]{1,0:T(8,128)S(1)}, u32[]{:S(2)}, u32[]{:S(2)}) collective-permute-start(f32[56,128]{1,0:T(8,128)S(1)} %add.27.refs_0_), channel_id=1, source_target_pairs={{0,8},{4,12},{8,0},{12,4},{1,9},{5,13},{9,1},{13,5},{2,10},{6,14},... | collective-permute-start | bytes 86024 | tf_op jit(solution)/shard_map/ppermute | solution.py:472
  29.2 5.7 %collective-permute-start.7 = (f32[56,128]{1,0:T(8,128)S(1)}, f32[56,128]{1,0:T(8,128)S(1)}, u32[]{:S(2)}, u32[]{:S(2)}) collective-permute-start(f32[56,128]{1,0:T(8,128)S(1)} %add.27.refs_0_), channel_id=1, source_target_pairs={{0,12},{4,8},{8,4},{12,0},{1,13},{5,9},{9,5},{13,1},{2,14},{6,10},... | collective-permute-start | bytes 86024 | tf_op jit(solution)/shard_map/ppermute | solution.py:472
  34.9 4.7 %collective-permute-start.8 = (f32[6,128]{1,0:T(8,128)S(1)}, f32[6,128]{1,0:T(8,128)S(1)}, u32[]{:S(2)}, u32[]{:S(2)}) collective-permute-start(f32[6,128]{1,0:T(8,128)S(1)} %dynamic-slice_add_fusion), channel_id=1, source_target_pairs={{0,2},{2,0},{1,3},{3,1},{4,6},{6,4},{5,7},{7,5},{8,10},{10,8},{9,1... | collective-permute-start | bytes 9224 | tf_op jit(solution)/shard_map/ppermute | solution.py:472

commit v3 on v2

--- a/solution.py
+++ b/solution.py
@@ -103,20 +103,52 @@
     padded = [np.pad(part, ((0, M - W), (0, 0))) for part in (wide_cos, wide_sin)]
     high, low = split_np(np.concatenate(padded, 0))
     grad_cols = np.concatenate([high, low], 0)
-    return dict(
-        spec_cols=spec_cols,
-        spec_rows=spec_rows,
-        lift_cols=lift_cols,
-        lift_rows=lift_rows,
-        fine_cols=fine_cols,
-        fold_cols=fold_cols,
-        fine_rows=fine_rows,
-        fold_rows=fold_rows,
-        drop_rows=drop_rows,
-        drop_cols=drop_cols,
-        grad_rows=grad_rows,
-        grad_cols=grad_cols,
-    )
+    chapters = [
+        dict(lift_cols=lift_cols, lift_rows=lift_rows),
+        dict(fine_cols=fine_cols, fold_cols=fold_cols),
+        dict(drop_rows=drop_rows, drop_cols=drop_cols),
+        dict(grad_cols=grad_cols),
+    ]
+    for block in range(blocks):
+        chapters.append(dict(fine_rows=fine_rows[block], fold_rows=fold_rows[block]))
+    for block in range(blocks):
+        chapters.append(dict(grad_rows=grad_rows[block]))
+    pages, starts, places, at = [], [], {}, 0
+    for chapter in chapters:
+        starts.append(at)
+        for name, value in chapter.items():
+            places[name] = (at - starts[-1], value.shape)
+            for lane in range(0, value.shape[1], LANES):
+                page = value[:, lane : lane + LANES]
+                pages.append(np.pad(page, ((0, 0), (0, LANES - page.shape[1]))))
+                at += page.shape[0]
+    starts.append(at)
+    return spec_cols, spec_rows, Book(np.concatenate(pages, 0), starts, places, blocks)
+
+
+class Book:
+    def __init__(self, pages, starts, places, blocks):
+        self.pages, self.starts, self.places, self.blocks = pages, starts, places, blocks
+
+    def rows(self, chapter):
+        return self.starts[chapter + 1] - self.starts[chapter]
+
+    def shapes(self, *chapters):
+        return [jax.ShapeDtypeStruct((self.rows(chapter), LANES), bf16) for chapter in chapters]
+
+    def where(self, ref, chapter, block=0):
+        return ref.at[pl.ds(self.starts[chapter] + block * self.rows(chapter), self.rows(chapter))]
+
+    def read(self, ref, name):
+        at, (rows, lanes) = self.places[name]
+        pages = [
+            ref[at + number * rows : at + (number + 1) * rows, : min(LANES, lanes - lane)]
+            for number, lane in enumerate(range(0, lanes, LANES))
+        ]
+        return pages[0] if len(pages) == 1 else jnp.concatenate(pages, 1)
+
+
+LIFT, FINE, DROP, GRAD, IMAGE_ROWS = range(5)
 
 
 def dot(left, right):
@@ -159,11 +191,16 @@
 
 
 def spectrum_kernel(
-    mask_ref, pupil_ref, weight_ref, cell_ref, active_ref, cols_ref, rows_ref,
-    part_ref, sent_ref,
-    mask_in, pupil_in, weight_in, cell_in, active_in, cols, rows, sems, lined, paired,
+    mask_ref, pupil_ref, weight_ref, cell_ref, active_ref, class_ref, thresholds_ref,
+    cols_ref, rows_ref,
+    part_ref, sent_ref, threshold_ref,
+    mask_in, pupil_in, weight_in, cell_in, active_in, thresholds, cols, rows,
+    sems, lined, paired,
 ):
-    get_active, get_cell, get_pupil, get_weight, get_mask, get_cols, get_rows = copies(
+    (
+        get_active, get_cell, get_pupil, get_weight, get_mask, get_cols, get_rows,
+        get_thresholds,
+    ) = copies(
         sems,
         (active_ref, active_in),
         (cell_ref, cell_in),
@@ -172,6 +209,7 @@
         (mask_ref.at[0], mask_in),
         (cols_ref, cols),
         (rows_ref.at[my_block()], rows),
+        (thresholds_ref, thresholds),
     )
     get_active.wait()
     get_cell.wait()
@@ -223,6 +261,12 @@
     high, low = split(jnp.concatenate([part, turned], 0))
     product = dot(rows[...], jnp.concatenate([high, low], 1))
     part_ref[...] = product[:W, :LANES] + product[:W, LANES:] + product[W:, :LANES]
+    get_thresholds.wait()
+    kind = class_ref[0]
+    threshold = thresholds[0]
+    for number in range(1, CLASSES):
+        threshold = jnp.where(kind == number, thresholds[number], threshold)
+    threshold_ref[...] = jnp.full(threshold_ref.shape, threshold, f32)
 
 
 def pack_kernel(part_ref, *refs):
@@ -236,6 +280,23 @@
     out_ref[AT_PUPILS:] = sent_ref[...]
 
 
+def stage_kernel(book, target_ref, book_ref, *refs):
+    *out_refs, sems = refs
+    target_out, lift_out, fine_out, rows_out, drop_out, grad_out, grad_rows_out = out_refs
+    gets = copies(
+        sems,
+        (book.where(book_ref, LIFT), lift_out),
+        (book.where(book_ref, IMAGE_ROWS, my_block()), rows_out),
+        (book.where(book_ref, FINE), fine_out),
+        (target_ref.at[0], target_out),
+        (book.where(book_ref, DROP), drop_out),
+        (book.where(book_ref, GRAD), grad_out),
+        (book.where(book_ref, IMAGE_ROWS + book.blocks, my_block()), grad_rows_out),
+    )
+    for get in gets:
+        get.wait()
+
+
 def owners_of(refs):
     src = lax.axis_index("src")
     if len(refs) > 1:
@@ -280,31 +341,15 @@
     return lane_of((rows, LANES)) // K % 2 == 0
 
 
-def image_kernel(n_sent, *refs):
+def image_kernel(book, n_sent, *refs):
     sent_refs, refs = refs[:n_sent], refs[n_sent:]
     (
-        target_ref, class_ref, thresholds_ref,
-        lift_cols_ref, lift_rows_ref, fine_rows_ref, fine_cols_ref, fold_cols_ref, fold_rows_ref,
-        intensity_ref, fold_ref, fields_ref,
-        target, kinds, thresholds,
-        lift_cols, lift_rows, fine_rows, fine_cols, fold_cols, fold_rows,
+        threshold_ref, target, lift, fine, image_rows,
+        intensity_ref, fold_ref, fields,
         sems, codes_v, codes, spectrum, intensity_out,
     ) = refs
-    block = my_block()
     codes_of(sent_refs, codes_v)
-    gets = copies(
-        sems,
-        (codes_v, codes),
-        (lift_cols_ref, lift_cols),
-        (lift_rows_ref, lift_rows),
-        (class_ref, kinds),
-        (thresholds_ref, thresholds),
-        (fine_rows_ref.at[block], fine_rows),
-        (fine_cols_ref, fine_cols),
-        (target_ref.at[0], target),
-        (fold_cols_ref, fold_cols),
-        (fold_rows_ref.at[block], fold_rows),
-    )
+    (get_codes,) = copies(sems, (codes_v, codes))
 
     def gather(total, items):
         for ref, owner in items:
@@ -312,8 +357,8 @@
         return total
 
     spectrum[...] = over_owners(sent_refs, gather, jnp.zeros((W, LANES), f32))
-    for get in gets[:3]:
-        get.wait()
+    get_codes.wait()
+    lift_cols, lift_rows = book.read(lift, "lift_cols"), book.read(lift, "lift_rows")
     even = slot_lanes(K)
     turn_low = signs(K, -1.0, 1.0)
     turn = signs(M, -1.0, 1.0)
@@ -330,41 +375,36 @@
                 window = jnp.where(even, left, right)
                 waves.append((real * window + imag * (turn_low * swap(window))).astype(bf16))
         wave = jnp.concatenate(waves, 0)
-        high, low = split(dot(jnp.concatenate([wave, wave], 1), lift_cols[...]))
+        high, low = split(dot(jnp.concatenate([wave, wave], 1), lift_cols))
         number = 0
         for ref, owner in items:
             weights = ref[pl.ds(AT_TAIL, 16), :].astype(f32)
             for pair in range(PAIRS):
                 here = slice(number * K, (number + 1) * K)
                 number += 1
-                raw = dot(lift_rows[...], jnp.concatenate([high[here], high[here], low[here]], 0))
+                raw = dot(lift_rows, jnp.concatenate([high[here], high[here], low[here]], 0))
                 for slot in range(2):
                     mine = raw[:, slot * LANES : (slot + 1) * LANES]
                     field = mine[:M] + turn * swap(mine[M:])
-                    fields_ref[owner * MOST + 2 * pair + slot] = field
+                    fields[owner * MOST + 2 * pair + slot] = field
                     at = 2 * pair + slot
                     total = total + weights[at : at + 1] * (field * field)
         return total
 
     power = over_owners(sent_refs, forward, jnp.zeros((M, LANES), f32))
-    for get in gets[3:]:
-        get.wait()
     high, low = split(power + swap(power))
-    half = dot(fine_rows[...], jnp.concatenate([high, high, low, low], 0))
+    half = dot(book.read(image_rows, "fine_rows"), jnp.concatenate([high, high, low, low], 0))
     high, low = split(half)
-    intensity = dot(jnp.concatenate([high, low], 1), fine_cols[...])
+    intensity = dot(jnp.concatenate([high, low], 1), book.read(fine, "fine_cols"))
     intensity_out[...] = intensity
-    put = pltpu.make_async_copy(intensity_out, intensity_ref.at[0], sems.at[len(gets)])
+    put = pltpu.make_async_copy(intensity_out, intensity_ref.at[0], sems.at[1])
     put.start()
-    kind = kinds[0]
-    threshold = thresholds[0]
-    for number in range(1, CLASSES):
-        threshold = jnp.where(kind == number, thresholds[number], threshold)
+    threshold = threshold_ref[:1, :1]
     resist = 1.0 / (1.0 + jnp.exp(-STEEP * (intensity - threshold)))
     slope = (2.0 * STEEP * (resist - target[...]) * resist * (1.0 - resist)).astype(bf16)
-    folded = dot(slope, fold_cols[...])
+    folded = dot(slope, book.read(fine, "fold_cols"))
     high, low = split(folded + swap(folded))
-    grid = dot(fold_rows[...], jnp.concatenate([high, high, low], 0))
+    grid = dot(book.read(image_rows, "fold_rows"), jnp.concatenate([high, high, low], 0))
     lane = lane_of((M // 2, LANES))
     fold_ref[: M // 2] = jnp.where(lane < M, grid[: M // 2], grid[M // 2 :])
 
@@ -372,7 +412,7 @@
         for ref, owner in items:
             for slot in range(MOST):
                 number = owner * MOST + slot
-                field = fields_ref[number]
+                field = fields[number]
                 total = jnp.sum(grid * (field * field), 0, keepdims=True)
                 fold_ref[pl.ds(M // 2 + number, 1), :] = total
         return none
@@ -381,23 +421,16 @@
     put.wait()
 
 
-def gradient_kernel(n_fold, n_sent, *refs):
+def gradient_kernel(book, n_fold, n_sent, *refs):
     fold_refs, refs = refs[:n_fold], refs[n_fold:]
     sent_refs, refs = refs[:n_sent], refs[n_sent:]
     (
-        fields_ref, drop_rows_ref, drop_cols_ref, grad_rows_ref, grad_cols_ref,
+        fields, drop, grad_table, rows_table,
         mask_grad_ref,
-        drop_rows, drop_cols, grad_rows, grad_cols, sems, codes_v, codes, sums, mask_grad_out,
+        sems, codes_v, codes, sums, mask_grad_out,
     ) = refs
     codes_of(sent_refs, codes_v)
-    gets = copies(
-        sems,
-        (drop_rows_ref, drop_rows),
-        (codes_v, codes),
-        (drop_cols_ref, drop_cols),
-        (grad_rows_ref.at[my_block()], grad_rows),
-        (grad_cols_ref, grad_cols),
-    )
+    (get_codes,) = copies(sems, (codes_v, codes))
     packed = fold_refs[0][: M // 2]
     for ref in fold_refs[1:]:
         packed = packed + ref[: M // 2]
@@ -411,23 +444,23 @@
     turn = signs(K, 1.0, -1.0)
     even = slot_lanes(K)
     real_or_imag = lane_of((K, LANES)) % M < K
-    for get in gets[:3]:
-        get.wait()
+    get_codes.wait()
+    drop_rows, drop_cols = book.read(drop, "drop_rows"), book.read(drop, "drop_cols")
 
     def backward(none, items):
         waves = []
         for ref, owner in items:
             for pair in range(PAIRS):
-                fields = [grid * fields_ref[owner * MOST + 2 * pair + slot] for slot in range(2)]
-                high, low = split(jnp.concatenate(fields, 1))
-                raw = dot(drop_rows[...], jnp.concatenate([high, high, low], 0))
+                scaled = [grid * fields[owner * MOST + 2 * pair + slot] for slot in range(2)]
+                high, low = split(jnp.concatenate(scaled, 1))
+                raw = dot(drop_rows, jnp.concatenate([high, high, low], 0))
                 wave = []
                 for slot in range(2):
                     mine = raw[:, slot * LANES : (slot + 1) * LANES]
                     wave.append(mine[:K] + turn * swap(mine[K:]))
                 waves.append(jnp.concatenate(wave, 1))
         high, low = split(jnp.concatenate(waves, 0))
-        back = dot(jnp.concatenate([high, high, low], 1), drop_cols[...])
+        back = dot(jnp.concatenate([high, high, low], 1), drop_cols)
         number = 0
         for ref, owner in items:
             weights = ref[pl.ds(AT_TAIL, 16), :].astype(f32) * (2.0 / K)
@@ -446,24 +479,31 @@
         return none
 
     over_owners(sent_refs, backward, 0)
-    for get in gets[3:]:
-        get.wait()
+    grad_cols = book.read(grad_table, "grad_cols")
     grad = sums[0] + sums[1]
     turn = signs(W, 1.0, -1.0)
     high, low = split(jnp.concatenate([grad * turn, -swap(grad)], 0))
-    half = dot(grad_rows[...], jnp.concatenate([high, high, low], 0))
+    half = dot(book.read(rows_table, "grad_rows"), jnp.concatenate([high, high, low], 0))
     high, low = split(half)
-    mask_grad_out[...] = dot(jnp.concatenate([high, high], 1), grad_cols[...]) + dot(
+    mask_grad_out[...] = dot(jnp.concatenate([high, high], 1), grad_cols) + dot(
         low, grad_cols[:LANES]
     )
-    put = pltpu.make_async_copy(mask_grad_out, mask_grad_ref.at[0], sems.at[len(gets)])
+    put = pltpu.make_async_copy(mask_grad_out, mask_grad_ref.at[0], sems.at[1])
     put.start()
     put.wait()
 
 
 VMEM = pl.BlockSpec(memory_space=pltpu.VMEM)
+SMEM = pl.BlockSpec(memory_space=pltpu.SMEM)
 HBM = pl.BlockSpec(memory_space=pltpu.HBM)
-PARAMS = pltpu.CompilerParams(vmem_limit_bytes=48 * 1024 * 1024)
+
+
+def room(kib):
+    return pltpu.CompilerParams(vmem_limit_bytes=(64 * 1024 - kib) * 1024)
+
+
+def in_hbm(value):
+    return pltpu.with_memory_space_constraint(value, pltpu.HBM)
 
 
 def others(value, axis):
@@ -484,18 +524,20 @@
     slots = source_pupil.shape[0]
     src_count = lax.axis_size("src")
     few = src_count in (2, 4)
-    table = {name: jnp.asarray(value) for name, value in tables(period, span).items()}
+    spec_cols, spec_rows, book = tables(period, span)
+    pages = jnp.asarray(book.pages)
     src = lax.axis_index("src")
     sems = pltpu.SemaphoreType.DMA
     smem = pltpu.SMEM
 
-    part, sent = pl.pallas_call(
+    part, sent, threshold = pl.pallas_call(
         spectrum_kernel,
-        in_specs=[HBM] * 7,
-        out_specs=[VMEM, VMEM],
+        in_specs=[HBM] * 5 + [SMEM] + [HBM] * 3,
+        out_specs=[VMEM] * 3,
         out_shape=[
             jax.ShapeDtypeStruct((W, LANES), f32),
             jax.ShapeDtypeStruct((ROWS - AT_PUPILS, LANES), bf16),
+            jax.ShapeDtypeStruct((8, LANES), f32),
         ],
         scratch_shapes=[
             like(mask[0]),
@@ -503,17 +545,19 @@
             like(source_weight),
             smem(source_cell.shape, jnp.int32),
             smem(active_count.shape, jnp.int32),
-            like(table["spec_cols"]),
-            like(table["spec_rows"][0]),
-            sems((7,)),
+            smem(thresholds.shape, f32),
+            like(spec_cols),
+            like(spec_rows[0]),
+            sems((8,)),
             pltpu.VMEM((LANES, LANES), f32),
             pltpu.VMEM((PAIRS * K, LANES), f32),
         ],
-        compiler_params=PARAMS,
+        compiler_params=room(24576),
         name="spectrum",
     )(
-        mask, source_pupil, source_weight, source_cell, active_count,
-        table["spec_cols"], table["spec_rows"],
+        *map(in_hbm, (mask, source_pupil, source_weight, source_cell, active_count)),
+        tile_class,
+        *map(in_hbm, (thresholds, jnp.asarray(spec_cols), jnp.asarray(spec_rows))),
     )
     from_pix = others(part, "pix")
     sent = pl.pallas_call(
@@ -521,7 +565,7 @@
         in_specs=[VMEM] * (2 + len(from_pix)),
         out_specs=VMEM,
         out_shape=jax.ShapeDtypeStruct((ROWS, LANES), bf16),
-        compiler_params=PARAMS,
+        compiler_params=room(32768),
         name="pack",
     )(part, *from_pix, sent)
     if few:
@@ -529,13 +573,29 @@
     else:
         parcels = [lax.all_gather(sent, "src")]
 
+    late_target, late_pages, _ = lax.optimization_barrier((target, pages, sent))
+    staged_shapes = [
+        jax.ShapeDtypeStruct((span, period), f32),
+        *book.shapes(LIFT, FINE, IMAGE_ROWS, DROP, GRAD, IMAGE_ROWS + book.blocks),
+    ]
+    staged = pl.pallas_call(
+        functools.partial(stage_kernel, book),
+        in_specs=[HBM] * 2,
+        out_specs=[VMEM] * len(staged_shapes),
+        out_shape=staged_shapes,
+        scratch_shapes=[sems((len(staged_shapes),))],
+        compiler_params=room(24576),
+        name="stage",
+    )(in_hbm(late_target), in_hbm(late_pages))
+    for_image, for_gradient = staged[:4], staged[4:]
+
     numbers = src_count * MOST
     owners_up = -(-src_count // 8) * 8
     fold_out = M // 2 + -(-numbers // 8) * 8
     codes = [pltpu.VMEM((owners_up, LANES), jnp.int32), smem((owners_up, LANES), jnp.int32)]
     intensity, folded, fields = pl.pallas_call(
-        functools.partial(image_kernel, len(parcels)),
-        in_specs=[VMEM] * len(parcels) + [HBM] * 9,
+        functools.partial(image_kernel, book, len(parcels)),
+        in_specs=[VMEM] * (len(parcels) + 1 + len(for_image)),
         out_specs=[HBM, VMEM, VMEM],
         out_shape=[
             jax.ShapeDtypeStruct((1, span, period), f32),
@@ -543,27 +603,14 @@
             jax.ShapeDtypeStruct((numbers, M, LANES), f32),
         ],
         scratch_shapes=[
-            like(target[0]),
-            smem(tile_class.shape, jnp.int32),
-            smem(thresholds.shape, f32),
-            like(table["lift_cols"]),
-            like(table["lift_rows"]),
-            like(table["fine_rows"][0]),
-            like(table["fine_cols"]),
-            like(table["fold_cols"]),
-            like(table["fold_rows"][0]),
-            sems((11,)),
+            sems((2,)),
             *codes,
             pltpu.VMEM((W, LANES), f32),
             like(target[0]),
         ],
-        compiler_params=PARAMS,
+        compiler_params=room(24576),
         name="image",
-    )(
-        *parcels, target, tile_class, thresholds,
-        table["lift_cols"], table["lift_rows"], table["fine_rows"], table["fine_cols"],
-        table["fold_cols"], table["fold_rows"],
-    )
+    )(*parcels, threshold, *for_image)
 
     for other in others(folded, "pix"):
         folded = folded + other
@@ -573,26 +620,19 @@
     for other in others(rows, "tile"):
         rows = rows + other
     mask_grad = pl.pallas_call(
-        functools.partial(gradient_kernel, len(folds), len(parcels)),
-        in_specs=[VMEM] * (len(folds) + len(parcels) + 1) + [HBM] * 4,
+        functools.partial(gradient_kernel, book, len(folds), len(parcels)),
+        in_specs=[VMEM] * (len(folds) + len(parcels) + 1 + len(for_gradient)),
         out_specs=HBM,
         out_shape=jax.ShapeDtypeStruct((1, span, period), f32),
         scratch_shapes=[
-            like(table["drop_rows"]),
-            like(table["drop_cols"]),
-            like(table["grad_rows"][0]),
-            like(table["grad_cols"]),
-            sems((6,)),
+            sems((2,)),
             *codes,
             pltpu.VMEM((2, W, LANES), f32),
             like(mask[0]),
         ],
-        compiler_params=PARAMS,
+        compiler_params=room(24576),
         name="gradient",
-    )(
-        *folds, *parcels, fields,
-        table["drop_rows"], table["drop_cols"], table["grad_rows"], table["grad_cols"],
-    )
+    )(*folds, *parcels, fields, *for_gradient)
     sums = jnp.sum(rows, 1) * (1.0 / (period * K))
     source_grad = jnp.zeros((slots,), f32).at[:MOST].set(sums)
     return intensity, mask_grad, source_grad

time: 40.6 us -> 33.6 us (0.83)
  local copies, waits for them, and re-layouts: 8.47 us -> 0.52 us
  Pallas kernels: 7.54 us -> 9.88 us
  waiting for transfers between devices: 10.5 us -> 9.41 us
    unnamed x38 -> x0, local copies, waits for them, and re-layouts: 7.95 us -> none
    pallas_call x3 -> x4, Pallas kernels: 7.53 us -> 9.87 us  [the longest x1 3.27 us: shards(): pl.pallas_call(functools.partial(image_kernel, book, len(parcels)), in_sp...]
    ppermute x9, waiting for transfers between devices: 10.5 us -> 9.41 us  [others(): lax.ppermute(value, axis, [(i, i ^ step) for i in range(size)])]
  transfers between devices with their start and end apart: 9 -> 9, of which waited for: 6 -> 6; matrix products, arithmetic and copies ran while one was open for 0% -> 0% of each run, Pallas kernels for 8% -> 14%
where the time goes in v3:
time: 33.6 us; the launch traced here: 33.4 us
  starting transfers between devices  12.1 us (36%)
  Pallas kernels  9.88 us (29%)
  waiting for transfers between devices  9.41 us (28%)
  between operations  1.35 us (4%)
  local copies, waits for them, and re-layouts  0.52 us (2%)
    ppermute x9, starting transfers between devices, others(): lax.ppermute(value, axis, [(i, i ^ step) for i in range(size)])  12.1 us
    ppermute x9, waiting for transfers between devices, others(): lax.ppermute(value, axis, [(i, i ^ step) for i in range(size)])  9.41 us
    pallas_call x1, Pallas kernels, shards(): pl.pallas_call(functools.partial(image_kernel, book, len(parcels)), in_sp...  3.27 us
    pallas_call x1, Pallas kernels, shards(): pl.pallas_call(functools.partial(gradient_kernel, book, len(folds), len(p...  3 us
    pallas_call x1, Pallas kernels, shards(): pl.pallas_call(spectrum_kernel, in_specs=[HBM] * 5 + [SMEM] + [HBM] * 3,...  1.88 us
    pallas_call x1, Pallas kernels, shards(): pl.pallas_call(functools.partial(stage_kernel, book), in_specs=[HBM] * 2,...  1.71 us
  transfers between devices with their start and end apart: 9, of which 6 were waited for; matrix products, arithmetic and copies ran while one was open for 0% of the time, Pallas kernels for 14%

profile of v3, /device:TPU:0, one launch (start us, length us, event | category | flops | bytes accessed | tf_op | source)
XLA Modules:
  0.0 33.4 jit_solution(10373190483836791251)
XLA Ops:
  1.3 1.9 %spectrum.1 = (f32[48,128]{1,0:T(8,128)S(1)}, bf16[112,128]{1,0:T(8,128)(2,1)S(1)}, f32[8,128]{1,0:T(8,128)S(1)}) custom-call(f32[1,128,1024]{2,1,0:T(8,128)} %mask_ref.1, bf16[128,2048]{1,0:T(8,128)(2,1)} %pupil_ref.1, bf16[128]{0:T(256)(128)(2,1)} %weight_ref.1, s32[128]{0:T(128)} %cell_ref.1, s32[4]{0:T(128)} %active_ref.1, s32[1]{0:T(128)S(6)} %copy.14.class_ref, ...), custom_call_target="tpu_custom_call" | custom-call | tf_op jit(solution)/shard_map/spectrum/pallas_call | solution.py:533
  3.2 0.5 %collective-permute-start = (f32[48,128]{1,0:T(8,128)S(1)}, f32[48,128]{1,0:T(8,128)S(1)}, u32[]{:S(2)}, u32[]{:S(2)}) collective-permute-start(f32[48,128]{1,0:T(8,128)S(1)} %get-tuple-element.30.part_ref), channel_id=1, source_target_pairs={{0,1},{1,0},{2,3},{3,2},{4,5},{5,4},{6,7},{7,6},{8,9},{9,8},{10,11... | collective-permute-start | bytes 73736 | tf_op jit(solution)/shard_map/ppermute | solution.py:512
  3.7 0.8 %collective-permute-done.refs_0_ = f32[48,128]{1,0:T(8,128)S(1)} collective-permute-done((f32[48,128]{1,0:T(8,128)S(1)}, f32[48,128]{1,0:T(8,128)S(1)}, u32[]{:S(2)}, u32[]{:S(2)}) %collective-permute-start) | collective-permute-done | bytes 24608 | tf_op jit(solution)/shard_map/ppermute | solution.py:512
  4.5 3.0 %collective-permute-start.1 = (bf16[208,128]{1,0:T(8,128)(2,1)S(1)}, bf16[208,128]{1,0:T(8,128)(2,1)S(1)}, u32[]{:S(2)}, u32[]{:S(2)}) collective-permute-start(bf16[208,128]{1,0:T(8,128)(2,1)S(1)} %pack.1.refs_0_.refs_4_), channel_id=1, source_target_pairs={{0,4},{4,0},{8,12},{12,8},{1,5},{5,1},{9,13},{13,9},{2,6},{6,2},{1... | collective-permute-start | bytes 159752 | tf_op jit(solution)/shard_map/ppermute | solution.py:512
  7.5 2.6 %collective-permute-start.2 = (bf16[208,128]{1,0:T(8,128)(2,1)S(1)}, bf16[208,128]{1,0:T(8,128)(2,1)S(1)}, u32[]{:S(2)}, u32[]{:S(2)}) collective-permute-start(bf16[208,128]{1,0:T(8,128)(2,1)S(1)} %pack.1.refs_0_.refs_4_), channel_id=1, source_target_pairs={{0,8},{4,12},{8,0},{12,4},{1,9},{5,13},{9,1},{13,5},{2,10},{6,14},... | collective-permute-start | bytes 159752 | tf_op jit(solution)/shard_map/ppermute | solution.py:512
  10.1 0.0 collective-permute-start.3
  10.1 1.7 %stage.1 = (f32[128,1024]{1,0:T(8,128)S(1)}, bf16[640,128]{1,0:T(8,128)(2,1)S(1)}, bf16[3072,128]{1,0:T(8,128)(2,1)S(1)}, bf16[448,128]{1,0:T(8,128)(2,1)S(1)}, ...) custom-call(f32[1,128,1024]{2,1,0:T(8,128)} %target_ref, ...), custom_call_target="tpu_custom_call" | custom-call | tf_op jit(solution)/shard_map/stage/pallas_call | solution.py:581
  11.8 0.0 collective-permute-done.1.refs_1_.refs_5_
  11.9 1.9 %collective-permute-done.2.refs_2_.refs_6_ = bf16[208,128]{1,0:T(8,128)(2,1)S(1)} collective-permute-done((bf16[208,128]{1,0:T(8,128)(2,1)S(1)}, bf16[208,128]{1,0:T(8,128)(2,1)S(1)}, u32[]{:S(2)}, u32[]{:S(2)}) %collective-permute-start.2) | collective-permute-done | bytes 53280 | tf_op jit(solution)/shard_map/ppermute | solution.py:512
  13.7 2.3 %collective-permute-done.3.refs_3_.refs_7_ = bf16[208,128]{1,0:T(8,128)(2,1)S(1)} collective-permute-done((bf16[208,128]{1,0:T(8,128)(2,1)S(1)}, bf16[208,128]{1,0:T(8,128)(2,1)S(1)}, u32[]{:S(2)}, u32[]{:S(2)}) %collective-permute-start.3) | collective-permute-done | bytes 53280 | tf_op jit(solution)/shard_map/ppermute | solution.py:512
  16.0 3.3 %image.1 = (f32[1,128,1024]{2,1,0:T(8,128)}, f32[56,128]{1,0:T(8,128)S(1)}, f32[24,64,128]{2,1,0:T(8,128)S(1)}) custom-call(bf16[208,128]{1,0:T(8,128)(2,1)S(1)} %pack.1.refs_0_.refs_4_, bf16[208,128]{1,0:T(8,128)(2,1)S(1)} %collective-permute-done.1.refs_1_.refs_5_, bf16[208,128]{1,0:T(8,128)(2,1)S(1)} %collective-permute-done.2.refs_2_.refs_6_, ...), custom_call_target="tpu_custom_call" | custom-call | tf_op jit(solution)/shard_map/image/pallas_call | solution.py:596
  19.3 0.1 collective-permute-start.4
  19.4 1.2 %collective-permute-done.4 = f32[56,128]{1,0:T(8,128)S(1)} collective-permute-done((f32[56,128]{1,0:T(8,128)S(1)}, f32[56,128]{1,0:T(8,128)S(1)}, u32[]{:S(2)}, u32[]{:S(2)}) %collective-permute-start.4) | collective-permute-done | bytes 28704 | tf_op jit(solution)/shard_map/ppermute | solution.py:512
  20.6 0.0 collective-permute-start.5
  20.6 1.9 %collective-permute-start.6 = (f32[56,128]{1,0:T(8,128)S(1)}, f32[56,128]{1,0:T(8,128)S(1)}, u32[]{:S(2)}, u32[]{:S(2)}) collective-permute-start(f32[56,128]{1,0:T(8,128)S(1)} %add.27.refs_0_), channel_id=1, source_target_pairs={{0,8},{4,12},{8,0},{12,4},{1,9},{5,13},{9,1},{13,5},{2,10},{6,14},... | collective-permute-start | bytes 86024 | tf_op jit(solution)/shard_map/ppermute | solution.py:512
  22.5 2.5 %collective-permute-start.7 = (f32[56,128]{1,0:T(8,128)S(1)}, f32[56,128]{1,0:T(8,128)S(1)}, u32[]{:S(2)}, u32[]{:S(2)}) collective-permute-start(f32[56,128]{1,0:T(8,128)S(1)} %add.27.refs_0_), channel_id=1, source_target_pairs={{0,12},{4,8},{8,4},{12,0},{1,13},{5,9},{9,5},{13,1},{2,14},{6,10},... | collective-permute-start | bytes 86024 | tf_op jit(solution)/shard_map/ppermute | solution.py:512
  25.0 0.0 collective-permute-done.5.refs_1_
  25.0 1.0 %collective-permute-done.6.refs_2_ = f32[56,128]{1,0:T(8,128)S(1)} collective-permute-done((f32[56,128]{1,0:T(8,128)S(1)}, f32[56,128]{1,0:T(8,128)S(1)}, u32[]{:S(2)}, u32[]{:S(2)}) %collective-permute-start.6) | collective-permute-done | bytes 28704 | tf_op jit(solution)/shard_map/ppermute | solution.py:512
  25.9 2.2 %collective-permute-done.7.refs_3_ = f32[56,128]{1,0:T(8,128)S(1)} collective-permute-done((f32[56,128]{1,0:T(8,128)S(1)}, f32[56,128]{1,0:T(8,128)S(1)}, u32[]{:S(2)}, u32[]{:S(2)}) %collective-permute-start.7) | collective-permute-done | bytes 28704 | tf_op jit(solution)/shard_map/ppermute | solution.py:512
  28.2 1.6 %collective-permute-start.8 = (f32[6,128]{1,0:T(8,128)S(1)}, f32[6,128]{1,0:T(8,128)S(1)}, u32[]{:S(2)}, u32[]{:S(2)}) collective-permute-start(f32[6,128]{1,0:T(8,128)S(1)} %dynamic-slice_add_fusion), channel_id=1, source_target_pairs={{0,2},{2,0},{1,3},{3,1},{4,6},{6,4},{5,7},{7,5},{8,10},{10,8},{9,1... | collective-permute-start | bytes 9224 | tf_op jit(solution)/shard_map/ppermute | solution.py:512
  29.7 3.0 %gradient.1 = f32[1,128,1024]{2,1,0:T(8,128)} custom-call(f32[56,128]{1,0:T(8,128)S(1)} %add.27.refs_0_, f32[56,128]{1,0:T(8,128)S(1)} %collective-permute-done.5.refs_1_, f32[56,128]{1,0:T(8,128)S(1)} %collective-permute-done.6.refs_2_, f32[56,128]{1,0:T(8,128)S(1)} %collective-permute-done.7.refs_3_, bf16[208,128]{1,0:T(8,128)(2,1)S(1)} %pack.1.refs_0_.refs_4_, ...), custom_call_target="tpu_custom_call" | custom-call | tf_op jit(solution)/shard_map/gradient/pallas_call | solution.py:622
  32.7 0.0 collective-permute-done.8
  32.7 0.1 add_reduce_fusion
  32.9 0.5 %scatter.4 = f32[128]{0:T(128)} pad(f32[6]{0:T(128)S(1)} %broadcast_multiply_fusion, f32[]{:T(128)} %constant.46.clone.1), padding=0_122 | pad | bytes 540 | tf_op jit(solution)/shard_map/scatter | solution.py:637
  (4 shorter events, 0.0 us)
Async XLA Ops:
  3.2 1.4 %collective-permute-start = (f32[48,128]{1,0:T(8,128)S(1)}, f32[48,128]{1,0:T(8,128)S(1)}, u32[]{:S(2)}, u32[]{:S(2)}) collective-permute-start(f32[48,128]{1,0:T(8,128)S(1)} %get-tuple-element.30.part_ref), channel_id=1, source_target_pairs={{0,1},{1,0},{2,3},{3,2},{4,5},{5,4},{6,7},{7,6},{8,9},{9,8},{10,11... | collective-permute-start | bytes 73736 | tf_op jit(solution)/shard_map/ppermute | solution.py:512
  4.5 7.3 %collective-permute-start.1 = (bf16[208,128]{1,0:T(8,128)(2,1)S(1)}, bf16[208,128]{1,0:T(8,128)(2,1)S(1)}, u32[]{:S(2)}, u32[]{:S(2)}) collective-permute-start(bf16[208,128]{1,0:T(8,128)(2,1)S(1)} %pack.1.refs_0_.refs_4_), channel_id=1, source_target_pairs={{0,4},{4,0},{8,12},{12,8},{1,5},{5,1},{9,13},{13,9},{2,6},{6,2},{1... | collective-permute-start | bytes 159752 | tf_op jit(solution)/shard_map/ppermute | solution.py:512
  7.5 6.2 %collective-permute-start.2 = (bf16[208,128]{1,0:T(8,128)(2,1)S(1)}, bf16[208,128]{1,0:T(8,128)(2,1)S(1)}, u32[]{:S(2)}, u32[]{:S(2)}) collective-permute-start(bf16[208,128]{1,0:T(8,128)(2,1)S(1)} %pack.1.refs_0_.refs_4_), channel_id=1, source_target_pairs={{0,8},{4,12},{8,0},{12,4},{1,9},{5,13},{9,1},{13,5},{2,10},{6,14},... | collective-permute-start | bytes 159752 | tf_op jit(solution)/shard_map/ppermute | solution.py:512
  10.1 5.9 %collective-permute-start.3 = (bf16[208,128]{1,0:T(8,128)(2,1)S(1)}, bf16[208,128]{1,0:T(8,128)(2,1)S(1)}, u32[]{:S(2)}, u32[]{:S(2)}) collective-permute-start(bf16[208,128]{1,0:T(8,128)(2,1)S(1)} %pack.1.refs_0_.refs_4_), channel_id=1, source_target_pairs={{0,12},{4,8},{8,4},{12,0},{1,13},{5,9},{9,5},{13,1},{2,14},{6,10},... | collective-permute-start | bytes 159752 | tf_op jit(solution)/shard_map/ppermute | solution.py:512
  19.3 1.3 %collective-permute-start.4 = (f32[56,128]{1,0:T(8,128)S(1)}, f32[56,128]{1,0:T(8,128)S(1)}, u32[]{:S(2)}, u32[]{:S(2)}) collective-permute-start(f32[56,128]{1,0:T(8,128)S(1)} %get-tuple-element.40), channel_id=1, source_target_pairs={{0,1},{1,0},{2,3},{3,2},{4,5},{5,4},{6,7},{7,6},{8,9},{9,8},{10,11... | collective-permute-start | bytes 86024 | tf_op jit(solution)/shard_map/ppermute | solution.py:512
  20.6 4.4 %collective-permute-start.5 = (f32[56,128]{1,0:T(8,128)S(1)}, f32[56,128]{1,0:T(8,128)S(1)}, u32[]{:S(2)}, u32[]{:S(2)}) collective-permute-start(f32[56,128]{1,0:T(8,128)S(1)} %add.27.refs_0_), channel_id=1, source_target_pairs={{0,4},{4,0},{8,12},{12,8},{1,5},{5,1},{9,13},{13,9},{2,6},{6,2},{1... | collective-permute-start | bytes 86024 | tf_op jit(solution)/shard_map/ppermute | solution.py:512
  20.6 5.3 %collective-permute-start.6 = (f32[56,128]{1,0:T(8,128)S(1)}, f32[56,128]{1,0:T(8,128)S(1)}, u32[]{:S(2)}, u32[]{:S(2)}) collective-permute-start(f32[56,128]{1,0:T(8,128)S(1)} %add.27.refs_0_), channel_id=1, source_target_pairs={{0,8},{4,12},{8,0},{12,4},{1,9},{5,13},{9,1},{13,5},{2,10},{6,14},... | collective-permute-start | bytes 86024 | tf_op jit(solution)/shard_map/ppermute | solution.py:512
  22.5 5.7 %collective-permute-start.7 = (f32[56,128]{1,0:T(8,128)S(1)}, f32[56,128]{1,0:T(8,128)S(1)}, u32[]{:S(2)}, u32[]{:S(2)}) collective-permute-start(f32[56,128]{1,0:T(8,128)S(1)} %add.27.refs_0_), channel_id=1, source_target_pairs={{0,12},{4,8},{8,4},{12,0},{1,13},{5,9},{9,5},{13,1},{2,14},{6,10},... | collective-permute-start | bytes 86024 | tf_op jit(solution)/shard_map/ppermute | solution.py:512
  28.2 4.6 %collective-permute-start.8 = (f32[6,128]{1,0:T(8,128)S(1)}, f32[6,128]{1,0:T(8,128)S(1)}, u32[]{:S(2)}, u32[]{:S(2)}) collective-permute-start(f32[6,128]{1,0:T(8,128)S(1)} %dynamic-slice_add_fusion), channel_id=1, source_target_pairs={{0,2},{2,0},{1,3},{3,1},{4,6},{6,4},{5,7},{7,5},{8,10},{10,8},{9,1... | collective-permute-start | bytes 9224 | tf_op jit(solution)/shard_map/ppermute | solution.py:512

commit v4 on v3

--- a/solution.py
+++ b/solution.py
@@ -23,6 +23,8 @@
 AT_TAIL = AT_PUPILS + PAIRS * K
 ROWS = AT_TAIL + 16
 TAIL_PAIR, TAIL_CELL = 8, 12
+PIECES = 4
+SUMS = 8
 
 f32 = jnp.float32
 bf16 = jnp.bfloat16
@@ -178,6 +180,12 @@
 
 def my_block():
     return lax.axis_index("src") * lax.axis_size("pix") + lax.axis_index("pix")
+
+
+def chip_blocks():
+    pix, count = lax.axis_index("pix"), lax.axis_size("pix")
+    base = lax.axis_index("src") * count
+    return [base + jnp.bitwise_xor(pix, step) for step in range(count)]
 
 
 def copies(sems, *pairs):
@@ -282,13 +290,16 @@
 
 def stage_kernel(book, target_ref, book_ref, *refs):
     *out_refs, sems = refs
-    target_out, lift_out, fine_out, rows_out, drop_out, grad_out, grad_rows_out = out_refs
+    target_out, lift_out, fine_out, drop_out, grad_out, grad_rows_out, *rows_out = out_refs
     gets = copies(
         sems,
         (book.where(book_ref, LIFT), lift_out),
-        (book.where(book_ref, IMAGE_ROWS, my_block()), rows_out),
         (book.where(book_ref, FINE), fine_out),
         (target_ref.at[0], target_out),
+        *(
+            (book.where(book_ref, IMAGE_ROWS, block), out)
+            for block, out in zip(chip_blocks(), rows_out)
+        ),
         (book.where(book_ref, DROP), drop_out),
         (book.where(book_ref, GRAD), grad_out),
         (book.where(book_ref, IMAGE_ROWS + book.blocks, my_block()), grad_rows_out),
@@ -297,17 +308,9 @@
         get.wait()
 
 
-def owners_of(refs):
-    src = lax.axis_index("src")
+def over_owners(refs, body, carry):
     if len(refs) > 1:
-        return [(ref, jnp.bitwise_xor(src, step)) for step, ref in enumerate(refs)]
-    return None
-
-
-def over_owners(refs, body, carry):
-    together = owners_of(refs)
-    if together is not None:
-        return body(carry, together)
+        return body(carry, [(ref, place) for place, ref in enumerate(refs)])
     (ref,) = refs
     return lax.fori_loop(
         0, ref.shape[0], lambda owner, carry: body(carry, [(ref.at[owner], owner)]), carry
@@ -316,17 +319,17 @@
 
 def codes_of(refs, codes_v):
     def body(none, items):
-        for ref, owner in items:
+        for ref, place in items:
             tail = ref[pl.ds(AT_TAIL, 16), :].astype(f32)
             code = tail[TAIL_CELL : TAIL_CELL + 1] * 32.0 + tail[TAIL_CELL + 1 : TAIL_CELL + 2]
-            codes_v[pl.ds(owner, 1), :] = code.astype(jnp.int32)
+            codes_v[pl.ds(place, 1), :] = code.astype(jnp.int32)
         return none
 
     over_owners(refs, body, 0)
 
 
-def window_of(codes, owner, slot):
-    code = codes[owner, slot]
+def window_of(codes, place, slot):
+    code = codes[place, slot]
     return lax.div(code, 32), lax.rem(code, 32)
 
 
@@ -341,18 +344,20 @@
     return lane_of((rows, LANES)) // K % 2 == 0
 
 
-def image_kernel(book, n_sent, *refs):
+def image_kernel(book, n_sent, n_pix, *refs):
     sent_refs, refs = refs[:n_sent], refs[n_sent:]
+    targets, refs = refs[:n_pix], refs[n_pix:]
+    rows_refs, refs = refs[:n_pix], refs[n_pix:]
     (
-        threshold_ref, target, lift, fine, image_rows,
-        intensity_ref, fold_ref, fields,
+        threshold_ref, lift, fine,
+        intensity_ref, fields, *fold_refs,
         sems, codes_v, codes, spectrum, intensity_out,
     ) = refs
     codes_of(sent_refs, codes_v)
     (get_codes,) = copies(sems, (codes_v, codes))
 
     def gather(total, items):
-        for ref, owner in items:
+        for ref, place in items:
             total = total + (ref[:W].astype(f32) + ref[W : 2 * W].astype(f32))
         return total
 
@@ -365,19 +370,19 @@
 
     def forward(total, items):
         waves = []
-        for ref, owner in items:
+        for ref, place in items:
             for pair in range(PAIRS):
                 real, imag = pair_parts(ref, pair)
-                row, col = window_of(codes, owner, 2 * pair)
+                row, col = window_of(codes, place, 2 * pair)
                 left = pltpu.roll(spectrum[pl.ds(row, K), :], lax.rem(LANES - col, LANES), 1)
-                row, col = window_of(codes, owner, 2 * pair + 1)
+                row, col = window_of(codes, place, 2 * pair + 1)
                 right = pltpu.roll(spectrum[pl.ds(row, K), :], lax.rem(LANES + K - col, LANES), 1)
                 window = jnp.where(even, left, right)
                 waves.append((real * window + imag * (turn_low * swap(window))).astype(bf16))
         wave = jnp.concatenate(waves, 0)
         high, low = split(dot(jnp.concatenate([wave, wave], 1), lift_cols))
         number = 0
-        for ref, owner in items:
+        for ref, place in items:
             weights = ref[pl.ds(AT_TAIL, 16), :].astype(f32)
             for pair in range(PAIRS):
                 here = slice(number * K, (number + 1) * K)
@@ -386,35 +391,48 @@
                 for slot in range(2):
                     mine = raw[:, slot * LANES : (slot + 1) * LANES]
                     field = mine[:M] + turn * swap(mine[M:])
-                    fields[owner * MOST + 2 * pair + slot] = field
+                    fields[place * MOST + 2 * pair + slot] = field
                     at = 2 * pair + slot
                     total = total + weights[at : at + 1] * (field * field)
         return total
 
     power = over_owners(sent_refs, forward, jnp.zeros((M, LANES), f32))
     high, low = split(power + swap(power))
-    half = dot(book.read(image_rows, "fine_rows"), jnp.concatenate([high, high, low, low], 0))
-    high, low = split(half)
-    intensity = dot(jnp.concatenate([high, low], 1), book.read(fine, "fine_cols"))
-    intensity_out[...] = intensity
-    put = pltpu.make_async_copy(intensity_out, intensity_ref.at[0], sems.at[1])
-    put.start()
+    coarse = jnp.concatenate([high, high, low, low], 0)
+    fine_cols, fold_cols = book.read(fine, "fine_cols"), book.read(fine, "fold_cols")
     threshold = threshold_ref[:1, :1]
-    resist = 1.0 / (1.0 + jnp.exp(-STEEP * (intensity - threshold)))
-    slope = (2.0 * STEEP * (resist - target[...]) * resist * (1.0 - resist)).astype(bf16)
-    folded = dot(slope, book.read(fine, "fold_cols"))
-    high, low = split(folded + swap(folded))
-    grid = dot(book.read(image_rows, "fold_rows"), jnp.concatenate([high, high, low], 0))
+    grid = jnp.zeros((M, LANES), f32)
+    for number, (target, rows_ref) in enumerate(zip(targets, rows_refs)):
+        high, low = split(dot(book.read(rows_ref, "fine_rows"), coarse))
+        intensity = dot(jnp.concatenate([high, low], 1), fine_cols)
+        if number == 0:
+            intensity_out[...] = intensity
+            put = pltpu.make_async_copy(intensity_out, intensity_ref.at[0], sems.at[1])
+            put.start()
+        resist = 1.0 / (1.0 + jnp.exp(-STEEP * (intensity - threshold)))
+        slope = (2.0 * STEEP * (resist - target[...]) * resist * (1.0 - resist)).astype(bf16)
+        folded = dot(slope, fold_cols)
+        high, low = split(folded + swap(folded))
+        grid = grid + dot(
+            book.read(rows_ref, "fold_rows"), jnp.concatenate([high, high, low], 0)
+        )
     lane = lane_of((M // 2, LANES))
-    fold_ref[: M // 2] = jnp.where(lane < M, grid[: M // 2], grid[M // 2 :])
+    packed = jnp.where(lane < M, grid[: M // 2], grid[M // 2 :])
+    for fold_ref in fold_refs:
+        fold_ref[: M // 2] = packed
 
     def weigh(none, items):
-        for ref, owner in items:
+        for ref, place in items:
+            sums = []
             for slot in range(MOST):
-                number = owner * MOST + slot
-                field = fields[number]
-                total = jnp.sum(grid * (field * field), 0, keepdims=True)
-                fold_ref[pl.ds(M // 2 + number, 1), :] = total
+                field = fields[place * MOST + slot]
+                sums.append(jnp.sum(grid * (field * field), 0, keepdims=True))
+            sums = jnp.concatenate(sums + [jnp.zeros((SUMS - MOST, LANES), f32)], 0)
+            if len(fold_refs) > 1:
+                fold_refs[place][M // 2 :] = sums
+            else:
+                start = pl.multiple_of(M // 2 + place * SUMS, SUMS)
+                fold_refs[0][pl.ds(start, SUMS), :] = sums
         return none
 
     over_owners(sent_refs, weigh, 0)
@@ -449,9 +467,9 @@
 
     def backward(none, items):
         waves = []
-        for ref, owner in items:
+        for ref, place in items:
             for pair in range(PAIRS):
-                scaled = [grid * fields[owner * MOST + 2 * pair + slot] for slot in range(2)]
+                scaled = [grid * fields[place * MOST + 2 * pair + slot] for slot in range(2)]
                 high, low = split(jnp.concatenate(scaled, 1))
                 raw = dot(drop_rows, jnp.concatenate([high, high, low], 0))
                 wave = []
@@ -462,7 +480,7 @@
         high, low = split(jnp.concatenate(waves, 0))
         back = dot(jnp.concatenate([high, high, low], 1), drop_cols)
         number = 0
-        for ref, owner in items:
+        for ref, place in items:
             weights = ref[pl.ds(AT_TAIL, 16), :].astype(f32) * (2.0 / K)
             for pair in range(PAIRS):
                 mine = back[number * K : (number + 1) * K]
@@ -471,7 +489,7 @@
                 product = real * mine + imag * (turn * swap(mine))
                 product = weights[TAIL_PAIR + pair : TAIL_PAIR + pair + 1] * product
                 for slot in range(2):
-                    row, col = window_of(codes, owner, 2 * pair + slot)
+                    row, col = window_of(codes, place, 2 * pair + slot)
                     keep = even if slot == 0 else jnp.logical_not(even)
                     shift = lax.rem(col + LANES - slot * K, LANES)
                     moved = pltpu.roll(jnp.where(keep, product, 0.0), shift, 1)
@@ -485,12 +503,19 @@
     high, low = split(jnp.concatenate([grad * turn, -swap(grad)], 0))
     half = dot(book.read(rows_table, "grad_rows"), jnp.concatenate([high, high, low], 0))
     high, low = split(half)
-    mask_grad_out[...] = dot(jnp.concatenate([high, high], 1), grad_cols) + dot(
-        low, grad_cols[:LANES]
-    )
-    put = pltpu.make_async_copy(mask_grad_out, mask_grad_ref.at[0], sems.at[1])
-    put.start()
-    put.wait()
+    both = jnp.concatenate([high, high], 1)
+    chunk = grad_cols.shape[1] // PIECES
+    puts = []
+    for piece in range(PIECES):
+        here = slice(piece * chunk, (piece + 1) * chunk)
+        mask_grad_out[:, here] = dot(both, grad_cols[:, here]) + dot(low, grad_cols[:LANES, here])
+        place = mask_grad_ref.at[0, :, pl.ds(piece * chunk, chunk)]
+        puts.append(
+            pltpu.make_async_copy(mask_grad_out.at[:, pl.ds(piece * chunk, chunk)], place, sems.at[1 + piece])
+        )
+        puts[-1].start()
+    for put in puts:
+        put.wait()
 
 
 VMEM = pl.BlockSpec(memory_space=pltpu.VMEM)
@@ -506,11 +531,12 @@
     return pltpu.with_memory_space_constraint(value, pltpu.HBM)
 
 
+def exchange(value, axis, step):
+    return lax.ppermute(value, axis, [(i, i ^ step) for i in range(lax.axis_size(axis))])
+
+
 def others(value, axis):
-    size = lax.axis_size(axis)
-    return [
-        lax.ppermute(value, axis, [(i, i ^ step) for i in range(size)]) for step in range(1, size)
-    ]
+    return [exchange(value, axis, step) for step in range(1, lax.axis_size(axis))]
 
 
 def like(value):
@@ -576,7 +602,8 @@
     late_target, late_pages, _ = lax.optimization_barrier((target, pages, sent))
     staged_shapes = [
         jax.ShapeDtypeStruct((span, period), f32),
-        *book.shapes(LIFT, FINE, IMAGE_ROWS, DROP, GRAD, IMAGE_ROWS + book.blocks),
+        *book.shapes(LIFT, FINE, DROP, GRAD, IMAGE_ROWS + book.blocks),
+        *book.shapes(IMAGE_ROWS) * lax.axis_size("pix"),
     ]
     staged = pl.pallas_call(
         functools.partial(stage_kernel, book),
@@ -587,20 +614,24 @@
         compiler_params=room(24576),
         name="stage",
     )(in_hbm(late_target), in_hbm(late_pages))
-    for_image, for_gradient = staged[:4], staged[4:]
+    near_target, lift, fine, *for_gradient = staged[:6]
+    early_target, _ = lax.optimization_barrier((target, from_pix[0]))
+    targets = [near_target] + others(early_target[0], "pix")
+    image_rows = staged[6:]
 
     numbers = src_count * MOST
     owners_up = -(-src_count // 8) * 8
-    fold_out = M // 2 + -(-numbers // 8) * 8
+    fold_rows = M // 2 + (1 if few else src_count) * SUMS
+    fold_count = src_count if few else 1
     codes = [pltpu.VMEM((owners_up, LANES), jnp.int32), smem((owners_up, LANES), jnp.int32)]
-    intensity, folded, fields = pl.pallas_call(
-        functools.partial(image_kernel, book, len(parcels)),
-        in_specs=[VMEM] * (len(parcels) + 1 + len(for_image)),
-        out_specs=[HBM, VMEM, VMEM],
+    intensity, fields, *folded = pl.pallas_call(
+        functools.partial(image_kernel, book, len(parcels), len(targets)),
+        in_specs=[VMEM] * (len(parcels) + 2 * len(targets) + 3),
+        out_specs=[HBM, VMEM] + [VMEM] * fold_count,
         out_shape=[
             jax.ShapeDtypeStruct((1, span, period), f32),
-            jax.ShapeDtypeStruct((fold_out, LANES), f32),
             jax.ShapeDtypeStruct((numbers, M, LANES), f32),
+            *[jax.ShapeDtypeStruct((fold_rows, LANES), f32)] * fold_count,
         ],
         scratch_shapes=[
             sems((2,)),
@@ -610,13 +641,17 @@
         ],
         compiler_params=room(24576),
         name="image",
-    )(*parcels, threshold, *for_image)
-
-    for other in others(folded, "pix"):
-        folded = folded + other
-    folds = [folded] + others(folded, "src") if few else [lax.psum(folded, "src")]
-    first = M // 2 + src * MOST
-    rows = sum(lax.dynamic_slice_in_dim(fold, first, MOST, 0) for fold in folds)
+    )(*parcels, *targets, *image_rows, threshold, lift, fine)
+
+    if few:
+        folds = [
+            value if step == 0 else exchange(value, "src", step)
+            for step, value in enumerate(folded)
+        ]
+        rows = sum(fold[M // 2 :] for fold in folds)
+    else:
+        folds = [lax.psum(folded[0], "src")]
+        rows = lax.dynamic_slice_in_dim(folds[0], M // 2 + src * SUMS, SUMS, 0)
     for other in others(rows, "tile"):
         rows = rows + other
     mask_grad = pl.pallas_call(
@@ -625,7 +660,7 @@
         out_specs=HBM,
         out_shape=jax.ShapeDtypeStruct((1, span, period), f32),
         scratch_shapes=[
-            sems((2,)),
+            sems((1 + PIECES,)),
             *codes,
             pltpu.VMEM((2, W, LANES), f32),
             like(mask[0]),
@@ -634,7 +669,7 @@
         name="gradient",
     )(*folds, *parcels, fields, *for_gradient)
     sums = jnp.sum(rows, 1) * (1.0 / (period * K))
-    source_grad = jnp.zeros((slots,), f32).at[:MOST].set(sums)
+    source_grad = jnp.zeros((slots,), f32).at[:SUMS].set(sums)
     return intensity, mask_grad, source_grad
 
 

time: 33.6 us -> 32.3 us (0.961)
  waiting for transfers between devices: 9.41 us -> 7.67 us
    ppermute x9, waiting for transfers between devices: 9.41 us -> 7.67 us  [exchange(): lax.ppermute(value, axis, [(i, i ^ step) for i in range(lax.axis_size(axi...]
    pallas_call x1, Pallas kernels: 3.27 us -> 3.61 us  [shards(): pl.pallas_call(functools.partial(image_kernel, book, len(parcels), len(ta...]
  transfers between devices with their start and end apart: 9 -> 9, of which waited for: 6 -> 5; matrix products, arithmetic and copies ran while one was open for 0% -> 0% of each run, Pallas kernels for 14% -> 14%
where the time goes in v4:
time: 32.3 us; the launch traced here: 32.1 us
  starting transfers between devices  12.4 us (38%)
  Pallas kernels  10.1 us (31%)
  waiting for transfers between devices  7.67 us (24%)
  between operations  1.33 us (4%)
  local copies, waits for them, and re-layouts  0.52 us (2%)
    ppermute x9, starting transfers between devices, exchange(): lax.ppermute(value, axis, [(i, i ^ step) for i in range(lax.axis_size(axi...  12.4 us
    ppermute x9, waiting for transfers between devices, exchange(): lax.ppermute(value, axis, [(i, i ^ step) for i in range(lax.axis_size(axi...  7.67 us
    pallas_call x1, Pallas kernels, shards(): pl.pallas_call(functools.partial(image_kernel, book, len(parcels), len(ta...  3.61 us
    pallas_call x1, Pallas kernels, shards(): pl.pallas_call(functools.partial(gradient_kernel, book, len(folds), len(p...  2.9 us
    pallas_call x1, Pallas kernels, shards(): pl.pallas_call(spectrum_kernel, in_specs=[HBM] * 5 + [SMEM] + [HBM] * 3,...  1.88 us
    pallas_call x1, Pallas kernels, shards(): pl.pallas_call(functools.partial(stage_kernel, book), in_specs=[HBM] * 2,...  1.74 us
  transfers between devices with their start and end apart: 9, of which 5 were waited for; matrix products, arithmetic and copies ran while one was open for 0% of the time, Pallas kernels for 14%

profile of v4, /device:TPU:0, one launch (start us, length us, event | category | flops | bytes accessed | tf_op | source)
XLA Modules:
  0.0 32.1 jit_solution(4512593829342482791)
XLA Ops:
  1.3 1.9 %spectrum.1 = (f32[48,128]{1,0:T(8,128)S(1)}, bf16[112,128]{1,0:T(8,128)(2,1)S(1)}, f32[8,128]{1,0:T(8,128)S(1)}) custom-call(f32[1,128,1024]{2,1,0:T(8,128)} %mask_ref.1, bf16[128,2048]{1,0:T(8,128)(2,1)} %pupil_ref.1, bf16[128]{0:T(256)(128)(2,1)} %weight_ref.1, s32[128]{0:T(128)} %cell_ref.1, s32[4]{0:T(128)} %active_ref.1, s32[1]{0:T(128)S(6)} %copy.14.class_ref, ...), custom_call_target="tpu_custom_call" | custom-call | tf_op jit(solution)/shard_map/spectrum/pallas_call | solution.py:559
  3.2 0.5 %collective-permute-start = (f32[48,128]{1,0:T(8,128)S(1)}, f32[48,128]{1,0:T(8,128)S(1)}, u32[]{:S(2)}, u32[]{:S(2)}) collective-permute-start(f32[48,128]{1,0:T(8,128)S(1)} %get-tuple-element.35.part_ref), channel_id=1, source_target_pairs={{0,1},{1,0},{2,3},{3,2},{4,5},{5,4},{6,7},{7,6},{8,9},{9,8},{10,11... | collective-permute-start | bytes 73736 | tf_op jit(solution)/shard_map/ppermute | solution.py:535
  3.7 0.8 %collective-permute-done.refs_0_ = f32[48,128]{1,0:T(8,128)S(1)} collective-permute-done((f32[48,128]{1,0:T(8,128)S(1)}, f32[48,128]{1,0:T(8,128)S(1)}, u32[]{:S(2)}, u32[]{:S(2)}) %collective-permute-start) | collective-permute-done | bytes 24608 | tf_op jit(solution)/shard_map/ppermute | solution.py:535
  4.5 0.3 %collective-permute-start.4 = (f32[128,1024]{1,0:T(8,128)}, f32[128,1024]{1,0:T(8,128)S(1)}, u32[]{:S(2)}, u32[]{:S(2)}) collective-permute-start(f32[128,1024]{1,0:T(8,128)} %bitcast.1), channel_id=1, source_target_pairs={{0,1},{1,0},{2,3},{3,2},{4,5},{5,4},{6,7},{7,6},{8,9},{9,8},{10,11... | collective-permute-start | bytes 1572872 | tf_op jit(solution)/shard_map/ppermute | solution.py:535
  4.9 4.8 %collective-permute-start.3 = (bf16[208,128]{1,0:T(8,128)(2,1)S(1)}, bf16[208,128]{1,0:T(8,128)(2,1)S(1)}, u32[]{:S(2)}, u32[]{:S(2)}) collective-permute-start(bf16[208,128]{1,0:T(8,128)(2,1)S(1)} %pack.1.refs_0_.refs_4_), channel_id=1, source_target_pairs={{0,12},{4,8},{8,4},{12,0},{1,13},{5,9},{9,5},{13,1},{2,14},{6,10},... | collective-permute-start | bytes 159752 | tf_op jit(solution)/shard_map/ppermute | solution.py:535
  9.7 0.0 collective-permute-start.2
  9.7 0.6 %collective-permute-start.1 = (bf16[208,128]{1,0:T(8,128)(2,1)S(1)}, bf16[208,128]{1,0:T(8,128)(2,1)S(1)}, u32[]{:S(2)}, u32[]{:S(2)}) collective-permute-start(bf16[208,128]{1,0:T(8,128)(2,1)S(1)} %pack.1.refs_0_.refs_4_), channel_id=1, source_target_pairs={{0,4},{4,0},{8,12},{12,8},{1,5},{5,1},{9,13},{13,9},{2,6},{6,2},{1... | collective-permute-start | bytes 159752 | tf_op jit(solution)/shard_map/ppermute | solution.py:535
  10.4 1.7 %stage.1 = (f32[128,1024]{1,0:T(8,128)S(1)}, bf16[640,128]{1,0:T(8,128)(2,1)S(1)}, bf16[3072,128]{1,0:T(8,128)(2,1)S(1)}, bf16[896,128]{1,0:T(8,128)(2,1)S(1)}, ...) custom-call(f32[1,128,1024]{2,1,0:T(8,128)} %target_ref, ...), custom_call_target="tpu_custom_call" | custom-call | tf_op jit(solution)/shard_map/stage/pallas_call | solution.py:608
  12.1 0.1 collective-permute-done.3.refs_3_.refs_7_
  12.2 2.8 %collective-permute-done.2.refs_2_.refs_6_ = bf16[208,128]{1,0:T(8,128)(2,1)S(1)} collective-permute-done((bf16[208,128]{1,0:T(8,128)(2,1)S(1)}, bf16[208,128]{1,0:T(8,128)(2,1)S(1)}, u32[]{:S(2)}, u32[]{:S(2)}) %collective-permute-start.2) | collective-permute-done | bytes 53280 | tf_op jit(solution)/shard_map/ppermute | solution.py:535
  15.0 0.0 collective-permute-done.1.refs_1_.refs_5_
  15.0 0.0 collective-permute-done.4.refs_5_
  15.0 3.6 %image.1 = (f32[1,128,1024]{2,1,0:T(8,128)}, f32[24,64,128]{2,1,0:T(8,128)S(1)}, f32[40,128]{1,0:T(8,128)S(1)}, f32[40,128]{1,0:T(8,128)S(1)}, f32[40,128]{1,0:T(8,128)S(1)}, /*index=5*/f32[40,128]{1,0:T(8,128)S(1)}) custom-call(bf16[208,128]{1,0:T(8,128)(2,1)S(1)} %pack.1.refs_0_.refs_4_, bf16[208,128]{1,0:T(8,128)(2,1)S(1)} %collective-permute-done.1.refs_1_.refs_5_, ...), custom_call_target="tpu_custom_call" | custom-call | tf_op jit(solution)/shard_map/image/pallas_call | solution.py:627
  18.6 1.2 %collective-permute-start.5 = (f32[40,128]{1,0:T(8,128)S(1)}, f32[40,128]{1,0:T(8,128)S(1)}, u32[]{:S(2)}, u32[]{:S(2)}) collective-permute-start(f32[40,128]{1,0:T(8,128)S(1)} %get-tuple-element.48), channel_id=1, source_target_pairs={{0,4},{4,0},{8,12},{12,8},{1,5},{5,1},{9,13},{13,9},{2,6},{6,2},{1... | collective-permute-start | bytes 61448 | tf_op jit(solution)/shard_map/ppermute | solution.py:535
  19.8 1.6 %collective-permute-start.6 = (f32[40,128]{1,0:T(8,128)S(1)}, f32[40,128]{1,0:T(8,128)S(1)}, u32[]{:S(2)}, u32[]{:S(2)}) collective-permute-start(f32[40,128]{1,0:T(8,128)S(1)} %get-tuple-element.49), channel_id=1, source_target_pairs={{0,8},{4,12},{8,0},{12,4},{1,9},{5,13},{9,1},{13,5},{2,10},{6,14},... | collective-permute-start | bytes 61448 | tf_op jit(solution)/shard_map/ppermute | solution.py:535
  21.4 1.7 %collective-permute-start.7 = (f32[40,128]{1,0:T(8,128)S(1)}, f32[40,128]{1,0:T(8,128)S(1)}, u32[]{:S(2)}, u32[]{:S(2)}) collective-permute-start(f32[40,128]{1,0:T(8,128)S(1)} %get-tuple-element.50), channel_id=1, source_target_pairs={{0,12},{4,8},{8,4},{12,0},{1,13},{5,9},{9,5},{13,1},{2,14},{6,10},... | collective-permute-start | bytes 61448 | tf_op jit(solution)/shard_map/ppermute | solution.py:535
  23.1 0.0 collective-permute-done.5.refs_1_
  23.1 1.4 %collective-permute-done.6.refs_2_ = f32[40,128]{1,0:T(8,128)S(1)} collective-permute-done((f32[40,128]{1,0:T(8,128)S(1)}, f32[40,128]{1,0:T(8,128)S(1)}, u32[]{:S(2)}, u32[]{:S(2)}) %collective-permute-start.6) | collective-permute-done | bytes 20512 | tf_op jit(solution)/shard_map/ppermute | solution.py:535
  24.5 2.5 %collective-permute-done.7.refs_3_ = f32[40,128]{1,0:T(8,128)S(1)} collective-permute-done((f32[40,128]{1,0:T(8,128)S(1)}, f32[40,128]{1,0:T(8,128)S(1)}, u32[]{:S(2)}, u32[]{:S(2)}) %collective-permute-start.7) | collective-permute-done | bytes 20512 | tf_op jit(solution)/shard_map/ppermute | solution.py:535
  27.0 1.6 %collective-permute-start.8 = (f32[8,128]{1,0:T(8,128)S(1)}, f32[8,128]{1,0:T(8,128)S(1)}, u32[]{:S(2)}, u32[]{:S(2)}) collective-permute-start(f32[8,128]{1,0:T(8,128)S(1)} %slice_add_fusion), channel_id=1, source_target_pairs={{0,2},{2,0},{1,3},{3,1},{4,6},{6,4},{5,7},{7,5},{8,10},{10,8},{9,1... | collective-permute-start | bytes 12296 | tf_op jit(solution)/shard_map/ppermute | solution.py:535
  28.6 2.9 %gradient.1 = f32[1,128,1024]{2,1,0:T(8,128)} custom-call(f32[40,128]{1,0:T(8,128)S(1)} %get-tuple-element.47.refs_0_, f32[40,128]{1,0:T(8,128)S(1)} %collective-permute-done.5.refs_1_, f32[40,128]{1,0:T(8,128)S(1)} %collective-permute-done.6.refs_2_, f32[40,128]{1,0:T(8,128)S(1)} %collective-permute-done.7.refs_3_, ...), custom_call_target="tpu_custom_call" | custom-call | tf_op jit(solution)/shard_map/gradient/pallas_call | solution.py:657
  31.5 0.0 collective-permute-done.8
  31.5 0.1 add_reduce_fusion
  31.6 0.5 %scatter.4 = f32[128]{0:T(128)} pad(f32[8]{0:T(128)S(1)} %broadcast_multiply_fusion, f32[]{:T(128)} %constant.32.clone.1), padding=0_120 | pad | bytes 548 | tf_op jit(solution)/shard_map/scatter | solution.py:672
  (3 shorter events, 0.0 us)
Async XLA Ops:
  3.2 1.4 %collective-permute-start = (f32[48,128]{1,0:T(8,128)S(1)}, f32[48,128]{1,0:T(8,128)S(1)}, u32[]{:S(2)}, u32[]{:S(2)}) collective-permute-start(f32[48,128]{1,0:T(8,128)S(1)} %get-tuple-element.35.part_ref), channel_id=1, source_target_pairs={{0,1},{1,0},{2,3},{3,2},{4,5},{5,4},{6,7},{7,6},{8,9},{9,8},{10,11... | collective-permute-start | bytes 73736 | tf_op jit(solution)/shard_map/ppermute | solution.py:535
  4.5 10.5 %collective-permute-start.4 = (f32[128,1024]{1,0:T(8,128)}, f32[128,1024]{1,0:T(8,128)S(1)}, u32[]{:S(2)}, u32[]{:S(2)}) collective-permute-start(f32[128,1024]{1,0:T(8,128)} %bitcast.1), channel_id=1, source_target_pairs={{0,1},{1,0},{2,3},{3,2},{4,5},{5,4},{6,7},{7,6},{8,9},{9,8},{10,11... | collective-permute-start | bytes 1572872 | tf_op jit(solution)/shard_map/ppermute | solution.py:535
  4.9 7.3 %collective-permute-start.3 = (bf16[208,128]{1,0:T(8,128)(2,1)S(1)}, bf16[208,128]{1,0:T(8,128)(2,1)S(1)}, u32[]{:S(2)}, u32[]{:S(2)}) collective-permute-start(bf16[208,128]{1,0:T(8,128)(2,1)S(1)} %pack.1.refs_0_.refs_4_), channel_id=1, source_target_pairs={{0,12},{4,8},{8,4},{12,0},{1,13},{5,9},{9,5},{13,1},{2,14},{6,10},... | collective-permute-start | bytes 159752 | tf_op jit(solution)/shard_map/ppermute | solution.py:535
  9.7 5.3 %collective-permute-start.2 = (bf16[208,128]{1,0:T(8,128)(2,1)S(1)}, bf16[208,128]{1,0:T(8,128)(2,1)S(1)}, u32[]{:S(2)}, u32[]{:S(2)}) collective-permute-start(bf16[208,128]{1,0:T(8,128)(2,1)S(1)} %pack.1.refs_0_.refs_4_), channel_id=1, source_target_pairs={{0,8},{4,12},{8,0},{12,4},{1,9},{5,13},{9,1},{13,5},{2,10},{6,14},... | collective-permute-start | bytes 159752 | tf_op jit(solution)/shard_map/ppermute | solution.py:535
  9.7 5.3 %collective-permute-start.1 = (bf16[208,128]{1,0:T(8,128)(2,1)S(1)}, bf16[208,128]{1,0:T(8,128)(2,1)S(1)}, u32[]{:S(2)}, u32[]{:S(2)}) collective-permute-start(bf16[208,128]{1,0:T(8,128)(2,1)S(1)} %pack.1.refs_0_.refs_4_), channel_id=1, source_target_pairs={{0,4},{4,0},{8,12},{12,8},{1,5},{5,1},{9,13},{13,9},{2,6},{6,2},{1... | collective-permute-start | bytes 159752 | tf_op jit(solution)/shard_map/ppermute | solution.py:535
  18.6 4.5 %collective-permute-start.5 = (f32[40,128]{1,0:T(8,128)S(1)}, f32[40,128]{1,0:T(8,128)S(1)}, u32[]{:S(2)}, u32[]{:S(2)}) collective-permute-start(f32[40,128]{1,0:T(8,128)S(1)} %get-tuple-element.48), channel_id=1, source_target_pairs={{0,4},{4,0},{8,12},{12,8},{1,5},{5,1},{9,13},{13,9},{2,6},{6,2},{1... | collective-permute-start | bytes 61448 | tf_op jit(solution)/shard_map/ppermute | solution.py:535
  19.8 4.7 %collective-permute-start.6 = (f32[40,128]{1,0:T(8,128)S(1)}, f32[40,128]{1,0:T(8,128)S(1)}, u32[]{:S(2)}, u32[]{:S(2)}) collective-permute-start(f32[40,128]{1,0:T(8,128)S(1)} %get-tuple-element.49), channel_id=1, source_target_pairs={{0,8},{4,12},{8,0},{12,4},{1,9},{5,13},{9,1},{13,5},{2,10},{6,14},... | collective-permute-start | bytes 61448 | tf_op jit(solution)/shard_map/ppermute | solution.py:535
  21.4 5.6 %collective-permute-start.7 = (f32[40,128]{1,0:T(8,128)S(1)}, f32[40,128]{1,0:T(8,128)S(1)}, u32[]{:S(2)}, u32[]{:S(2)}) collective-permute-start(f32[40,128]{1,0:T(8,128)S(1)} %get-tuple-element.50), channel_id=1, source_target_pairs={{0,12},{4,8},{8,4},{12,0},{1,13},{5,9},{9,5},{13,1},{2,14},{6,10},... | collective-permute-start | bytes 61448 | tf_op jit(solution)/shard_map/ppermute | solution.py:535
  27.0 4.5 %collective-permute-start.8 = (f32[8,128]{1,0:T(8,128)S(1)}, f32[8,128]{1,0:T(8,128)S(1)}, u32[]{:S(2)}, u32[]{:S(2)}) collective-permute-start(f32[8,128]{1,0:T(8,128)S(1)} %slice_add_fusion), channel_id=1, source_target_pairs={{0,2},{2,0},{1,3},{3,1},{4,6},{6,4},{5,7},{7,5},{8,10},{10,8},{9,1... | collective-permute-start | bytes 12296 | tf_op jit(solution)/shard_map/ppermute | solution.py:535

commit v5 on v4

--- a/solution.py
+++ b/solution.py
@@ -19,7 +19,7 @@
 M = 64
 LANES = 128
 PAIRS = MOST // 2
-AT_PUPILS = 2 * W
+AT_PUPILS = W
 AT_TAIL = AT_PUPILS + PAIRS * K
 ROWS = AT_TAIL + 16
 TAIL_PAIR, TAIL_CELL = 8, 12
@@ -75,10 +75,11 @@
             out[imag : imag + K, at : at + 2 * M] = np.concatenate([-sin, cos], 1)
         return out
 
-    high, low = split_np(pair_table(rounded_cos, rounded_sin))
+    lift = pair_table(rounded_cos, rounded_sin)
+    turned = pair_table(-rounded_sin, rounded_cos)
+    high, low = split_np(np.concatenate([lift, turned], 1))
     lift_cols = np.concatenate([high, low], 0)
-    high, low = split_np(np.concatenate([rounded_cos.T, rounded_sin.T], 0) / K)
-    lift_rows = np.concatenate([high, low, high], 1)
+    lift_rows = np.concatenate(split_np(rounded_cos.T / K) + split_np(rounded_sin.T / K), 1)
     orders = np.arange(-(M // 2 - 1), M // 2)
     places = pixels[:, None] * (M / period) - np.arange(M)[None, :]
     inter = np.cos(2.0 * np.pi / M * places[:, :, None] * orders).sum(-1) / M
@@ -90,8 +91,10 @@
     low_t = low.reshape(blocks, span, M).transpose(0, 2, 1)
     fold_rows = np.concatenate([high_t, low_t, high_t], 2)
     high, low = split_np(np.concatenate([rounded_cos, rounded_sin], 0))
-    drop_rows = np.concatenate([high, low, high], 1)
-    high, low = split_np(pair_table(coarse_cos, coarse_sin).T)
+    drop_rows = np.concatenate([high, low], 1)
+    drop = pair_table(coarse_cos, coarse_sin).T
+    drop = np.concatenate([drop, drop[:, M:], -drop[:, :M]], 1)
+    high, low = split_np(drop)
     drop_cols = np.concatenate([high, low, high], 0)
     rows = np.concatenate(
         [
@@ -283,8 +286,8 @@
     for ref in other_refs:
         part = part + ref[...]
     high, low = split(part)
-    out_ref[:W] = high
-    out_ref[W : 2 * W] = low
+    rest = pltpu.roll(low.astype(f32), K, 1)
+    out_ref[:W] = jnp.where(lane_of(part.shape) % M < W, high.astype(f32), rest).astype(bf16)
     out_ref[AT_PUPILS:] = sent_ref[...]
 
 
@@ -358,7 +361,9 @@
 
     def gather(total, items):
         for ref, place in items:
-            total = total + (ref[:W].astype(f32) + ref[W : 2 * W].astype(f32))
+            value = ref[:W].astype(f32)
+            rest = jnp.where(lane_of(value.shape) % M < W, 0.0, value)
+            total = total + (value + pltpu.roll(rest, LANES - K, 1))
         return total
 
     spectrum[...] = over_owners(sent_refs, gather, jnp.zeros((W, LANES), f32))
@@ -366,7 +371,6 @@
     lift_cols, lift_rows = book.read(lift, "lift_cols"), book.read(lift, "lift_rows")
     even = slot_lanes(K)
     turn_low = signs(K, -1.0, 1.0)
-    turn = signs(M, -1.0, 1.0)
 
     def forward(total, items):
         waves = []
@@ -380,17 +384,17 @@
                 window = jnp.where(even, left, right)
                 waves.append((real * window + imag * (turn_low * swap(window))).astype(bf16))
         wave = jnp.concatenate(waves, 0)
-        high, low = split(dot(jnp.concatenate([wave, wave], 1), lift_cols))
+        wave = dot(jnp.concatenate([wave, wave], 1), lift_cols).astype(bf16)
         number = 0
         for ref, place in items:
             weights = ref[pl.ds(AT_TAIL, 16), :].astype(f32)
             for pair in range(PAIRS):
                 here = slice(number * K, (number + 1) * K)
                 number += 1
-                raw = dot(lift_rows, jnp.concatenate([high[here], high[here], low[here]], 0))
+                own, turned = wave[here, : 2 * LANES], wave[here, 2 * LANES :]
+                raw = dot(lift_rows, jnp.concatenate([own, own, turned, turned], 0))
                 for slot in range(2):
-                    mine = raw[:, slot * LANES : (slot + 1) * LANES]
-                    field = mine[:M] + turn * swap(mine[M:])
+                    field = raw[:, slot * LANES : (slot + 1) * LANES]
                     fields[place * MOST + 2 * pair + slot] = field
                     at = 2 * pair + slot
                     total = total + weights[at : at + 1] * (field * field)
@@ -402,19 +406,26 @@
     fine_cols, fold_cols = book.read(fine, "fine_cols"), book.read(fine, "fold_cols")
     threshold = threshold_ref[:1, :1]
     grid = jnp.zeros((M, LANES), f32)
-    for number, (target, rows_ref) in enumerate(zip(targets, rows_refs)):
-        high, low = split(dot(book.read(rows_ref, "fine_rows"), coarse))
-        intensity = dot(jnp.concatenate([high, low], 1), fine_cols)
-        if number == 0:
-            intensity_out[...] = intensity
-            put = pltpu.make_async_copy(intensity_out, intensity_ref.at[0], sems.at[1])
-            put.start()
+    fine_rows = [book.read(rows_ref, "fine_rows") for rows_ref in rows_refs]
+    high, low = split(dot(jnp.concatenate(fine_rows, 0), coarse))
+    intensities = dot(jnp.concatenate([high, low], 1), fine_cols)
+    span = intensity_out.shape[0]
+    intensity_out[...] = intensities[:span]
+    put = pltpu.make_async_copy(intensity_out, intensity_ref.at[0], sems.at[1])
+    put.start()
+    slopes = []
+    for number, target in enumerate(targets):
+        intensity = intensities[number * span : (number + 1) * span]
         resist = 1.0 / (1.0 + jnp.exp(-STEEP * (intensity - threshold)))
-        slope = (2.0 * STEEP * (resist - target[...]) * resist * (1.0 - resist)).astype(bf16)
-        folded = dot(slope, fold_cols)
-        high, low = split(folded + swap(folded))
+        slope = 2.0 * STEEP * (resist - target[...]) * resist * (1.0 - resist)
+        slopes.append(slope.astype(bf16))
+    folded = dot(jnp.concatenate(slopes, 0), fold_cols)
+    high, low = split(folded + swap(folded))
+    for number, rows_ref in enumerate(rows_refs):
+        here = slice(number * span, (number + 1) * span)
         grid = grid + dot(
-            book.read(rows_ref, "fold_rows"), jnp.concatenate([high, high, low], 0)
+            book.read(rows_ref, "fold_rows"),
+            jnp.concatenate([high[here], high[here], low[here]], 0),
         )
     lane = lane_of((M // 2, LANES))
     packed = jnp.where(lane < M, grid[: M // 2], grid[M // 2 :])
@@ -470,8 +481,8 @@
         for ref, place in items:
             for pair in range(PAIRS):
                 scaled = [grid * fields[place * MOST + 2 * pair + slot] for slot in range(2)]
-                high, low = split(jnp.concatenate(scaled, 1))
-                raw = dot(drop_rows, jnp.concatenate([high, high, low], 0))
+                pull = jnp.concatenate(scaled, 1).astype(bf16)
+                raw = dot(drop_rows, jnp.concatenate([pull, pull], 0))
                 wave = []
                 for slot in range(2):
                     mine = raw[:, slot * LANES : (slot + 1) * LANES]
@@ -486,7 +497,7 @@
                 mine = back[number * K : (number + 1) * K]
                 number += 1
                 real, imag = pair_parts(ref, pair)
-                product = real * mine + imag * (turn * swap(mine))
+                product = real * mine[:, :LANES] + imag * mine[:, LANES:]
                 product = weights[TAIL_PAIR + pair : TAIL_PAIR + pair + 1] * product
                 for slot in range(2):
                     row, col = window_of(codes, place, 2 * pair + slot)

time: 32.3 us -> 31 us (0.960)
  waiting for transfers between devices: 7.67 us -> 6.9 us
  Pallas kernels: 10.1 us -> 9.59 us
    ppermute x9, waiting for transfers between devices: 7.67 us -> 6.9 us  [exchange(): lax.ppermute(value, axis, [(i, i ^ step) for i in range(lax.axis_size(axi...]
    pallas_call x1, Pallas kernels: 3.61 us -> 3.06 us  [shards(): pl.pallas_call(functools.partial(image_kernel, book, len(parcels), len(ta...]
  transfers between devices with their start and end apart: 9 -> 9, of which waited for: 5 -> 4; matrix products, arithmetic and copies ran while one was open for 0% -> 0% of each run, Pallas kernels for 14% -> 15%
where the time goes in v5:
time: 31 us; the launch traced here: 30.8 us
  starting transfers between devices  12.4 us (40%)
  Pallas kernels  9.59 us (31%)
  waiting for transfers between devices  6.9 us (22%)
  between operations  1.34 us (4%)
  local copies, waits for them, and re-layouts  0.52 us (2%)
    ppermute x9, starting transfers between devices, exchange(): lax.ppermute(value, axis, [(i, i ^ step) for i in range(lax.axis_size(axi...  12.4 us
    ppermute x9, waiting for transfers between devices, exchange(): lax.ppermute(value, axis, [(i, i ^ step) for i in range(lax.axis_size(axi...  6.9 us
    pallas_call x1, Pallas kernels, shards(): pl.pallas_call(functools.partial(image_kernel, book, len(parcels), len(ta...  3.06 us
    pallas_call x1, Pallas kernels, shards(): pl.pallas_call(functools.partial(gradient_kernel, book, len(folds), len(p...  2.78 us
    pallas_call x1, Pallas kernels, shards(): pl.pallas_call(spectrum_kernel, in_specs=[HBM] * 5 + [SMEM] + [HBM] * 3,...  1.88 us
    pallas_call x1, Pallas kernels, shards(): pl.pallas_call(functools.partial(stage_kernel, book), in_specs=[HBM] * 2,...  1.79 us
  transfers between devices with their start and end apart: 9, of which 4 were waited for; matrix products, arithmetic and copies ran while one was open for 0% of the time, Pallas kernels for 15%

profile of v5, /device:TPU:0, one launch (start us, length us, event | category | flops | bytes accessed | tf_op | source)
XLA Modules:
  0.0 30.8 jit_solution(15615543220904402360)
XLA Ops:
  1.3 1.9 %spectrum.1 = (f32[48,128]{1,0:T(8,128)S(1)}, bf16[112,128]{1,0:T(8,128)(2,1)S(1)}, f32[8,128]{1,0:T(8,128)S(1)}) custom-call(f32[1,128,1024]{2,1,0:T(8,128)} %mask_ref.1, bf16[128,2048]{1,0:T(8,128)(2,1)} %pupil_ref.1, bf16[128]{0:T(256)(128)(2,1)} %weight_ref.1, s32[128]{0:T(128)} %cell_ref.1, s32[4]{0:T(128)} %active_ref.1, s32[1]{0:T(128)S(6)} %copy.14.class_ref, ...), custom_call_target="tpu_custom_call" | custom-call | tf_op jit(solution)/shard_map/spectrum/pallas_call | solution.py:570
  3.2 0.5 %collective-permute-start = (f32[48,128]{1,0:T(8,128)S(1)}, f32[48,128]{1,0:T(8,128)S(1)}, u32[]{:S(2)}, u32[]{:S(2)}) collective-permute-start(f32[48,128]{1,0:T(8,128)S(1)} %get-tuple-element.35.part_ref), channel_id=1, source_target_pairs={{0,1},{1,0},{2,3},{3,2},{4,5},{5,4},{6,7},{7,6},{8,9},{9,8},{10,11... | collective-permute-start | bytes 73736 | tf_op jit(solution)/shard_map/ppermute | solution.py:546
  3.7 0.8 %collective-permute-done.refs_0_ = f32[48,128]{1,0:T(8,128)S(1)} collective-permute-done((f32[48,128]{1,0:T(8,128)S(1)}, f32[48,128]{1,0:T(8,128)S(1)}, u32[]{:S(2)}, u32[]{:S(2)}) %collective-permute-start) | collective-permute-done | bytes 24608 | tf_op jit(solution)/shard_map/ppermute | solution.py:546
  4.5 0.3 %collective-permute-start.4 = (f32[128,1024]{1,0:T(8,128)}, f32[128,1024]{1,0:T(8,128)S(1)}, u32[]{:S(2)}, u32[]{:S(2)}) collective-permute-start(f32[128,1024]{1,0:T(8,128)} %bitcast.1), channel_id=1, source_target_pairs={{0,1},{1,0},{2,3},{3,2},{4,5},{5,4},{6,7},{7,6},{8,9},{9,8},{10,11... | collective-permute-start | bytes 1572872 | tf_op jit(solution)/shard_map/ppermute | solution.py:546
  4.9 0.1 pack.1.refs_0_.refs_4_
  5.0 4.8 %collective-permute-start.3 = (bf16[160,128]{1,0:T(8,128)(2,1)S(1)}, bf16[160,128]{1,0:T(8,128)(2,1)S(1)}, u32[]{:S(2)}, u32[]{:S(2)}) collective-permute-start(bf16[160,128]{1,0:T(8,128)(2,1)S(1)} %pack.1.refs_0_.refs_4_), channel_id=1, source_target_pairs={{0,12},{4,8},{8,4},{12,0},{1,13},{5,9},{9,5},{13,1},{2,14},{6,10},... | collective-permute-start | bytes 122888 | tf_op jit(solution)/shard_map/ppermute | solution.py:546
  9.7 0.0 collective-permute-start.2
  9.7 0.6 %collective-permute-start.1 = (bf16[160,128]{1,0:T(8,128)(2,1)S(1)}, bf16[160,128]{1,0:T(8,128)(2,1)S(1)}, u32[]{:S(2)}, u32[]{:S(2)}) collective-permute-start(bf16[160,128]{1,0:T(8,128)(2,1)S(1)} %pack.1.refs_0_.refs_4_), channel_id=1, source_target_pairs={{0,4},{4,0},{8,12},{12,8},{1,5},{5,1},{9,13},{13,9},{2,6},{6,2},{1... | collective-permute-start | bytes 122888 | tf_op jit(solution)/shard_map/ppermute | solution.py:546
  10.4 1.8 %stage.1 = (f32[128,1024]{1,0:T(8,128)S(1)}, bf16[1088,128]{1,0:T(8,128)(2,1)S(1)}, bf16[3072,128]{1,0:T(8,128)(2,1)S(1)}, bf16[1600,128]{1,0:T(8,128)(2,1)S(1)}...) custom-call(f32[1,128,1024]{2,1,0:T(8,128)} %target_ref, ...), custom_call_target="tpu_custom_call" | custom-call | tf_op jit(solution)/shard_map/stage/pallas_call | solution.py:619
  12.2 0.0 collective-permute-done.3.refs_3_.refs_7_
  12.2 2.5 %collective-permute-done.2.refs_2_.refs_6_ = bf16[160,128]{1,0:T(8,128)(2,1)S(1)} collective-permute-done((bf16[160,128]{1,0:T(8,128)(2,1)S(1)}, bf16[160,128]{1,0:T(8,128)(2,1)S(1)}, u32[]{:S(2)}, u32[]{:S(2)}) %collective-permute-start.2) | collective-permute-done | bytes 40992 | tf_op jit(solution)/shard_map/ppermute | solution.py:546
  14.6 0.0 collective-permute-done.1.refs_1_.refs_5_
  14.6 0.0 collective-permute-done.4.refs_5_
  14.6 3.1 %image.1 = (f32[1,128,1024]{2,1,0:T(8,128)}, f32[24,64,128]{2,1,0:T(8,128)S(1)}, f32[40,128]{1,0:T(8,128)S(1)}, f32[40,128]{1,0:T(8,128)S(1)}, f32[40,128]{1,0:T(8,128)S(1)}, /*index=5*/f32[40,128]{1,0:T(8,128)S(1)}) custom-call(bf16[160,128]{1,0:T(8,128)(2,1)S(1)} %pack.1.refs_0_.refs_4_, bf16[160,128]{1,0:T(8,128)(2,1)S(1)} %collective-permute-done.1.refs_1_.refs_5_, ...), custom_call_target="tpu_custom_call" | custom-call | tf_op jit(solution)/shard_map/image/pallas_call | solution.py:638
  17.7 0.8 %collective-permute-start.5 = (f32[40,128]{1,0:T(8,128)S(1)}, f32[40,128]{1,0:T(8,128)S(1)}, u32[]{:S(2)}, u32[]{:S(2)}) collective-permute-start(f32[40,128]{1,0:T(8,128)S(1)} %get-tuple-element.48), channel_id=1, source_target_pairs={{0,4},{4,0},{8,12},{12,8},{1,5},{5,1},{9,13},{13,9},{2,6},{6,2},{1... | collective-permute-start | bytes 61448 | tf_op jit(solution)/shard_map/ppermute | solution.py:546
  18.5 1.7 %collective-permute-start.6 = (f32[40,128]{1,0:T(8,128)S(1)}, f32[40,128]{1,0:T(8,128)S(1)}, u32[]{:S(2)}, u32[]{:S(2)}) collective-permute-start(f32[40,128]{1,0:T(8,128)S(1)} %get-tuple-element.49), channel_id=1, source_target_pairs={{0,8},{4,12},{8,0},{12,4},{1,9},{5,13},{9,1},{13,5},{2,10},{6,14},... | collective-permute-start | bytes 61448 | tf_op jit(solution)/shard_map/ppermute | solution.py:546
  20.2 2.0 %collective-permute-start.7 = (f32[40,128]{1,0:T(8,128)S(1)}, f32[40,128]{1,0:T(8,128)S(1)}, u32[]{:S(2)}, u32[]{:S(2)}) collective-permute-start(f32[40,128]{1,0:T(8,128)S(1)} %get-tuple-element.50), channel_id=1, source_target_pairs={{0,12},{4,8},{8,4},{12,0},{1,13},{5,9},{9,5},{13,1},{2,14},{6,10},... | collective-permute-start | bytes 61448 | tf_op jit(solution)/shard_map/ppermute | solution.py:546
  22.2 0.0 collective-permute-done.5.refs_1_
  22.2 1.0 %collective-permute-done.6.refs_2_ = f32[40,128]{1,0:T(8,128)S(1)} collective-permute-done((f32[40,128]{1,0:T(8,128)S(1)}, f32[40,128]{1,0:T(8,128)S(1)}, u32[]{:S(2)}, u32[]{:S(2)}) %collective-permute-start.6) | collective-permute-done | bytes 20512 | tf_op jit(solution)/shard_map/ppermute | solution.py:546
  23.2 2.6 %collective-permute-done.7.refs_3_ = f32[40,128]{1,0:T(8,128)S(1)} collective-permute-done((f32[40,128]{1,0:T(8,128)S(1)}, f32[40,128]{1,0:T(8,128)S(1)}, u32[]{:S(2)}, u32[]{:S(2)}) %collective-permute-start.7) | collective-permute-done | bytes 20512 | tf_op jit(solution)/shard_map/ppermute | solution.py:546
  25.8 1.6 %collective-permute-start.8 = (f32[8,128]{1,0:T(8,128)S(1)}, f32[8,128]{1,0:T(8,128)S(1)}, u32[]{:S(2)}, u32[]{:S(2)}) collective-permute-start(f32[8,128]{1,0:T(8,128)S(1)} %slice_add_fusion), channel_id=1, source_target_pairs={{0,2},{2,0},{1,3},{3,1},{4,6},{6,4},{5,7},{7,5},{8,10},{10,8},{9,1... | collective-permute-start | bytes 12296 | tf_op jit(solution)/shard_map/ppermute | solution.py:546
  27.4 2.8 %gradient.1 = f32[1,128,1024]{2,1,0:T(8,128)} custom-call(f32[40,128]{1,0:T(8,128)S(1)} %get-tuple-element.47.refs_0_, f32[40,128]{1,0:T(8,128)S(1)} %collective-permute-done.5.refs_1_, f32[40,128]{1,0:T(8,128)S(1)} %collective-permute-done.6.refs_2_, f32[40,128]{1,0:T(8,128)S(1)} %collective-permute-done.7.refs_3_, ...), custom_call_target="tpu_custom_call" | custom-call | tf_op jit(solution)/shard_map/gradient/pallas_call | solution.py:668
  30.2 0.0 collective-permute-done.8
  30.2 0.1 add_reduce_fusion
  30.3 0.5 %scatter.4 = f32[128]{0:T(128)} pad(f32[8]{0:T(128)S(1)} %broadcast_multiply_fusion, f32[]{:T(128)} %constant.32.clone.1), padding=0_120 | pad | bytes 548 | tf_op jit(solution)/shard_map/scatter | solution.py:683
  (2 shorter events, 0.0 us)
Async XLA Ops:
  3.2 1.4 %collective-permute-start = (f32[48,128]{1,0:T(8,128)S(1)}, f32[48,128]{1,0:T(8,128)S(1)}, u32[]{:S(2)}, u32[]{:S(2)}) collective-permute-start(f32[48,128]{1,0:T(8,128)S(1)} %get-tuple-element.35.part_ref), channel_id=1, source_target_pairs={{0,1},{1,0},{2,3},{3,2},{4,5},{5,4},{6,7},{7,6},{8,9},{9,8},{10,11... | collective-permute-start | bytes 73736 | tf_op jit(solution)/shard_map/ppermute | solution.py:546
  4.5 10.1 %collective-permute-start.4 = (f32[128,1024]{1,0:T(8,128)}, f32[128,1024]{1,0:T(8,128)S(1)}, u32[]{:S(2)}, u32[]{:S(2)}) collective-permute-start(f32[128,1024]{1,0:T(8,128)} %bitcast.1), channel_id=1, source_target_pairs={{0,1},{1,0},{2,3},{3,2},{4,5},{5,4},{6,7},{7,6},{8,9},{9,8},{10,11... | collective-permute-start | bytes 1572872 | tf_op jit(solution)/shard_map/ppermute | solution.py:546
  5.0 7.2 %collective-permute-start.3 = (bf16[160,128]{1,0:T(8,128)(2,1)S(1)}, bf16[160,128]{1,0:T(8,128)(2,1)S(1)}, u32[]{:S(2)}, u32[]{:S(2)}) collective-permute-start(bf16[160,128]{1,0:T(8,128)(2,1)S(1)} %pack.1.refs_0_.refs_4_), channel_id=1, source_target_pairs={{0,12},{4,8},{8,4},{12,0},{1,13},{5,9},{9,5},{13,1},{2,14},{6,10},... | collective-permute-start | bytes 122888 | tf_op jit(solution)/shard_map/ppermute | solution.py:546
  9.7 4.9 %collective-permute-start.2 = (bf16[160,128]{1,0:T(8,128)(2,1)S(1)}, bf16[160,128]{1,0:T(8,128)(2,1)S(1)}, u32[]{:S(2)}, u32[]{:S(2)}) collective-permute-start(bf16[160,128]{1,0:T(8,128)(2,1)S(1)} %pack.1.refs_0_.refs_4_), channel_id=1, source_target_pairs={{0,8},{4,12},{8,0},{12,4},{1,9},{5,13},{9,1},{13,5},{2,10},{6,14},... | collective-permute-start | bytes 122888 | tf_op jit(solution)/shard_map/ppermute | solution.py:546
  9.7 4.9 %collective-permute-start.1 = (bf16[160,128]{1,0:T(8,128)(2,1)S(1)}, bf16[160,128]{1,0:T(8,128)(2,1)S(1)}, u32[]{:S(2)}, u32[]{:S(2)}) collective-permute-start(bf16[160,128]{1,0:T(8,128)(2,1)S(1)} %pack.1.refs_0_.refs_4_), channel_id=1, source_target_pairs={{0,4},{4,0},{8,12},{12,8},{1,5},{5,1},{9,13},{13,9},{2,6},{6,2},{1... | collective-permute-start | bytes 122888 | tf_op jit(solution)/shard_map/ppermute | solution.py:546
  17.7 4.5 %collective-permute-start.5 = (f32[40,128]{1,0:T(8,128)S(1)}, f32[40,128]{1,0:T(8,128)S(1)}, u32[]{:S(2)}, u32[]{:S(2)}) collective-permute-start(f32[40,128]{1,0:T(8,128)S(1)} %get-tuple-element.48), channel_id=1, source_target_pairs={{0,4},{4,0},{8,12},{12,8},{1,5},{5,1},{9,13},{13,9},{2,6},{6,2},{1... | collective-permute-start | bytes 61448 | tf_op jit(solution)/shard_map/ppermute | solution.py:546
  18.5 4.7 %collective-permute-start.6 = (f32[40,128]{1,0:T(8,128)S(1)}, f32[40,128]{1,0:T(8,128)S(1)}, u32[]{:S(2)}, u32[]{:S(2)}) collective-permute-start(f32[40,128]{1,0:T(8,128)S(1)} %get-tuple-element.49), channel_id=1, source_target_pairs={{0,8},{4,12},{8,0},{12,4},{1,9},{5,13},{9,1},{13,5},{2,10},{6,14},... | collective-permute-start | bytes 61448 | tf_op jit(solution)/shard_map/ppermute | solution.py:546
  20.2 5.6 %collective-permute-start.7 = (f32[40,128]{1,0:T(8,128)S(1)}, f32[40,128]{1,0:T(8,128)S(1)}, u32[]{:S(2)}, u32[]{:S(2)}) collective-permute-start(f32[40,128]{1,0:T(8,128)S(1)} %get-tuple-element.50), channel_id=1, source_target_pairs={{0,12},{4,8},{8,4},{12,0},{1,13},{5,9},{9,5},{13,1},{2,14},{6,10},... | collective-permute-start | bytes 61448 | tf_op jit(solution)/shard_map/ppermute | solution.py:546
  25.8 4.4 %collective-permute-start.8 = (f32[8,128]{1,0:T(8,128)S(1)}, f32[8,128]{1,0:T(8,128)S(1)}, u32[]{:S(2)}, u32[]{:S(2)}) collective-permute-start(f32[8,128]{1,0:T(8,128)S(1)} %slice_add_fusion), channel_id=1, source_target_pairs={{0,2},{2,0},{1,3},{3,1},{4,6},{6,4},{5,7},{7,5},{8,10},{10,8},{9,1... | collective-permute-start | bytes 12296 | tf_op jit(solution)/shard_map/ppermute | solution.py:546

commit v6 on v5

--- a/solution.py
+++ b/solution.py
@@ -181,6 +181,10 @@
     return jnp.where(lane_of((rows, LANES)) < M, f32(low), f32(high))
 
 
+def place_is_static(place):
+    return isinstance(place, int)
+
+
 def my_block():
     return lax.axis_index("src") * lax.axis_size("pix") + lax.axis_index("pix")
 
@@ -209,16 +213,16 @@
     sems, lined, paired,
 ):
     (
-        get_active, get_cell, get_pupil, get_weight, get_mask, get_cols, get_rows,
+        get_pupil, get_mask, get_cols, get_active, get_cell, get_weight, get_rows,
         get_thresholds,
     ) = copies(
         sems,
+        (pupil_ref.at[pl.ds(0, 16)], pupil_in),
+        (mask_ref.at[0], mask_in),
+        (cols_ref, cols),
         (active_ref, active_in),
         (cell_ref, cell_in),
-        (pupil_ref.at[pl.ds(0, 16)], pupil_in),
         (weight_ref, weight_in),
-        (mask_ref.at[0], mask_in),
-        (cols_ref, cols),
         (rows_ref.at[my_block()], rows),
         (thresholds_ref, thresholds),
     )
@@ -367,16 +371,20 @@
         return total
 
     spectrum[...] = over_owners(sent_refs, gather, jnp.zeros((W, LANES), f32))
-    get_codes.wait()
+    if len(sent_refs) == 1:
+        get_codes.wait()
     lift_cols, lift_rows = book.read(lift, "lift_cols"), book.read(lift, "lift_rows")
     even = slot_lanes(K)
     turn_low = signs(K, -1.0, 1.0)
 
     def forward(total, items):
         waves = []
+        parts = [pair_parts(ref, pair) for ref, place in items for pair in range(PAIRS)]
+        if len(items) > 1:
+            get_codes.wait()
         for ref, place in items:
             for pair in range(PAIRS):
-                real, imag = pair_parts(ref, pair)
+                real, imag = parts.pop(0)
                 row, col = window_of(codes, place, 2 * pair)
                 left = pltpu.roll(spectrum[pl.ds(row, K), :], lax.rem(LANES - col, LANES), 1)
                 row, col = window_of(codes, place, 2 * pair + 1)
@@ -430,7 +438,7 @@
     lane = lane_of((M // 2, LANES))
     packed = jnp.where(lane < M, grid[: M // 2], grid[M // 2 :])
     for fold_ref in fold_refs:
-        fold_ref[: M // 2] = packed
+        fold_ref[: M // 2] = packed.astype(fold_ref.dtype)
 
     def weigh(none, items):
         for ref, place in items:
@@ -439,7 +447,10 @@
                 field = fields[place * MOST + slot]
                 sums.append(jnp.sum(grid * (field * field), 0, keepdims=True))
             sums = jnp.concatenate(sums + [jnp.zeros((SUMS - MOST, LANES), f32)], 0)
-            if len(fold_refs) > 1:
+            if place_is_static(place) and place > 0:
+                high, low = split(sums)
+                fold_refs[place][M // 2 :] = jnp.concatenate([high, low], 0)
+            elif len(fold_refs) > 1:
                 fold_refs[place][M // 2 :] = sums
             else:
                 start = pl.multiple_of(M // 2 + place * SUMS, SUMS)
@@ -462,7 +473,7 @@
     (get_codes,) = copies(sems, (codes_v, codes))
     packed = fold_refs[0][: M // 2]
     for ref in fold_refs[1:]:
-        packed = packed + ref[: M // 2]
+        packed = packed + ref[: M // 2].astype(f32)
     other = swap(packed)
     low_half = lane_of(packed.shape) < M
     grid = jnp.concatenate(
@@ -642,7 +653,8 @@
         out_shape=[
             jax.ShapeDtypeStruct((1, span, period), f32),
             jax.ShapeDtypeStruct((numbers, M, LANES), f32),
-            *[jax.ShapeDtypeStruct((fold_rows, LANES), f32)] * fold_count,
+            jax.ShapeDtypeStruct((fold_rows, LANES), f32),
+            *[jax.ShapeDtypeStruct((M // 2 + 2 * SUMS, LANES), bf16)] * (fold_count - 1),
         ],
         scratch_shapes=[
             sems((2,)),
@@ -659,7 +671,10 @@
             value if step == 0 else exchange(value, "src", step)
             for step, value in enumerate(folded)
         ]
-        rows = sum(fold[M // 2 :] for fold in folds)
+        rows = folds[0][M // 2 :]
+        for fold in folds[1:]:
+            sums = fold[M // 2 :].astype(f32)
+            rows = rows + (sums[:SUMS] + sums[SUMS:])
     else:
         folds = [lax.psum(folded[0], "src")]
         rows = lax.dynamic_slice_in_dim(folds[0], M // 2 + src * SUMS, SUMS, 0)

time: 31 us -> 30.5 us (0.984)
  Pallas kernels: 9.59 us -> 9.13 us
    pallas_call x1, Pallas kernels: 3.06 us -> 2.62 us  [shards(): pl.pallas_call(functools.partial(image_kernel, book, len(parcels), len(ta...]
where the time goes in v6:
time: 30.5 us; the launch traced here: 30.3 us
  starting transfers between devices  12.4 us (41%)
  Pallas kernels  9.13 us (30%)
  waiting for transfers between devices  6.8 us (22%)
  between operations  1.34 us (4%)
  local copies, waits for them, and re-layouts  0.52 us (2%)
    ppermute x9, starting transfers between devices, exchange(): lax.ppermute(value, axis, [(i, i ^ step) for i in range(lax.axis_size(axi...  12.4 us
    ppermute x9, waiting for transfers between devices, exchange(): lax.ppermute(value, axis, [(i, i ^ step) for i in range(lax.axis_size(axi...  6.8 us
    pallas_call x1, Pallas kernels, shards(): pl.pallas_call(functools.partial(gradient_kernel, book, len(folds), len(p...  2.78 us
    pallas_call x1, Pallas kernels, shards(): pl.pallas_call(functools.partial(image_kernel, book, len(parcels), len(ta...  2.62 us
    pallas_call x1, Pallas kernels, shards(): pl.pallas_call(spectrum_kernel, in_specs=[HBM] * 5 + [SMEM] + [HBM] * 3,...  1.86 us
    pallas_call x1, Pallas kernels, shards(): pl.pallas_call(functools.partial(stage_kernel, book), in_specs=[HBM] * 2,...  1.79 us
  transfers between devices with their start and end apart: 9, of which 4 were waited for; matrix products, arithmetic and copies ran while one was open for 0% of the time, Pallas kernels for 15%

profile of v6, /device:TPU:0, one launch (start us, length us, event | category | flops | bytes accessed | tf_op | source)
XLA Modules:
  0.0 30.3 jit_solution(1052353197783243798)
XLA Ops:
  1.3 1.9 %spectrum.1 = (f32[48,128]{1,0:T(8,128)S(1)}, bf16[112,128]{1,0:T(8,128)(2,1)S(1)}, f32[8,128]{1,0:T(8,128)S(1)}) custom-call(f32[1,128,1024]{2,1,0:T(8,128)} %mask_ref.1, bf16[128,2048]{1,0:T(8,128)(2,1)} %pupil_ref.1, bf16[128]{0:T(256)(128)(2,1)} %weight_ref.1, s32[128]{0:T(128)} %cell_ref.1, s32[4]{0:T(128)} %active_ref.1, s32[1]{0:T(128)S(6)} %copy.14.class_ref, ...), custom_call_target="tpu_custom_call" | custom-call | tf_op jit(solution)/shard_map/spectrum/pallas_call | solution.py:581
  3.1 0.5 %collective-permute-start = (f32[48,128]{1,0:T(8,128)S(1)}, f32[48,128]{1,0:T(8,128)S(1)}, u32[]{:S(2)}, u32[]{:S(2)}) collective-permute-start(f32[48,128]{1,0:T(8,128)S(1)} %get-tuple-element.35.part_ref), channel_id=1, source_target_pairs={{0,1},{1,0},{2,3},{3,2},{4,5},{5,4},{6,7},{7,6},{8,9},{9,8},{10,11... | collective-permute-start | bytes 73736 | tf_op jit(solution)/shard_map/ppermute | solution.py:557
  3.7 0.8 %collective-permute-done.refs_0_ = f32[48,128]{1,0:T(8,128)S(1)} collective-permute-done((f32[48,128]{1,0:T(8,128)S(1)}, f32[48,128]{1,0:T(8,128)S(1)}, u32[]{:S(2)}, u32[]{:S(2)}) %collective-permute-start) | collective-permute-done | bytes 24608 | tf_op jit(solution)/shard_map/ppermute | solution.py:557
  4.5 0.3 %collective-permute-start.4 = (f32[128,1024]{1,0:T(8,128)}, f32[128,1024]{1,0:T(8,128)S(1)}, u32[]{:S(2)}, u32[]{:S(2)}) collective-permute-start(f32[128,1024]{1,0:T(8,128)} %bitcast.1), channel_id=1, source_target_pairs={{0,1},{1,0},{2,3},{3,2},{4,5},{5,4},{6,7},{7,6},{8,9},{9,8},{10,11... | collective-permute-start | bytes 1572872 | tf_op jit(solution)/shard_map/ppermute | solution.py:557
  4.9 0.1 pack.1.refs_0_.refs_4_
  4.9 4.8 %collective-permute-start.3 = (bf16[160,128]{1,0:T(8,128)(2,1)S(1)}, bf16[160,128]{1,0:T(8,128)(2,1)S(1)}, u32[]{:S(2)}, u32[]{:S(2)}) collective-permute-start(bf16[160,128]{1,0:T(8,128)(2,1)S(1)} %pack.1.refs_0_.refs_4_), channel_id=1, source_target_pairs={{0,12},{4,8},{8,4},{12,0},{1,13},{5,9},{9,5},{13,1},{2,14},{6,10},... | collective-permute-start | bytes 122888 | tf_op jit(solution)/shard_map/ppermute | solution.py:557
  9.7 0.0 collective-permute-start.2
  9.7 0.6 %collective-permute-start.1 = (bf16[160,128]{1,0:T(8,128)(2,1)S(1)}, bf16[160,128]{1,0:T(8,128)(2,1)S(1)}, u32[]{:S(2)}, u32[]{:S(2)}) collective-permute-start(bf16[160,128]{1,0:T(8,128)(2,1)S(1)} %pack.1.refs_0_.refs_4_), channel_id=1, source_target_pairs={{0,4},{4,0},{8,12},{12,8},{1,5},{5,1},{9,13},{13,9},{2,6},{6,2},{1... | collective-permute-start | bytes 122888 | tf_op jit(solution)/shard_map/ppermute | solution.py:557
  10.3 1.8 %stage.1 = (f32[128,1024]{1,0:T(8,128)S(1)}, bf16[1088,128]{1,0:T(8,128)(2,1)S(1)}, bf16[3072,128]{1,0:T(8,128)(2,1)S(1)}, bf16[1600,128]{1,0:T(8,128)(2,1)S(1)}...) custom-call(f32[1,128,1024]{2,1,0:T(8,128)} %target_ref, ...), custom_call_target="tpu_custom_call" | custom-call | tf_op jit(solution)/shard_map/stage/pallas_call | solution.py:630
  12.1 0.0 collective-permute-done.3.refs_3_.refs_7_
  12.2 2.5 %collective-permute-done.2.refs_2_.refs_6_ = bf16[160,128]{1,0:T(8,128)(2,1)S(1)} collective-permute-done((bf16[160,128]{1,0:T(8,128)(2,1)S(1)}, bf16[160,128]{1,0:T(8,128)(2,1)S(1)}, u32[]{:S(2)}, u32[]{:S(2)}) %collective-permute-start.2) | collective-permute-done | bytes 40992 | tf_op jit(solution)/shard_map/ppermute | solution.py:557
  14.6 0.0 collective-permute-done.1.refs_1_.refs_5_
  14.6 0.0 collective-permute-done.4.refs_5_
  14.6 2.6 %image.1 = (f32[1,128,1024]{2,1,0:T(8,128)}, f32[24,64,128]{2,1,0:T(8,128)S(1)}, f32[40,128]{1,0:T(8,128)S(1)}, bf16[48,128]{1,0:T(8,128)(2,1)S(1)}, bf16[48,128...) custom-call(bf16[160,128]{1,0:T(8,128)(2,1)S(1)} %pack.1.refs_0_.refs_4_, ...), custom_call_target="tpu_custom_call" | custom-call | tf_op jit(solution)/shard_map/image/pallas_call | solution.py:649
  17.2 0.8 %collective-permute-start.5 = (bf16[48,128]{1,0:T(8,128)(2,1)S(1)}, bf16[48,128]{1,0:T(8,128)(2,1)S(1)}, u32[]{:S(2)}, u32[]{:S(2)}) collective-permute-start(bf16[48,128]{1,0:T(8,128)(2,1)S(1)} %get-tuple-element.48), channel_id=1, source_target_pairs={{0,4},{4,0},{8,12},{12,8},{1,5},{5,1},{9,13},{13,9},{2,6},{6,2},{1... | collective-permute-start | bytes 36872 | tf_op jit(solution)/shard_map/ppermute | solution.py:557
  18.0 1.7 %collective-permute-start.6 = (bf16[48,128]{1,0:T(8,128)(2,1)S(1)}, bf16[48,128]{1,0:T(8,128)(2,1)S(1)}, u32[]{:S(2)}, u32[]{:S(2)}) collective-permute-start(bf16[48,128]{1,0:T(8,128)(2,1)S(1)} %get-tuple-element.49), channel_id=1, source_target_pairs={{0,8},{4,12},{8,0},{12,4},{1,9},{5,13},{9,1},{13,5},{2,10},{6,14},... | collective-permute-start | bytes 36872 | tf_op jit(solution)/shard_map/ppermute | solution.py:557
  19.7 2.0 %collective-permute-start.7 = (bf16[48,128]{1,0:T(8,128)(2,1)S(1)}, bf16[48,128]{1,0:T(8,128)(2,1)S(1)}, u32[]{:S(2)}, u32[]{:S(2)}) collective-permute-start(bf16[48,128]{1,0:T(8,128)(2,1)S(1)} %get-tuple-element.50), channel_id=1, source_target_pairs={{0,12},{4,8},{8,4},{12,0},{1,13},{5,9},{9,5},{13,1},{2,14},{6,10},... | collective-permute-start | bytes 36872 | tf_op jit(solution)/shard_map/ppermute | solution.py:557
  21.7 0.0 collective-permute-done.5.refs_1_
  21.7 0.9 %collective-permute-done.6.refs_2_ = bf16[48,128]{1,0:T(8,128)(2,1)S(1)} collective-permute-done((bf16[48,128]{1,0:T(8,128)(2,1)S(1)}, bf16[48,128]{1,0:T(8,128)(2,1)S(1)}, u32[]{:S(2)}, u32[]{:S(2)}) %collective-permute-start.6) | collective-permute-done | bytes 12320 | tf_op jit(solution)/shard_map/ppermute | solution.py:557
  22.6 2.6 %collective-permute-done.7.refs_3_ = bf16[48,128]{1,0:T(8,128)(2,1)S(1)} collective-permute-done((bf16[48,128]{1,0:T(8,128)(2,1)S(1)}, bf16[48,128]{1,0:T(8,128)(2,1)S(1)}, u32[]{:S(2)}, u32[]{:S(2)}) %collective-permute-start.7) | collective-permute-done | bytes 12320 | tf_op jit(solution)/shard_map/ppermute | solution.py:557
  25.2 1.7 %collective-permute-start.8 = (f32[8,128]{1,0:T(8,128)S(1)}, f32[8,128]{1,0:T(8,128)S(1)}, u32[]{:S(2)}, u32[]{:S(2)}) collective-permute-start(f32[8,128]{1,0:T(8,128)S(1)} %fusion), channel_id=1, source_target_pairs={{0,2},{2,0},{1,3},{3,1},{4,6},{6,4},{5,7},{7,5},{8,10},{10,8},{9,1... | collective-permute-start | bytes 12296 | tf_op jit(solution)/shard_map/ppermute | solution.py:557
  26.9 2.8 %gradient.1 = f32[1,128,1024]{2,1,0:T(8,128)} custom-call(f32[40,128]{1,0:T(8,128)S(1)} %get-tuple-element.47.refs_0_, bf16[48,128]{1,0:T(8,128)(2,1)S(1)} %collective-permute-done.5.refs_1_, bf16[48,128]{1,0:T(8,128)(2,1)S(1)} %collective-permute-done.6.refs_2_, bf16[48,128]{1,0:T(8,128)(2,1)S(1)} %collective-permute-done.7.refs_3_, ...), custom_call_target="tpu_custom_call" | custom-call | tf_op jit(solution)/shard_map/gradient/pallas_call | solution.py:683
  29.7 0.0 collective-permute-done.8
  29.7 0.1 add_reduce_fusion
  29.8 0.5 %scatter.4 = f32[128]{0:T(128)} pad(f32[8]{0:T(128)S(1)} %broadcast_multiply_fusion, f32[]{:T(128)} %constant.32.clone.1), padding=0_120 | pad | bytes 548 | tf_op jit(solution)/shard_map/scatter | solution.py:698
  (5 shorter events, 0.0 us)
Async XLA Ops:
  3.1 1.4 %collective-permute-start = (f32[48,128]{1,0:T(8,128)S(1)}, f32[48,128]{1,0:T(8,128)S(1)}, u32[]{:S(2)}, u32[]{:S(2)}) collective-permute-start(f32[48,128]{1,0:T(8,128)S(1)} %get-tuple-element.35.part_ref), channel_id=1, source_target_pairs={{0,1},{1,0},{2,3},{3,2},{4,5},{5,4},{6,7},{7,6},{8,9},{9,8},{10,11... | collective-permute-start | bytes 73736 | tf_op jit(solution)/shard_map/ppermute | solution.py:557
  4.5 10.1 %collective-permute-start.4 = (f32[128,1024]{1,0:T(8,128)}, f32[128,1024]{1,0:T(8,128)S(1)}, u32[]{:S(2)}, u32[]{:S(2)}) collective-permute-start(f32[128,1024]{1,0:T(8,128)} %bitcast.1), channel_id=1, source_target_pairs={{0,1},{1,0},{2,3},{3,2},{4,5},{5,4},{6,7},{7,6},{8,9},{9,8},{10,11... | collective-permute-start | bytes 1572872 | tf_op jit(solution)/shard_map/ppermute | solution.py:557
  4.9 7.2 %collective-permute-start.3 = (bf16[160,128]{1,0:T(8,128)(2,1)S(1)}, bf16[160,128]{1,0:T(8,128)(2,1)S(1)}, u32[]{:S(2)}, u32[]{:S(2)}) collective-permute-start(bf16[160,128]{1,0:T(8,128)(2,1)S(1)} %pack.1.refs_0_.refs_4_), channel_id=1, source_target_pairs={{0,12},{4,8},{8,4},{12,0},{1,13},{5,9},{9,5},{13,1},{2,14},{6,10},... | collective-permute-start | bytes 122888 | tf_op jit(solution)/shard_map/ppermute | solution.py:557
  9.7 4.9 %collective-permute-start.2 = (bf16[160,128]{1,0:T(8,128)(2,1)S(1)}, bf16[160,128]{1,0:T(8,128)(2,1)S(1)}, u32[]{:S(2)}, u32[]{:S(2)}) collective-permute-start(bf16[160,128]{1,0:T(8,128)(2,1)S(1)} %pack.1.refs_0_.refs_4_), channel_id=1, source_target_pairs={{0,8},{4,12},{8,0},{12,4},{1,9},{5,13},{9,1},{13,5},{2,10},{6,14},... | collective-permute-start | bytes 122888 | tf_op jit(solution)/shard_map/ppermute | solution.py:557
  9.7 4.9 %collective-permute-start.1 = (bf16[160,128]{1,0:T(8,128)(2,1)S(1)}, bf16[160,128]{1,0:T(8,128)(2,1)S(1)}, u32[]{:S(2)}, u32[]{:S(2)}) collective-permute-start(bf16[160,128]{1,0:T(8,128)(2,1)S(1)} %pack.1.refs_0_.refs_4_), channel_id=1, source_target_pairs={{0,4},{4,0},{8,12},{12,8},{1,5},{5,1},{9,13},{13,9},{2,6},{6,2},{1... | collective-permute-start | bytes 122888 | tf_op jit(solution)/shard_map/ppermute | solution.py:557
  17.2 4.5 %collective-permute-start.5 = (bf16[48,128]{1,0:T(8,128)(2,1)S(1)}, bf16[48,128]{1,0:T(8,128)(2,1)S(1)}, u32[]{:S(2)}, u32[]{:S(2)}) collective-permute-start(bf16[48,128]{1,0:T(8,128)(2,1)S(1)} %get-tuple-element.48), channel_id=1, source_target_pairs={{0,4},{4,0},{8,12},{12,8},{1,5},{5,1},{9,13},{13,9},{2,6},{6,2},{1... | collective-permute-start | bytes 36872 | tf_op jit(solution)/shard_map/ppermute | solution.py:557
  18.0 4.6 %collective-permute-start.6 = (bf16[48,128]{1,0:T(8,128)(2,1)S(1)}, bf16[48,128]{1,0:T(8,128)(2,1)S(1)}, u32[]{:S(2)}, u32[]{:S(2)}) collective-permute-start(bf16[48,128]{1,0:T(8,128)(2,1)S(1)} %get-tuple-element.49), channel_id=1, source_target_pairs={{0,8},{4,12},{8,0},{12,4},{1,9},{5,13},{9,1},{13,5},{2,10},{6,14},... | collective-permute-start | bytes 36872 | tf_op jit(solution)/shard_map/ppermute | solution.py:557
  19.7 5.5 %collective-permute-start.7 = (bf16[48,128]{1,0:T(8,128)(2,1)S(1)}, bf16[48,128]{1,0:T(8,128)(2,1)S(1)}, u32[]{:S(2)}, u32[]{:S(2)}) collective-permute-start(bf16[48,128]{1,0:T(8,128)(2,1)S(1)} %get-tuple-element.50), channel_id=1, source_target_pairs={{0,12},{4,8},{8,4},{12,0},{1,13},{5,9},{9,5},{13,1},{2,14},{6,10},... | collective-permute-start | bytes 36872 | tf_op jit(solution)/shard_map/ppermute | solution.py:557
  25.2 4.5 %collective-permute-start.8 = (f32[8,128]{1,0:T(8,128)S(1)}, f32[8,128]{1,0:T(8,128)S(1)}, u32[]{:S(2)}, u32[]{:S(2)}) collective-permute-start(f32[8,128]{1,0:T(8,128)S(1)} %fusion), channel_id=1, source_target_pairs={{0,2},{2,0},{1,3},{3,1},{4,6},{6,4},{5,7},{7,5},{8,10},{10,8},{9,1... | collective-permute-start | bytes 12296 | tf_op jit(solution)/shard_map/ppermute | solution.py:557

commit v7 on v6

--- a/solution.py
+++ b/solution.py
@@ -95,7 +95,7 @@
     drop = pair_table(coarse_cos, coarse_sin).T
     drop = np.concatenate([drop, drop[:, M:], -drop[:, :M]], 1)
     high, low = split_np(drop)
-    drop_cols = np.concatenate([high, low, high], 0)
+    drop_cols = np.concatenate([high, low], 0)
     rows = np.concatenate(
         [
             wide_cos.reshape(W, blocks, span).transpose(1, 2, 0),
@@ -499,8 +499,8 @@
                     mine = raw[:, slot * LANES : (slot + 1) * LANES]
                     wave.append(mine[:K] + turn * swap(mine[K:]))
                 waves.append(jnp.concatenate(wave, 1))
-        high, low = split(jnp.concatenate(waves, 0))
-        back = dot(jnp.concatenate([high, high, low], 1), drop_cols)
+        wave = jnp.concatenate(waves, 0).astype(bf16)
+        back = dot(jnp.concatenate([wave, wave], 1), drop_cols)
         number = 0
         for ref, place in items:
             weights = ref[pl.ds(AT_TAIL, 16), :].astype(f32) * (2.0 / K)
@@ -524,13 +524,13 @@
     turn = signs(W, 1.0, -1.0)
     high, low = split(jnp.concatenate([grad * turn, -swap(grad)], 0))
     half = dot(book.read(rows_table, "grad_rows"), jnp.concatenate([high, high, low], 0))
-    high, low = split(half)
-    both = jnp.concatenate([high, high], 1)
+    half = half.astype(bf16)
+    both = jnp.concatenate([half, half], 1)
     chunk = grad_cols.shape[1] // PIECES
     puts = []
     for piece in range(PIECES):
         here = slice(piece * chunk, (piece + 1) * chunk)
-        mask_grad_out[:, here] = dot(both, grad_cols[:, here]) + dot(low, grad_cols[:LANES, here])
+        mask_grad_out[:, here] = dot(both, grad_cols[:, here])
         place = mask_grad_ref.at[0, :, pl.ds(piece * chunk, chunk)]
         puts.append(
             pltpu.make_async_copy(mask_grad_out.at[:, pl.ds(piece * chunk, chunk)], place, sems.at[1 + piece])

time: 30.5 us -> 30.3 us (level)
  no operation moved by 1% of the time
where the time goes in v7:
time: 30.3 us; the launch traced here: 30.1 us
  starting transfers between devices  12.4 us (41%)
  Pallas kernels  8.87 us (29%)
  waiting for transfers between devices  6.84 us (23%)
  between operations  1.34 us (4%)
  local copies, waits for them, and re-layouts  0.52 us (2%)
    ppermute x9, starting transfers between devices, exchange(): lax.ppermute(value, axis, [(i, i ^ step) for i in range(lax.axis_size(axi...  12.4 us
    ppermute x9, waiting for transfers between devices, exchange(): lax.ppermute(value, axis, [(i, i ^ step) for i in range(lax.axis_size(axi...  6.84 us
    pallas_call x1, Pallas kernels, shards(): pl.pallas_call(functools.partial(image_kernel, book, len(parcels), len(ta...  2.62 us
    pallas_call x1, Pallas kernels, shards(): pl.pallas_call(functools.partial(gradient_kernel, book, len(folds), len(p...  2.56 us
    pallas_call x1, Pallas kernels, shards(): pl.pallas_call(spectrum_kernel, in_specs=[HBM] * 5 + [SMEM] + [HBM] * 3,...  1.86 us
    pallas_call x1, Pallas kernels, shards(): pl.pallas_call(functools.partial(stage_kernel, book), in_specs=[HBM] * 2,...  1.75 us
  transfers between devices with their start and end apart: 9, of which 4 were waited for; matrix products, arithmetic and copies ran while one was open for 0% of the time, Pallas kernels for 15%

profile of v7, /device:TPU:0, one launch (start us, length us, event | category | flops | bytes accessed | tf_op | source)
XLA Modules:
  0.0 30.1 jit_solution(6640431885270667359)
XLA Ops:
  1.3 1.9 %spectrum.1 = (f32[48,128]{1,0:T(8,128)S(1)}, bf16[112,128]{1,0:T(8,128)(2,1)S(1)}, f32[8,128]{1,0:T(8,128)S(1)}) custom-call(f32[1,128,1024]{2,1,0:T(8,128)} %mask_ref.1, bf16[128,2048]{1,0:T(8,128)(2,1)} %pupil_ref.1, bf16[128]{0:T(256)(128)(2,1)} %weight_ref.1, s32[128]{0:T(128)} %cell_ref.1, s32[4]{0:T(128)} %active_ref.1, s32[1]{0:T(128)S(6)} %copy.14.class_ref, ...), custom_call_target="tpu_custom_call" | custom-call | tf_op jit(solution)/shard_map/spectrum/pallas_call | solution.py:581
  3.1 0.5 %collective-permute-start = (f32[48,128]{1,0:T(8,128)S(1)}, f32[48,128]{1,0:T(8,128)S(1)}, u32[]{:S(2)}, u32[]{:S(2)}) collective-permute-start(f32[48,128]{1,0:T(8,128)S(1)} %get-tuple-element.35.part_ref), channel_id=1, source_target_pairs={{0,1},{1,0},{2,3},{3,2},{4,5},{5,4},{6,7},{7,6},{8,9},{9,8},{10,11... | collective-permute-start | bytes 73736 | tf_op jit(solution)/shard_map/ppermute | solution.py:557
  3.7 0.8 %collective-permute-done.refs_0_ = f32[48,128]{1,0:T(8,128)S(1)} collective-permute-done((f32[48,128]{1,0:T(8,128)S(1)}, f32[48,128]{1,0:T(8,128)S(1)}, u32[]{:S(2)}, u32[]{:S(2)}) %collective-permute-start) | collective-permute-done | bytes 24608 | tf_op jit(solution)/shard_map/ppermute | solution.py:557
  4.5 0.3 %collective-permute-start.4 = (f32[128,1024]{1,0:T(8,128)}, f32[128,1024]{1,0:T(8,128)S(1)}, u32[]{:S(2)}, u32[]{:S(2)}) collective-permute-start(f32[128,1024]{1,0:T(8,128)} %bitcast.1), channel_id=1, source_target_pairs={{0,1},{1,0},{2,3},{3,2},{4,5},{5,4},{6,7},{7,6},{8,9},{9,8},{10,11... | collective-permute-start | bytes 1572872 | tf_op jit(solution)/shard_map/ppermute | solution.py:557
  4.9 0.1 pack.1.refs_0_.refs_4_
  4.9 4.8 %collective-permute-start.3 = (bf16[160,128]{1,0:T(8,128)(2,1)S(1)}, bf16[160,128]{1,0:T(8,128)(2,1)S(1)}, u32[]{:S(2)}, u32[]{:S(2)}) collective-permute-start(bf16[160,128]{1,0:T(8,128)(2,1)S(1)} %pack.1.refs_0_.refs_4_), channel_id=1, source_target_pairs={{0,12},{4,8},{8,4},{12,0},{1,13},{5,9},{9,5},{13,1},{2,14},{6,10},... | collective-permute-start | bytes 122888 | tf_op jit(solution)/shard_map/ppermute | solution.py:557
  9.7 0.0 collective-permute-start.2
  9.7 0.6 %collective-permute-start.1 = (bf16[160,128]{1,0:T(8,128)(2,1)S(1)}, bf16[160,128]{1,0:T(8,128)(2,1)S(1)}, u32[]{:S(2)}, u32[]{:S(2)}) collective-permute-start(bf16[160,128]{1,0:T(8,128)(2,1)S(1)} %pack.1.refs_0_.refs_4_), channel_id=1, source_target_pairs={{0,4},{4,0},{8,12},{12,8},{1,5},{5,1},{9,13},{13,9},{2,6},{6,2},{1... | collective-permute-start | bytes 122888 | tf_op jit(solution)/shard_map/ppermute | solution.py:557
  10.3 1.7 %stage.1 = (f32[128,1024]{1,0:T(8,128)S(1)}, bf16[1088,128]{1,0:T(8,128)(2,1)S(1)}, bf16[3072,128]{1,0:T(8,128)(2,1)S(1)}, bf16[1088,128]{1,0:T(8,128)(2,1)S(1)}...) custom-call(f32[1,128,1024]{2,1,0:T(8,128)} %target_ref, ...), custom_call_target="tpu_custom_call" | custom-call | tf_op jit(solution)/shard_map/stage/pallas_call | solution.py:630
  12.1 0.0 collective-permute-done.3.refs_3_.refs_7_
  12.1 2.5 %collective-permute-done.2.refs_2_.refs_6_ = bf16[160,128]{1,0:T(8,128)(2,1)S(1)} collective-permute-done((bf16[160,128]{1,0:T(8,128)(2,1)S(1)}, bf16[160,128]{1,0:T(8,128)(2,1)S(1)}, u32[]{:S(2)}, u32[]{:S(2)}) %collective-permute-start.2) | collective-permute-done | bytes 40992 | tf_op jit(solution)/shard_map/ppermute | solution.py:557
  14.6 0.0 collective-permute-done.1.refs_1_.refs_5_
  14.6 0.0 collective-permute-done.4.refs_5_
  14.6 2.6 %image.1 = (f32[1,128,1024]{2,1,0:T(8,128)}, f32[24,64,128]{2,1,0:T(8,128)S(1)}, f32[40,128]{1,0:T(8,128)S(1)}, bf16[48,128]{1,0:T(8,128)(2,1)S(1)}, bf16[48,128...) custom-call(bf16[160,128]{1,0:T(8,128)(2,1)S(1)} %pack.1.refs_0_.refs_4_, ...), custom_call_target="tpu_custom_call" | custom-call | tf_op jit(solution)/shard_map/image/pallas_call | solution.py:649
  17.2 0.8 %collective-permute-start.5 = (bf16[48,128]{1,0:T(8,128)(2,1)S(1)}, bf16[48,128]{1,0:T(8,128)(2,1)S(1)}, u32[]{:S(2)}, u32[]{:S(2)}) collective-permute-start(bf16[48,128]{1,0:T(8,128)(2,1)S(1)} %get-tuple-element.48), channel_id=1, source_target_pairs={{0,4},{4,0},{8,12},{12,8},{1,5},{5,1},{9,13},{13,9},{2,6},{6,2},{1... | collective-permute-start | bytes 36872 | tf_op jit(solution)/shard_map/ppermute | solution.py:557
  18.0 1.7 %collective-permute-start.6 = (bf16[48,128]{1,0:T(8,128)(2,1)S(1)}, bf16[48,128]{1,0:T(8,128)(2,1)S(1)}, u32[]{:S(2)}, u32[]{:S(2)}) collective-permute-start(bf16[48,128]{1,0:T(8,128)(2,1)S(1)} %get-tuple-element.49), channel_id=1, source_target_pairs={{0,8},{4,12},{8,0},{12,4},{1,9},{5,13},{9,1},{13,5},{2,10},{6,14},... | collective-permute-start | bytes 36872 | tf_op jit(solution)/shard_map/ppermute | solution.py:557
  19.7 2.0 %collective-permute-start.7 = (bf16[48,128]{1,0:T(8,128)(2,1)S(1)}, bf16[48,128]{1,0:T(8,128)(2,1)S(1)}, u32[]{:S(2)}, u32[]{:S(2)}) collective-permute-start(bf16[48,128]{1,0:T(8,128)(2,1)S(1)} %get-tuple-element.50), channel_id=1, source_target_pairs={{0,12},{4,8},{8,4},{12,0},{1,13},{5,9},{9,5},{13,1},{2,14},{6,10},... | collective-permute-start | bytes 36872 | tf_op jit(solution)/shard_map/ppermute | solution.py:557
  21.7 0.0 collective-permute-done.5.refs_1_
  21.7 0.9 %collective-permute-done.6.refs_2_ = bf16[48,128]{1,0:T(8,128)(2,1)S(1)} collective-permute-done((bf16[48,128]{1,0:T(8,128)(2,1)S(1)}, bf16[48,128]{1,0:T(8,128)(2,1)S(1)}, u32[]{:S(2)}, u32[]{:S(2)}) %collective-permute-start.6) | collective-permute-done | bytes 12320 | tf_op jit(solution)/shard_map/ppermute | solution.py:557
  22.6 2.6 %collective-permute-done.7.refs_3_ = bf16[48,128]{1,0:T(8,128)(2,1)S(1)} collective-permute-done((bf16[48,128]{1,0:T(8,128)(2,1)S(1)}, bf16[48,128]{1,0:T(8,128)(2,1)S(1)}, u32[]{:S(2)}, u32[]{:S(2)}) %collective-permute-start.7) | collective-permute-done | bytes 12320 | tf_op jit(solution)/shard_map/ppermute | solution.py:557
  25.2 1.7 %collective-permute-start.8 = (f32[8,128]{1,0:T(8,128)S(1)}, f32[8,128]{1,0:T(8,128)S(1)}, u32[]{:S(2)}, u32[]{:S(2)}) collective-permute-start(f32[8,128]{1,0:T(8,128)S(1)} %fusion), channel_id=1, source_target_pairs={{0,2},{2,0},{1,3},{3,1},{4,6},{6,4},{5,7},{7,5},{8,10},{10,8},{9,1... | collective-permute-start | bytes 12296 | tf_op jit(solution)/shard_map/ppermute | solution.py:557
  26.9 2.6 %gradient.1 = f32[1,128,1024]{2,1,0:T(8,128)} custom-call(f32[40,128]{1,0:T(8,128)S(1)} %get-tuple-element.47.refs_0_, bf16[48,128]{1,0:T(8,128)(2,1)S(1)} %collective-permute-done.5.refs_1_, bf16[48,128]{1,0:T(8,128)(2,1)S(1)} %collective-permute-done.6.refs_2_, bf16[48,128]{1,0:T(8,128)(2,1)S(1)} %collective-permute-done.7.refs_3_, ...), custom_call_target="tpu_custom_call" | custom-call | tf_op jit(solution)/shard_map/gradient/pallas_call | solution.py:683
  29.5 0.0 collective-permute-done.8
  29.5 0.1 add_reduce_fusion
  29.6 0.5 %scatter.4 = f32[128]{0:T(128)} pad(f32[8]{0:T(128)S(1)} %broadcast_multiply_fusion, f32[]{:T(128)} %constant.32.clone.1), padding=0_120 | pad | bytes 548 | tf_op jit(solution)/shard_map/scatter | solution.py:698
  (5 shorter events, 0.0 us)
Async XLA Ops:
  3.1 1.4 %collective-permute-start = (f32[48,128]{1,0:T(8,128)S(1)}, f32[48,128]{1,0:T(8,128)S(1)}, u32[]{:S(2)}, u32[]{:S(2)}) collective-permute-start(f32[48,128]{1,0:T(8,128)S(1)} %get-tuple-element.35.part_ref), channel_id=1, source_target_pairs={{0,1},{1,0},{2,3},{3,2},{4,5},{5,4},{6,7},{7,6},{8,9},{9,8},{10,11... | collective-permute-start | bytes 73736 | tf_op jit(solution)/shard_map/ppermute | solution.py:557
  4.5 10.1 %collective-permute-start.4 = (f32[128,1024]{1,0:T(8,128)}, f32[128,1024]{1,0:T(8,128)S(1)}, u32[]{:S(2)}, u32[]{:S(2)}) collective-permute-start(f32[128,1024]{1,0:T(8,128)} %bitcast.1), channel_id=1, source_target_pairs={{0,1},{1,0},{2,3},{3,2},{4,5},{5,4},{6,7},{7,6},{8,9},{9,8},{10,11... | collective-permute-start | bytes 1572872 | tf_op jit(solution)/shard_map/ppermute | solution.py:557
  4.9 7.2 %collective-permute-start.3 = (bf16[160,128]{1,0:T(8,128)(2,1)S(1)}, bf16[160,128]{1,0:T(8,128)(2,1)S(1)}, u32[]{:S(2)}, u32[]{:S(2)}) collective-permute-start(bf16[160,128]{1,0:T(8,128)(2,1)S(1)} %pack.1.refs_0_.refs_4_), channel_id=1, source_target_pairs={{0,12},{4,8},{8,4},{12,0},{1,13},{5,9},{9,5},{13,1},{2,14},{6,10},... | collective-permute-start | bytes 122888 | tf_op jit(solution)/shard_map/ppermute | solution.py:557
  9.7 4.9 %collective-permute-start.2 = (bf16[160,128]{1,0:T(8,128)(2,1)S(1)}, bf16[160,128]{1,0:T(8,128)(2,1)S(1)}, u32[]{:S(2)}, u32[]{:S(2)}) collective-permute-start(bf16[160,128]{1,0:T(8,128)(2,1)S(1)} %pack.1.refs_0_.refs_4_), channel_id=1, source_target_pairs={{0,8},{4,12},{8,0},{12,4},{1,9},{5,13},{9,1},{13,5},{2,10},{6,14},... | collective-permute-start | bytes 122888 | tf_op jit(solution)/shard_map/ppermute | solution.py:557
  9.7 4.9 %collective-permute-start.1 = (bf16[160,128]{1,0:T(8,128)(2,1)S(1)}, bf16[160,128]{1,0:T(8,128)(2,1)S(1)}, u32[]{:S(2)}, u32[]{:S(2)}) collective-permute-start(bf16[160,128]{1,0:T(8,128)(2,1)S(1)} %pack.1.refs_0_.refs_4_), channel_id=1, source_target_pairs={{0,4},{4,0},{8,12},{12,8},{1,5},{5,1},{9,13},{13,9},{2,6},{6,2},{1... | collective-permute-start | bytes 122888 | tf_op jit(solution)/shard_map/ppermute | solution.py:557
  17.2 4.5 %collective-permute-start.5 = (bf16[48,128]{1,0:T(8,128)(2,1)S(1)}, bf16[48,128]{1,0:T(8,128)(2,1)S(1)}, u32[]{:S(2)}, u32[]{:S(2)}) collective-permute-start(bf16[48,128]{1,0:T(8,128)(2,1)S(1)} %get-tuple-element.48), channel_id=1, source_target_pairs={{0,4},{4,0},{8,12},{12,8},{1,5},{5,1},{9,13},{13,9},{2,6},{6,2},{1... | collective-permute-start | bytes 36872 | tf_op jit(solution)/shard_map/ppermute | solution.py:557
  18.0 4.6 %collective-permute-start.6 = (bf16[48,128]{1,0:T(8,128)(2,1)S(1)}, bf16[48,128]{1,0:T(8,128)(2,1)S(1)}, u32[]{:S(2)}, u32[]{:S(2)}) collective-permute-start(bf16[48,128]{1,0:T(8,128)(2,1)S(1)} %get-tuple-element.49), channel_id=1, source_target_pairs={{0,8},{4,12},{8,0},{12,4},{1,9},{5,13},{9,1},{13,5},{2,10},{6,14},... | collective-permute-start | bytes 36872 | tf_op jit(solution)/shard_map/ppermute | solution.py:557
  19.7 5.5 %collective-permute-start.7 = (bf16[48,128]{1,0:T(8,128)(2,1)S(1)}, bf16[48,128]{1,0:T(8,128)(2,1)S(1)}, u32[]{:S(2)}, u32[]{:S(2)}) collective-permute-start(bf16[48,128]{1,0:T(8,128)(2,1)S(1)} %get-tuple-element.50), channel_id=1, source_target_pairs={{0,12},{4,8},{8,4},{12,0},{1,13},{5,9},{9,5},{13,1},{2,14},{6,10},... | collective-permute-start | bytes 36872 | tf_op jit(solution)/shard_map/ppermute | solution.py:557
  25.2 4.3 %collective-permute-start.8 = (f32[8,128]{1,0:T(8,128)S(1)}, f32[8,128]{1,0:T(8,128)S(1)}, u32[]{:S(2)}, u32[]{:S(2)}) collective-permute-start(f32[8,128]{1,0:T(8,128)S(1)} %fusion), channel_id=1, source_target_pairs={{0,2},{2,0},{1,3},{3,1},{4,6},{6,4},{5,7},{7,5},{8,10},{10,8},{9,1... | collective-permute-start | bytes 12296 | tf_op jit(solution)/shard_map/ppermute | solution.py:557

commit v8 on v7

--- a/solution.py
+++ b/solution.py
@@ -20,9 +20,8 @@
 LANES = 128
 PAIRS = MOST // 2
 AT_PUPILS = W
-AT_TAIL = AT_PUPILS + PAIRS * K
-ROWS = AT_TAIL + 16
-TAIL_PAIR, TAIL_CELL = 8, 12
+ROWS = AT_PUPILS + PAIRS * K
+FACTS = M - 1
 PIECES = 4
 SUMS = 8
 
@@ -252,20 +251,13 @@
     shape = (8, LANES)
     weights = jnp.broadcast_to(weight_in[...].astype(f32).reshape(1, -1)[:, :LANES], shape)
     column = jnp.sum(jnp.where(row_of(shape) == lane_of(shape), weights, 0.0), 1, keepdims=True)
-    column = jnp.broadcast_to(column, shape)
-    tail = [column]
-    for pair in range(PAIRS):
-        even = lane_of((1, LANES)) // K % 2 == 0
-        tail.append(jnp.where(even, column[2 * pair : 2 * pair + 1], column[2 * pair + 1 : 2 * pair + 2]))
-    tail.append(jnp.zeros((1, LANES), f32))
-    place = lane_of((1, LANES))
-    row_code, col_code = jnp.zeros((1, LANES), f32), jnp.zeros((1, LANES), f32)
+    row_code, col_code = jnp.zeros(shape, f32), jnp.zeros(shape, f32)
     for slot in range(MOST):
         cell = cell_in[slot]
-        row_code = jnp.where(place == slot, lax.div(cell, SG).astype(f32), row_code)
-        col_code = jnp.where(place == slot, lax.rem(cell, SG).astype(f32), col_code)
-    tail += [row_code, col_code, jnp.zeros((2, LANES), f32)]
-    sent_ref[PAIRS * K :] = jnp.concatenate(tail, 0).astype(bf16)
+        row_code = jnp.where(row_of(shape) == slot, lax.div(cell, SG).astype(f32), row_code)
+        col_code = jnp.where(row_of(shape) == slot, lax.rem(cell, SG).astype(f32), col_code)
+    facts = [jnp.broadcast_to(column, shape), row_code, col_code, jnp.zeros((W - 24, LANES), f32)]
+    sent_ref[PAIRS * K :] = jnp.concatenate(facts, 0).astype(bf16)
     get_mask.wait()
     get_cols.wait()
     get_rows.wait()
@@ -291,8 +283,11 @@
         part = part + ref[...]
     high, low = split(part)
     rest = pltpu.roll(low.astype(f32), K, 1)
-    out_ref[:W] = jnp.where(lane_of(part.shape) % M < W, high.astype(f32), rest).astype(bf16)
-    out_ref[AT_PUPILS:] = sent_ref[...]
+    lane = lane_of(part.shape)
+    mixed = jnp.where(lane % M < W, high.astype(f32), rest)
+    facts = sent_ref[PAIRS * K :].astype(f32)
+    out_ref[:W] = jnp.where(lane == FACTS, facts, mixed).astype(bf16)
+    out_ref[AT_PUPILS:] = sent_ref[: PAIRS * K]
 
 
 def stage_kernel(book, target_ref, book_ref, *refs):
@@ -327,12 +322,18 @@
 def codes_of(refs, codes_v):
     def body(none, items):
         for ref, place in items:
-            tail = ref[pl.ds(AT_TAIL, 16), :].astype(f32)
-            code = tail[TAIL_CELL : TAIL_CELL + 1] * 32.0 + tail[TAIL_CELL + 1 : TAIL_CELL + 2]
+            facts = ref[:W].astype(f32)[:, FACTS : FACTS + 1]
+            shape = (8, LANES)
+            code = jnp.broadcast_to(facts[8:16] * 32.0 + facts[16:24], shape)
+            code = jnp.sum(jnp.where(row_of(shape) == lane_of(shape), code, 0.0), 0, keepdims=True)
             codes_v[pl.ds(place, 1), :] = code.astype(jnp.int32)
         return none
 
     over_owners(refs, body, 0)
+
+
+def weights_of(ref):
+    return jnp.broadcast_to(ref[:16].astype(f32)[:8, FACTS : FACTS + 1], (8, LANES))
 
 
 def window_of(codes, place, slot):
@@ -366,7 +367,8 @@
     def gather(total, items):
         for ref, place in items:
             value = ref[:W].astype(f32)
-            rest = jnp.where(lane_of(value.shape) % M < W, 0.0, value)
+            lane = lane_of(value.shape)
+            rest = jnp.where((lane % M < W) | (lane == FACTS), 0.0, value)
             total = total + (value + pltpu.roll(rest, LANES - K, 1))
         return total
 
@@ -395,7 +397,7 @@
         wave = dot(jnp.concatenate([wave, wave], 1), lift_cols).astype(bf16)
         number = 0
         for ref, place in items:
-            weights = ref[pl.ds(AT_TAIL, 16), :].astype(f32)
+            weights = weights_of(ref)
             for pair in range(PAIRS):
                 here = slice(number * K, (number + 1) * K)
                 number += 1
@@ -503,13 +505,14 @@
         back = dot(jnp.concatenate([wave, wave], 1), drop_cols)
         number = 0
         for ref, place in items:
-            weights = ref[pl.ds(AT_TAIL, 16), :].astype(f32) * (2.0 / K)
+            weights = weights_of(ref) * (2.0 / K)
             for pair in range(PAIRS):
                 mine = back[number * K : (number + 1) * K]
                 number += 1
                 real, imag = pair_parts(ref, pair)
                 product = real * mine[:, :LANES] + imag * mine[:, LANES:]
-                product = weights[TAIL_PAIR + pair : TAIL_PAIR + pair + 1] * product
+                first, second = weights[2 * pair : 2 * pair + 1], weights[2 * pair + 1 : 2 * pair + 2]
+                product = jnp.where(even[:1], first, second) * product
                 for slot in range(2):
                     row, col = window_of(codes, place, 2 * pair + slot)
                     keep = even if slot == 0 else jnp.logical_not(even)
@@ -584,7 +587,7 @@
         out_specs=[VMEM] * 3,
         out_shape=[
             jax.ShapeDtypeStruct((W, LANES), f32),
-            jax.ShapeDtypeStruct((ROWS - AT_PUPILS, LANES), bf16),
+            jax.ShapeDtypeStruct((PAIRS * K + W, LANES), bf16),
             jax.ShapeDtypeStruct((8, LANES), f32),
         ],
         scratch_shapes=[

time: 30.3 us -> 30.2 us (level)
  no operation moved by 1% of the time
where the time goes in v8:
time: 30.2 us; the launch traced here: 30 us
  starting transfers between devices  12.4 us (41%)
  Pallas kernels  9 us (30%)
  waiting for transfers between devices  6.62 us (22%)
  between operations  1.34 us (4%)
  local copies, waits for them, and re-layouts  0.52 us (2%)
    ppermute x9, starting transfers between devices, exchange(): lax.ppermute(value, axis, [(i, i ^ step) for i in range(lax.axis_size(axi...  12.4 us
    ppermute x9, waiting for transfers between devices, exchange(): lax.ppermute(value, axis, [(i, i ^ step) for i in range(lax.axis_size(axi...  6.62 us
    pallas_call x1, Pallas kernels, shards(): pl.pallas_call(functools.partial(image_kernel, book, len(parcels), len(ta...  2.67 us
    pallas_call x1, Pallas kernels, shards(): pl.pallas_call(functools.partial(gradient_kernel, book, len(folds), len(p...  2.64 us
    pallas_call x1, Pallas kernels, shards(): pl.pallas_call(spectrum_kernel, in_specs=[HBM] * 5 + [SMEM] + [HBM] * 3,...  1.86 us
    pallas_call x1, Pallas kernels, shards(): pl.pallas_call(functools.partial(stage_kernel, book), in_specs=[HBM] * 2,...  1.75 us
  transfers between devices with their start and end apart: 9, of which 4 were waited for; matrix products, arithmetic and copies ran while one was open for 0% of the time, Pallas kernels for 15%

profile of v8, /device:TPU:0, one launch (start us, length us, event | category | flops | bytes accessed | tf_op | source)
XLA Modules:
  0.0 30.0 jit_solution(8680213505991348966)
XLA Ops:
  1.3 1.9 %spectrum.1 = (f32[48,128]{1,0:T(8,128)S(1)}, bf16[144,128]{1,0:T(8,128)(2,1)S(1)}, f32[8,128]{1,0:T(8,128)S(1)}) custom-call(f32[1,128,1024]{2,1,0:T(8,128)} %mask_ref.1, bf16[128,2048]{1,0:T(8,128)(2,1)} %pupil_ref.1, bf16[128]{0:T(256)(128)(2,1)} %weight_ref.1, s32[128]{0:T(128)} %cell_ref.1, s32[4]{0:T(128)} %active_ref.1, s32[1]{0:T(128)S(6)} %copy.14.class_ref, ...), custom_call_target="tpu_custom_call" | custom-call | tf_op jit(solution)/shard_map/spectrum/pallas_call | solution.py:584
  3.1 0.5 %collective-permute-start = (f32[48,128]{1,0:T(8,128)S(1)}, f32[48,128]{1,0:T(8,128)S(1)}, u32[]{:S(2)}, u32[]{:S(2)}) collective-permute-start(f32[48,128]{1,0:T(8,128)S(1)} %get-tuple-element.35.part_ref), channel_id=1, source_target_pairs={{0,1},{1,0},{2,3},{3,2},{4,5},{5,4},{6,7},{7,6},{8,9},{9,8},{10,11... | collective-permute-start | bytes 73736 | tf_op jit(solution)/shard_map/ppermute | solution.py:560
  3.7 0.8 %collective-permute-done.refs_0_ = f32[48,128]{1,0:T(8,128)S(1)} collective-permute-done((f32[48,128]{1,0:T(8,128)S(1)}, f32[48,128]{1,0:T(8,128)S(1)}, u32[]{:S(2)}, u32[]{:S(2)}) %collective-permute-start) | collective-permute-done | bytes 24608 | tf_op jit(solution)/shard_map/ppermute | solution.py:560
  4.5 0.3 %collective-permute-start.4 = (f32[128,1024]{1,0:T(8,128)}, f32[128,1024]{1,0:T(8,128)S(1)}, u32[]{:S(2)}, u32[]{:S(2)}) collective-permute-start(f32[128,1024]{1,0:T(8,128)} %bitcast.1), channel_id=1, source_target_pairs={{0,1},{1,0},{2,3},{3,2},{4,5},{5,4},{6,7},{7,6},{8,9},{9,8},{10,11... | collective-permute-start | bytes 1572872 | tf_op jit(solution)/shard_map/ppermute | solution.py:560
  4.9 0.1 pack.1.refs_0_.refs_4_
  4.9 4.8 %collective-permute-start.3 = (bf16[144,128]{1,0:T(8,128)(2,1)S(1)}, bf16[144,128]{1,0:T(8,128)(2,1)S(1)}, u32[]{:S(2)}, u32[]{:S(2)}) collective-permute-start(bf16[144,128]{1,0:T(8,128)(2,1)S(1)} %pack.1.refs_0_.refs_4_), channel_id=1, source_target_pairs={{0,12},{4,8},{8,4},{12,0},{1,13},{5,9},{9,5},{13,1},{2,14},{6,10},... | collective-permute-start | bytes 110600 | tf_op jit(solution)/shard_map/ppermute | solution.py:560
  9.7 0.0 collective-permute-start.2
  9.7 0.6 %collective-permute-start.1 = (bf16[144,128]{1,0:T(8,128)(2,1)S(1)}, bf16[144,128]{1,0:T(8,128)(2,1)S(1)}, u32[]{:S(2)}, u32[]{:S(2)}) collective-permute-start(bf16[144,128]{1,0:T(8,128)(2,1)S(1)} %pack.1.refs_0_.refs_4_), channel_id=1, source_target_pairs={{0,4},{4,0},{8,12},{12,8},{1,5},{5,1},{9,13},{13,9},{2,6},{6,2},{1... | collective-permute-start | bytes 110600 | tf_op jit(solution)/shard_map/ppermute | solution.py:560
  10.3 1.7 %stage.1 = (f32[128,1024]{1,0:T(8,128)S(1)}, bf16[1088,128]{1,0:T(8,128)(2,1)S(1)}, bf16[3072,128]{1,0:T(8,128)(2,1)S(1)}, bf16[1088,128]{1,0:T(8,128)(2,1)S(1)}...) custom-call(f32[1,128,1024]{2,1,0:T(8,128)} %target_ref, ...), custom_call_target="tpu_custom_call" | custom-call | tf_op jit(solution)/shard_map/stage/pallas_call | solution.py:633
  12.1 0.0 collective-permute-done.3.refs_3_.refs_7_
  12.1 2.4 %collective-permute-done.2.refs_2_.refs_6_ = bf16[144,128]{1,0:T(8,128)(2,1)S(1)} collective-permute-done((bf16[144,128]{1,0:T(8,128)(2,1)S(1)}, bf16[144,128]{1,0:T(8,128)(2,1)S(1)}, u32[]{:S(2)}, u32[]{:S(2)}) %collective-permute-start.2) | collective-permute-done | bytes 36896 | tf_op jit(solution)/shard_map/ppermute | solution.py:560
  14.6 0.0 collective-permute-done.1.refs_1_.refs_5_
  14.6 0.0 collective-permute-done.4.refs_5_
  14.6 2.7 %image.1 = (f32[1,128,1024]{2,1,0:T(8,128)}, f32[24,64,128]{2,1,0:T(8,128)S(1)}, f32[40,128]{1,0:T(8,128)S(1)}, bf16[48,128]{1,0:T(8,128)(2,1)S(1)}, bf16[48,128...) custom-call(bf16[144,128]{1,0:T(8,128)(2,1)S(1)} %pack.1.refs_0_.refs_4_, ...), custom_call_target="tpu_custom_call" | custom-call | tf_op jit(solution)/shard_map/image/pallas_call | solution.py:652
  17.2 0.6 %collective-permute-start.5 = (bf16[48,128]{1,0:T(8,128)(2,1)S(1)}, bf16[48,128]{1,0:T(8,128)(2,1)S(1)}, u32[]{:S(2)}, u32[]{:S(2)}) collective-permute-start(bf16[48,128]{1,0:T(8,128)(2,1)S(1)} %get-tuple-element.48), channel_id=1, source_target_pairs={{0,4},{4,0},{8,12},{12,8},{1,5},{5,1},{9,13},{13,9},{2,6},{6,2},{1... | collective-permute-start | bytes 36872 | tf_op jit(solution)/shard_map/ppermute | solution.py:560
  17.8 1.7 %collective-permute-start.6 = (bf16[48,128]{1,0:T(8,128)(2,1)S(1)}, bf16[48,128]{1,0:T(8,128)(2,1)S(1)}, u32[]{:S(2)}, u32[]{:S(2)}) collective-permute-start(bf16[48,128]{1,0:T(8,128)(2,1)S(1)} %get-tuple-element.49), channel_id=1, source_target_pairs={{0,8},{4,12},{8,0},{12,4},{1,9},{5,13},{9,1},{13,5},{2,10},{6,14},... | collective-permute-start | bytes 36872 | tf_op jit(solution)/shard_map/ppermute | solution.py:560
  19.5 2.2 %collective-permute-start.7 = (bf16[48,128]{1,0:T(8,128)(2,1)S(1)}, bf16[48,128]{1,0:T(8,128)(2,1)S(1)}, u32[]{:S(2)}, u32[]{:S(2)}) collective-permute-start(bf16[48,128]{1,0:T(8,128)(2,1)S(1)} %get-tuple-element.50), channel_id=1, source_target_pairs={{0,12},{4,8},{8,4},{12,0},{1,13},{5,9},{9,5},{13,1},{2,14},{6,10},... | collective-permute-start | bytes 36872 | tf_op jit(solution)/shard_map/ppermute | solution.py:560
  21.7 0.0 collective-permute-done.5.refs_1_
  21.7 0.7 %collective-permute-done.6.refs_2_ = bf16[48,128]{1,0:T(8,128)(2,1)S(1)} collective-permute-done((bf16[48,128]{1,0:T(8,128)(2,1)S(1)}, bf16[48,128]{1,0:T(8,128)(2,1)S(1)}, u32[]{:S(2)}, u32[]{:S(2)}) %collective-permute-start.6) | collective-permute-done | bytes 12320 | tf_op jit(solution)/shard_map/ppermute | solution.py:560
  22.4 2.6 %collective-permute-done.7.refs_3_ = bf16[48,128]{1,0:T(8,128)(2,1)S(1)} collective-permute-done((bf16[48,128]{1,0:T(8,128)(2,1)S(1)}, bf16[48,128]{1,0:T(8,128)(2,1)S(1)}, u32[]{:S(2)}, u32[]{:S(2)}) %collective-permute-start.7) | collective-permute-done | bytes 12320 | tf_op jit(solution)/shard_map/ppermute | solution.py:560
  25.0 1.7 %collective-permute-start.8 = (f32[8,128]{1,0:T(8,128)S(1)}, f32[8,128]{1,0:T(8,128)S(1)}, u32[]{:S(2)}, u32[]{:S(2)}) collective-permute-start(f32[8,128]{1,0:T(8,128)S(1)} %fusion), channel_id=1, source_target_pairs={{0,2},{2,0},{1,3},{3,1},{4,6},{6,4},{5,7},{7,5},{8,10},{10,8},{9,1... | collective-permute-start | bytes 12296 | tf_op jit(solution)/shard_map/ppermute | solution.py:560
  26.7 2.6 %gradient.1 = f32[1,128,1024]{2,1,0:T(8,128)} custom-call(f32[40,128]{1,0:T(8,128)S(1)} %get-tuple-element.47.refs_0_, bf16[48,128]{1,0:T(8,128)(2,1)S(1)} %collective-permute-done.5.refs_1_, bf16[48,128]{1,0:T(8,128)(2,1)S(1)} %collective-permute-done.6.refs_2_, bf16[48,128]{1,0:T(8,128)(2,1)S(1)} %collective-permute-done.7.refs_3_, ...), custom_call_target="tpu_custom_call" | custom-call | tf_op jit(solution)/shard_map/gradient/pallas_call | solution.py:686
  29.4 0.0 collective-permute-done.8
  29.4 0.1 add_reduce_fusion
  29.5 0.5 %scatter.4 = f32[128]{0:T(128)} pad(f32[8]{0:T(128)S(1)} %broadcast_multiply_fusion, f32[]{:T(128)} %constant.32.clone.1), padding=0_120 | pad | bytes 548 | tf_op jit(solution)/shard_map/scatter | solution.py:701
  (5 shorter events, 0.0 us)
Async XLA Ops:
  3.1 1.4 %collective-permute-start = (f32[48,128]{1,0:T(8,128)S(1)}, f32[48,128]{1,0:T(8,128)S(1)}, u32[]{:S(2)}, u32[]{:S(2)}) collective-permute-start(f32[48,128]{1,0:T(8,128)S(1)} %get-tuple-element.35.part_ref), channel_id=1, source_target_pairs={{0,1},{1,0},{2,3},{3,2},{4,5},{5,4},{6,7},{7,6},{8,9},{9,8},{10,11... | collective-permute-start | bytes 73736 | tf_op jit(solution)/shard_map/ppermute | solution.py:560
  4.5 10.1 %collective-permute-start.4 = (f32[128,1024]{1,0:T(8,128)}, f32[128,1024]{1,0:T(8,128)S(1)}, u32[]{:S(2)}, u32[]{:S(2)}) collective-permute-start(f32[128,1024]{1,0:T(8,128)} %bitcast.1), channel_id=1, source_target_pairs={{0,1},{1,0},{2,3},{3,2},{4,5},{5,4},{6,7},{7,6},{8,9},{9,8},{10,11... | collective-permute-start | bytes 1572872 | tf_op jit(solution)/shard_map/ppermute | solution.py:560
  4.9 7.2 %collective-permute-start.3 = (bf16[144,128]{1,0:T(8,128)(2,1)S(1)}, bf16[144,128]{1,0:T(8,128)(2,1)S(1)}, u32[]{:S(2)}, u32[]{:S(2)}) collective-permute-start(bf16[144,128]{1,0:T(8,128)(2,1)S(1)} %pack.1.refs_0_.refs_4_), channel_id=1, source_target_pairs={{0,12},{4,8},{8,4},{12,0},{1,13},{5,9},{9,5},{13,1},{2,14},{6,10},... | collective-permute-start | bytes 110600 | tf_op jit(solution)/shard_map/ppermute | solution.py:560
  9.7 4.9 %collective-permute-start.2 = (bf16[144,128]{1,0:T(8,128)(2,1)S(1)}, bf16[144,128]{1,0:T(8,128)(2,1)S(1)}, u32[]{:S(2)}, u32[]{:S(2)}) collective-permute-start(bf16[144,128]{1,0:T(8,128)(2,1)S(1)} %pack.1.refs_0_.refs_4_), channel_id=1, source_target_pairs={{0,8},{4,12},{8,0},{12,4},{1,9},{5,13},{9,1},{13,5},{2,10},{6,14},... | collective-permute-start | bytes 110600 | tf_op jit(solution)/shard_map/ppermute | solution.py:560
  9.7 4.9 %collective-permute-start.1 = (bf16[144,128]{1,0:T(8,128)(2,1)S(1)}, bf16[144,128]{1,0:T(8,128)(2,1)S(1)}, u32[]{:S(2)}, u32[]{:S(2)}) collective-permute-start(bf16[144,128]{1,0:T(8,128)(2,1)S(1)} %pack.1.refs_0_.refs_4_), channel_id=1, source_target_pairs={{0,4},{4,0},{8,12},{12,8},{1,5},{5,1},{9,13},{13,9},{2,6},{6,2},{1... | collective-permute-start | bytes 110600 | tf_op jit(solution)/shard_map/ppermute | solution.py:560
  17.2 4.5 %collective-permute-start.5 = (bf16[48,128]{1,0:T(8,128)(2,1)S(1)}, bf16[48,128]{1,0:T(8,128)(2,1)S(1)}, u32[]{:S(2)}, u32[]{:S(2)}) collective-permute-start(bf16[48,128]{1,0:T(8,128)(2,1)S(1)} %get-tuple-element.48), channel_id=1, source_target_pairs={{0,4},{4,0},{8,12},{12,8},{1,5},{5,1},{9,13},{13,9},{2,6},{6,2},{1... | collective-permute-start | bytes 36872 | tf_op jit(solution)/shard_map/ppermute | solution.py:560
  17.8 4.6 %collective-permute-start.6 = (bf16[48,128]{1,0:T(8,128)(2,1)S(1)}, bf16[48,128]{1,0:T(8,128)(2,1)S(1)}, u32[]{:S(2)}, u32[]{:S(2)}) collective-permute-start(bf16[48,128]{1,0:T(8,128)(2,1)S(1)} %get-tuple-element.49), channel_id=1, source_target_pairs={{0,8},{4,12},{8,0},{12,4},{1,9},{5,13},{9,1},{13,5},{2,10},{6,14},... | collective-permute-start | bytes 36872 | tf_op jit(solution)/shard_map/ppermute | solution.py:560
  19.5 5.5 %collective-permute-start.7 = (bf16[48,128]{1,0:T(8,128)(2,1)S(1)}, bf16[48,128]{1,0:T(8,128)(2,1)S(1)}, u32[]{:S(2)}, u32[]{:S(2)}) collective-permute-start(bf16[48,128]{1,0:T(8,128)(2,1)S(1)} %get-tuple-element.50), channel_id=1, source_target_pairs={{0,12},{4,8},{8,4},{12,0},{1,13},{5,9},{9,5},{13,1},{2,14},{6,10},... | collective-permute-start | bytes 36872 | tf_op jit(solution)/shard_map/ppermute | solution.py:560
  25.0 4.3 %collective-permute-start.8 = (f32[8,128]{1,0:T(8,128)S(1)}, f32[8,128]{1,0:T(8,128)S(1)}, u32[]{:S(2)}, u32[]{:S(2)}) collective-permute-start(f32[8,128]{1,0:T(8,128)S(1)} %fusion), channel_id=1, source_target_pairs={{0,2},{2,0},{1,3},{3,1},{4,6},{6,4},{5,7},{7,5},{8,10},{10,8},{9,1... | collective-permute-start | bytes 12296 | tf_op jit(solution)/shard_map/ppermute | solution.py:560

commit v9 on v8

--- a/solution.py
+++ b/solution.py
@@ -426,8 +426,8 @@
     slopes = []
     for number, target in enumerate(targets):
         intensity = intensities[number * span : (number + 1) * span]
-        resist = 1.0 / (1.0 + jnp.exp(-STEEP * (intensity - threshold)))
-        slope = 2.0 * STEEP * (resist - target[...]) * resist * (1.0 - resist)
+        bend = jnp.tanh((0.5 * STEEP) * (intensity - threshold))
+        slope = (0.5 * STEEP) * (0.5 * bend + (0.5 - target[...])) * (1.0 - bend * bend)
         slopes.append(slope.astype(bf16))
     folded = dot(jnp.concatenate(slopes, 0), fold_cols)
     high, low = split(folded + swap(folded))
@@ -481,7 +481,7 @@
     grid = jnp.concatenate(
         [jnp.where(low_half, packed, other), jnp.where(low_half, other, packed)], 0
     )
-    for number in range(2):
+    for number in range(MOST):
         sums[number] = jnp.zeros((W, LANES), f32)
     turn = signs(K, 1.0, -1.0)
     even = slot_lanes(K)
@@ -518,12 +518,12 @@
                     keep = even if slot == 0 else jnp.logical_not(even)
                     shift = lax.rem(col + LANES - slot * K, LANES)
                     moved = pltpu.roll(jnp.where(keep, product, 0.0), shift, 1)
-                    sums[slot, pl.ds(row, K), :] += moved
+                    sums[2 * pair + slot, pl.ds(row, K), :] += moved
         return none
 
     over_owners(sent_refs, backward, 0)
     grad_cols = book.read(grad_table, "grad_cols")
-    grad = sums[0] + sums[1]
+    grad = sum(sums[number] for number in range(1, MOST)) + sums[0]
     turn = signs(W, 1.0, -1.0)
     high, low = split(jnp.concatenate([grad * turn, -swap(grad)], 0))
     half = dot(book.read(rows_table, "grad_rows"), jnp.concatenate([high, high, low], 0))
@@ -691,7 +691,7 @@
         scratch_shapes=[
             sems((1 + PIECES,)),
             *codes,
-            pltpu.VMEM((2, W, LANES), f32),
+            pltpu.VMEM((MOST, W, LANES), f32),
             like(mask[0]),
         ],
         compiler_params=room(24576),

time: 30.2 us -> 30.2 us (level)
  no operation moved by 1% of the time
where the time goes in v9:
time: 30.2 us; the launch traced here: 30 us
  starting transfers between devices  12.4 us (41%)
  Pallas kernels  8.98 us (30%)
  waiting for transfers between devices  6.62 us (22%)
  between operations  1.34 us (4%)
  local copies, waits for them, and re-layouts  0.52 us (2%)
    ppermute x9, starting transfers between devices, exchange(): lax.ppermute(value, axis, [(i, i ^ step) for i in range(lax.axis_size(axi...  12.4 us
    ppermute x9, waiting for transfers between devices, exchange(): lax.ppermute(value, axis, [(i, i ^ step) for i in range(lax.axis_size(axi...  6.62 us
    pallas_call x1, Pallas kernels, shards(): pl.pallas_call(functools.partial(image_kernel, book, len(parcels), len(ta...  2.65 us
    pallas_call x1, Pallas kernels, shards(): pl.pallas_call(functools.partial(gradient_kernel, book, len(folds), len(p...  2.64 us
    pallas_call x1, Pallas kernels, shards(): pl.pallas_call(spectrum_kernel, in_specs=[HBM] * 5 + [SMEM] + [HBM] * 3,...  1.86 us
    pallas_call x1, Pallas kernels, shards(): pl.pallas_call(functools.partial(stage_kernel, book), in_specs=[HBM] * 2,...  1.75 us
  transfers between devices with their start and end apart: 9, of which 4 were waited for; matrix products, arithmetic and copies ran while one was open for 0% of the time, Pallas kernels for 15%

profile of v9, /device:TPU:0, one launch (start us, length us, event | category | flops | bytes accessed | tf_op | source)
XLA Modules:
  0.0 30.0 jit_solution(7335398761244276020)
XLA Ops:
  1.3 1.9 %spectrum.1 = (f32[48,128]{1,0:T(8,128)S(1)}, bf16[144,128]{1,0:T(8,128)(2,1)S(1)}, f32[8,128]{1,0:T(8,128)S(1)}) custom-call(f32[1,128,1024]{2,1,0:T(8,128)} %mask_ref.1, bf16[128,2048]{1,0:T(8,128)(2,1)} %pupil_ref.1, bf16[128]{0:T(256)(128)(2,1)} %weight_ref.1, s32[128]{0:T(128)} %cell_ref.1, s32[4]{0:T(128)} %active_ref.1, s32[1]{0:T(128)S(6)} %copy.14.class_ref, ...), custom_call_target="tpu_custom_call" | custom-call | tf_op jit(solution)/shard_map/spectrum/pallas_call | solution.py:584
  3.1 0.5 %collective-permute-start = (f32[48,128]{1,0:T(8,128)S(1)}, f32[48,128]{1,0:T(8,128)S(1)}, u32[]{:S(2)}, u32[]{:S(2)}) collective-permute-start(f32[48,128]{1,0:T(8,128)S(1)} %get-tuple-element.35.part_ref), channel_id=1, source_target_pairs={{0,1},{1,0},{2,3},{3,2},{4,5},{5,4},{6,7},{7,6},{8,9},{9,8},{10,11... | collective-permute-start | bytes 73736 | tf_op jit(solution)/shard_map/ppermute | solution.py:560
  3.7 0.8 %collective-permute-done.refs_0_ = f32[48,128]{1,0:T(8,128)S(1)} collective-permute-done((f32[48,128]{1,0:T(8,128)S(1)}, f32[48,128]{1,0:T(8,128)S(1)}, u32[]{:S(2)}, u32[]{:S(2)}) %collective-permute-start) | collective-permute-done | bytes 24608 | tf_op jit(solution)/shard_map/ppermute | solution.py:560
  4.5 0.3 %collective-permute-start.4 = (f32[128,1024]{1,0:T(8,128)}, f32[128,1024]{1,0:T(8,128)S(1)}, u32[]{:S(2)}, u32[]{:S(2)}) collective-permute-start(f32[128,1024]{1,0:T(8,128)} %bitcast.1), channel_id=1, source_target_pairs={{0,1},{1,0},{2,3},{3,2},{4,5},{5,4},{6,7},{7,6},{8,9},{9,8},{10,11... | collective-permute-start | bytes 1572872 | tf_op jit(solution)/shard_map/ppermute | solution.py:560
  4.9 0.1 pack.1.refs_0_.refs_4_
  4.9 4.8 %collective-permute-start.3 = (bf16[144,128]{1,0:T(8,128)(2,1)S(1)}, bf16[144,128]{1,0:T(8,128)(2,1)S(1)}, u32[]{:S(2)}, u32[]{:S(2)}) collective-permute-start(bf16[144,128]{1,0:T(8,128)(2,1)S(1)} %pack.1.refs_0_.refs_4_), channel_id=1, source_target_pairs={{0,12},{4,8},{8,4},{12,0},{1,13},{5,9},{9,5},{13,1},{2,14},{6,10},... | collective-permute-start | bytes 110600 | tf_op jit(solution)/shard_map/ppermute | solution.py:560
  9.7 0.0 collective-permute-start.2
  9.7 0.6 %collective-permute-start.1 = (bf16[144,128]{1,0:T(8,128)(2,1)S(1)}, bf16[144,128]{1,0:T(8,128)(2,1)S(1)}, u32[]{:S(2)}, u32[]{:S(2)}) collective-permute-start(bf16[144,128]{1,0:T(8,128)(2,1)S(1)} %pack.1.refs_0_.refs_4_), channel_id=1, source_target_pairs={{0,4},{4,0},{8,12},{12,8},{1,5},{5,1},{9,13},{13,9},{2,6},{6,2},{1... | collective-permute-start | bytes 110600 | tf_op jit(solution)/shard_map/ppermute | solution.py:560
  10.3 1.7 %stage.1 = (f32[128,1024]{1,0:T(8,128)S(1)}, bf16[1088,128]{1,0:T(8,128)(2,1)S(1)}, bf16[3072,128]{1,0:T(8,128)(2,1)S(1)}, bf16[1088,128]{1,0:T(8,128)(2,1)S(1)}...) custom-call(f32[1,128,1024]{2,1,0:T(8,128)} %target_ref, ...), custom_call_target="tpu_custom_call" | custom-call | tf_op jit(solution)/shard_map/stage/pallas_call | solution.py:633
  12.1 0.0 collective-permute-done.3.refs_3_.refs_7_
  12.1 2.4 %collective-permute-done.2.refs_2_.refs_6_ = bf16[144,128]{1,0:T(8,128)(2,1)S(1)} collective-permute-done((bf16[144,128]{1,0:T(8,128)(2,1)S(1)}, bf16[144,128]{1,0:T(8,128)(2,1)S(1)}, u32[]{:S(2)}, u32[]{:S(2)}) %collective-permute-start.2) | collective-permute-done | bytes 36896 | tf_op jit(solution)/shard_map/ppermute | solution.py:560
  14.6 0.0 collective-permute-done.1.refs_1_.refs_5_
  14.6 0.0 collective-permute-done.4.refs_5_
  14.6 2.7 %image.1 = (f32[1,128,1024]{2,1,0:T(8,128)}, f32[24,64,128]{2,1,0:T(8,128)S(1)}, f32[40,128]{1,0:T(8,128)S(1)}, bf16[48,128]{1,0:T(8,128)(2,1)S(1)}, bf16[48,128...) custom-call(bf16[144,128]{1,0:T(8,128)(2,1)S(1)} %pack.1.refs_0_.refs_4_, ...), custom_call_target="tpu_custom_call" | custom-call | tf_op jit(solution)/shard_map/image/pallas_call | solution.py:652
  17.2 0.6 %collective-permute-start.5 = (bf16[48,128]{1,0:T(8,128)(2,1)S(1)}, bf16[48,128]{1,0:T(8,128)(2,1)S(1)}, u32[]{:S(2)}, u32[]{:S(2)}) collective-permute-start(bf16[48,128]{1,0:T(8,128)(2,1)S(1)} %get-tuple-element.48), channel_id=1, source_target_pairs={{0,4},{4,0},{8,12},{12,8},{1,5},{5,1},{9,13},{13,9},{2,6},{6,2},{1... | collective-permute-start | bytes 36872 | tf_op jit(solution)/shard_map/ppermute | solution.py:560
  17.8 1.7 %collective-permute-start.6 = (bf16[48,128]{1,0:T(8,128)(2,1)S(1)}, bf16[48,128]{1,0:T(8,128)(2,1)S(1)}, u32[]{:S(2)}, u32[]{:S(2)}) collective-permute-start(bf16[48,128]{1,0:T(8,128)(2,1)S(1)} %get-tuple-element.49), channel_id=1, source_target_pairs={{0,8},{4,12},{8,0},{12,4},{1,9},{5,13},{9,1},{13,5},{2,10},{6,14},... | collective-permute-start | bytes 36872 | tf_op jit(solution)/shard_map/ppermute | solution.py:560
  19.5 2.2 %collective-permute-start.7 = (bf16[48,128]{1,0:T(8,128)(2,1)S(1)}, bf16[48,128]{1,0:T(8,128)(2,1)S(1)}, u32[]{:S(2)}, u32[]{:S(2)}) collective-permute-start(bf16[48,128]{1,0:T(8,128)(2,1)S(1)} %get-tuple-element.50), channel_id=1, source_target_pairs={{0,12},{4,8},{8,4},{12,0},{1,13},{5,9},{9,5},{13,1},{2,14},{6,10},... | collective-permute-start | bytes 36872 | tf_op jit(solution)/shard_map/ppermute | solution.py:560
  21.7 0.0 collective-permute-done.5.refs_1_
  21.7 0.7 %collective-permute-done.6.refs_2_ = bf16[48,128]{1,0:T(8,128)(2,1)S(1)} collective-permute-done((bf16[48,128]{1,0:T(8,128)(2,1)S(1)}, bf16[48,128]{1,0:T(8,128)(2,1)S(1)}, u32[]{:S(2)}, u32[]{:S(2)}) %collective-permute-start.6) | collective-permute-done | bytes 12320 | tf_op jit(solution)/shard_map/ppermute | solution.py:560
  22.4 2.6 %collective-permute-done.7.refs_3_ = bf16[48,128]{1,0:T(8,128)(2,1)S(1)} collective-permute-done((bf16[48,128]{1,0:T(8,128)(2,1)S(1)}, bf16[48,128]{1,0:T(8,128)(2,1)S(1)}, u32[]{:S(2)}, u32[]{:S(2)}) %collective-permute-start.7) | collective-permute-done | bytes 12320 | tf_op jit(solution)/shard_map/ppermute | solution.py:560
  25.0 1.7 %collective-permute-start.8 = (f32[8,128]{1,0:T(8,128)S(1)}, f32[8,128]{1,0:T(8,128)S(1)}, u32[]{:S(2)}, u32[]{:S(2)}) collective-permute-start(f32[8,128]{1,0:T(8,128)S(1)} %fusion), channel_id=1, source_target_pairs={{0,2},{2,0},{1,3},{3,1},{4,6},{6,4},{5,7},{7,5},{8,10},{10,8},{9,1... | collective-permute-start | bytes 12296 | tf_op jit(solution)/shard_map/ppermute | solution.py:560
  26.7 2.6 %gradient.1 = f32[1,128,1024]{2,1,0:T(8,128)} custom-call(f32[40,128]{1,0:T(8,128)S(1)} %get-tuple-element.47.refs_0_, bf16[48,128]{1,0:T(8,128)(2,1)S(1)} %collective-permute-done.5.refs_1_, bf16[48,128]{1,0:T(8,128)(2,1)S(1)} %collective-permute-done.6.refs_2_, bf16[48,128]{1,0:T(8,128)(2,1)S(1)} %collective-permute-done.7.refs_3_, ...), custom_call_target="tpu_custom_call" | custom-call | tf_op jit(solution)/shard_map/gradient/pallas_call | solution.py:686
  29.4 0.0 collective-permute-done.8
  29.4 0.1 add_reduce_fusion
  29.5 0.5 %scatter.4 = f32[128]{0:T(128)} pad(f32[8]{0:T(128)S(1)} %broadcast_multiply_fusion, f32[]{:T(128)} %constant.32.clone.1), padding=0_120 | pad | bytes 548 | tf_op jit(solution)/shard_map/scatter | solution.py:701
  (5 shorter events, 0.0 us)
Async XLA Ops:
  3.1 1.4 %collective-permute-start = (f32[48,128]{1,0:T(8,128)S(1)}, f32[48,128]{1,0:T(8,128)S(1)}, u32[]{:S(2)}, u32[]{:S(2)}) collective-permute-start(f32[48,128]{1,0:T(8,128)S(1)} %get-tuple-element.35.part_ref), channel_id=1, source_target_pairs={{0,1},{1,0},{2,3},{3,2},{4,5},{5,4},{6,7},{7,6},{8,9},{9,8},{10,11... | collective-permute-start | bytes 73736 | tf_op jit(solution)/shard_map/ppermute | solution.py:560
  4.5 10.1 %collective-permute-start.4 = (f32[128,1024]{1,0:T(8,128)}, f32[128,1024]{1,0:T(8,128)S(1)}, u32[]{:S(2)}, u32[]{:S(2)}) collective-permute-start(f32[128,1024]{1,0:T(8,128)} %bitcast.1), channel_id=1, source_target_pairs={{0,1},{1,0},{2,3},{3,2},{4,5},{5,4},{6,7},{7,6},{8,9},{9,8},{10,11... | collective-permute-start | bytes 1572872 | tf_op jit(solution)/shard_map/ppermute | solution.py:560
  4.9 7.2 %collective-permute-start.3 = (bf16[144,128]{1,0:T(8,128)(2,1)S(1)}, bf16[144,128]{1,0:T(8,128)(2,1)S(1)}, u32[]{:S(2)}, u32[]{:S(2)}) collective-permute-start(bf16[144,128]{1,0:T(8,128)(2,1)S(1)} %pack.1.refs_0_.refs_4_), channel_id=1, source_target_pairs={{0,12},{4,8},{8,4},{12,0},{1,13},{5,9},{9,5},{13,1},{2,14},{6,10},... | collective-permute-start | bytes 110600 | tf_op jit(solution)/shard_map/ppermute | solution.py:560
  9.7 4.9 %collective-permute-start.2 = (bf16[144,128]{1,0:T(8,128)(2,1)S(1)}, bf16[144,128]{1,0:T(8,128)(2,1)S(1)}, u32[]{:S(2)}, u32[]{:S(2)}) collective-permute-start(bf16[144,128]{1,0:T(8,128)(2,1)S(1)} %pack.1.refs_0_.refs_4_), channel_id=1, source_target_pairs={{0,8},{4,12},{8,0},{12,4},{1,9},{5,13},{9,1},{13,5},{2,10},{6,14},... | collective-permute-start | bytes 110600 | tf_op jit(solution)/shard_map/ppermute | solution.py:560
  9.7 4.9 %collective-permute-start.1 = (bf16[144,128]{1,0:T(8,128)(2,1)S(1)}, bf16[144,128]{1,0:T(8,128)(2,1)S(1)}, u32[]{:S(2)}, u32[]{:S(2)}) collective-permute-start(bf16[144,128]{1,0:T(8,128)(2,1)S(1)} %pack.1.refs_0_.refs_4_), channel_id=1, source_target_pairs={{0,4},{4,0},{8,12},{12,8},{1,5},{5,1},{9,13},{13,9},{2,6},{6,2},{1... | collective-permute-start | bytes 110600 | tf_op jit(solution)/shard_map/ppermute | solution.py:560
  17.2 4.5 %collective-permute-start.5 = (bf16[48,128]{1,0:T(8,128)(2,1)S(1)}, bf16[48,128]{1,0:T(8,128)(2,1)S(1)}, u32[]{:S(2)}, u32[]{:S(2)}) collective-permute-start(bf16[48,128]{1,0:T(8,128)(2,1)S(1)} %get-tuple-element.48), channel_id=1, source_target_pairs={{0,4},{4,0},{8,12},{12,8},{1,5},{5,1},{9,13},{13,9},{2,6},{6,2},{1... | collective-permute-start | bytes 36872 | tf_op jit(solution)/shard_map/ppermute | solution.py:560
  17.8 4.6 %collective-permute-start.6 = (bf16[48,128]{1,0:T(8,128)(2,1)S(1)}, bf16[48,128]{1,0:T(8,128)(2,1)S(1)}, u32[]{:S(2)}, u32[]{:S(2)}) collective-permute-start(bf16[48,128]{1,0:T(8,128)(2,1)S(1)} %get-tuple-element.49), channel_id=1, source_target_pairs={{0,8},{4,12},{8,0},{12,4},{1,9},{5,13},{9,1},{13,5},{2,10},{6,14},... | collective-permute-start | bytes 36872 | tf_op jit(solution)/shard_map/ppermute | solution.py:560
  19.5 5.5 %collective-permute-start.7 = (bf16[48,128]{1,0:T(8,128)(2,1)S(1)}, bf16[48,128]{1,0:T(8,128)(2,1)S(1)}, u32[]{:S(2)}, u32[]{:S(2)}) collective-permute-start(bf16[48,128]{1,0:T(8,128)(2,1)S(1)} %get-tuple-element.50), channel_id=1, source_target_pairs={{0,12},{4,8},{8,4},{12,0},{1,13},{5,9},{9,5},{13,1},{2,14},{6,10},... | collective-permute-start | bytes 36872 | tf_op jit(solution)/shard_map/ppermute | solution.py:560
  25.0 4.3 %collective-permute-start.8 = (f32[8,128]{1,0:T(8,128)S(1)}, f32[8,128]{1,0:T(8,128)S(1)}, u32[]{:S(2)}, u32[]{:S(2)}) collective-permute-start(f32[8,128]{1,0:T(8,128)S(1)} %fusion), channel_id=1, source_target_pairs={{0,2},{2,0},{1,3},{3,1},{4,6},{6,4},{5,7},{7,5},{8,10},{10,8},{9,1... | collective-permute-start | bytes 12296 | tf_op jit(solution)/shard_map/ppermute | solution.py:560
